TPU v7x, 32 devices: a whole 2x2x4 slice. The times are simulated.
32 devices in a mesh: fsdp: 4 (over z), ctx: 2 (over y), tp: 4 (over x, core).
Axes of the slice: x: 2, y: 2, z: 4, core: 2. Of those that a mesh axis runs over, the one named last changes fastest.
Arguments:
- tokens: bfloat16 [16, 1024, 1024], P(('fsdp', 'tp'), 'ctx'), may hold values from -6 to 6
- routes: int32 [16, 1024, 8], P('fsdp', 'ctx'), may hold values from 0 to 31, all different within a row; in each aligned block of 512 rows (0 to 511, 512 to 1023, ..., all dimensions but the last counted through in order) at most 192 rows name the same one
- cotangent: bfloat16 [16, 1024, 1024], P(('fsdp', 'tp'), 'ctx'), may hold values from -6 to 6
- norm_gains: bfloat16 [2, 1024], P(None, ('fsdp', 'ctx', 'tp')), may hold values from 0.25 to 1.75
- query_key_value: bfloat16 [2048, 1024], P(('fsdp', 'ctx', 'tp')), may hold values from -0.25 to 0.25
- attn_output: bfloat16 [1024, 1024], P(('fsdp', 'ctx', 'tp')), may hold values from -0.75 to 0.75
- router_weight: bfloat16 [32, 1024], P(None, ('fsdp', 'ctx', 'tp')), may hold values from -0.09375 to 0.09375
- expert_in: bfloat16 [32, 2, 1024, 512], P(None, None, ('fsdp', 'ctx'), 'tp'), may hold values from -0.1875 to 0.1875
- expert_out: bfloat16 [32, 1024, 512], P(None, ('fsdp', 'ctx'), 'tp'), may hold values from -1 to 1
Outputs:
- output: bfloat16 [16, 1024, 1024], P(('fsdp', 'tp'), 'ctx')
- input_grad: float32 [16, 1024, 1024], P(('fsdp', 'tp'), 'ctx')
- grad_norm_gains: float32 [2, 1024], P(None, ('fsdp', 'ctx', 'tp'))
- grad_query_key_value: float32 [2048, 1024], P(('fsdp', 'ctx', 'tp'))
- grad_attn_output: float32 [1024, 1024], P(('fsdp', 'ctx', 'tp'))
- grad_router_weight: float32 [32, 1024], P(None, ('fsdp', 'ctx', 'tp'))
- grad_expert_in: float32 [32, 2, 1024, 512], P(None, None, ('fsdp', 'ctx'), 'tp')
- grad_expert_out: float32 [32, 1024, 512], P(None, ('fsdp', 'ctx'), 'tp')
Inputs may be any that keep to these rules, and one draw needn't show every extreme that they name: `routes`: each row names 8 different experts. In each aligned block of 512 rows (one sequence's positions on one index of ctx), no expert is named by more than 192 rows, a bound that some block reaches.
All inputs are finite; a program needn't handle non-finite values.
Results may differ from a plain program's by a relative error of at most 0.014.
The roundings to bfloat16 on the way count: a program that leaves them out, or rounds other values in their place, can miss the bound.
Values may be sent and summed in bfloat16 or wider, within the bound.
No kernel may reach another device: no remote copies, remote signals or barrier semaphores. Data moves between devices by JAX's collectives and lax.ppermute only.
A program may use at most 320 MiB of HBM per device.

v0:
```python
import jax
import jax.numpy as jnp
from jax import lax
from jax.sharding import PartitionSpec as P

HEADS = 16
KV_HEADS = 8
HEAD = 64
EXPERTS = 32
TOP = 8


EPS = 1e-06
NEG = -1e30
HIGH = lax.Precision.HIGHEST


def times_transposed(left_side, right_side):
    return lax.dot_general(
        left_side, right_side, (((1,), (1,)), ((), ())), preferred_element_type=jnp.float32
    )


def transposed_times(left_side, right_side):
    return lax.dot_general(
        left_side, right_side, (((0,), (0,)), ((), ())), preferred_element_type=jnp.float32
    )


def angle_tables(positions, head_size):
    half_size = head_size // 2
    inverse = 10000.0 ** (-jnp.arange(half_size, dtype=jnp.float32) * 2.0 / head_size)
    angles = positions.astype(jnp.float32)[:, None] * inverse[None, :]
    return (jnp.cos(angles), jnp.sin(angles))


def rotary(values, cosine_table, sine_table):
    half_size = values.shape[-1] // 2
    former = values[..., :half_size]
    latter = values[..., half_size:]
    return jnp.concatenate(
        [former * cosine_table - latter * sine_table, latter * cosine_table + former * sine_table],
        axis=-1,
    )


def rotary_back(gradient, cosine_table, sine_table):
    half_size = gradient.shape[-1] // 2
    former = gradient[..., :half_size]
    latter = gradient[..., half_size:]
    return jnp.concatenate(
        [former * cosine_table + latter * sine_table, latter * cosine_table - former * sine_table],
        axis=-1,
    )


def rms_back(grad_normed, normed, inverse, gain_row):
    scaled_grad = grad_normed * gain_row
    return inverse * (scaled_grad - normed * jnp.mean(scaled_grad * normed, axis=1, keepdims=True))


def per_device(
    tokens,
    routes,
    cotangent,
    norm_gains,
    query_key_value,
    attn_output,
    router_weight,
    expert_in,
    expert_out,
):
    local_seqs, local_positions, model_width = tokens.shape
    context_count = lax.axis_size("ctx")
    length = local_positions * context_count
    row_count = local_seqs * local_positions
    local_groups = KV_HEADS // context_count
    head_size = HEAD
    score_scale = HEAD ** (-0.5)
    capacity = local_positions * 3 // 8
    inward_full, output_full, router_full, gain_full = (
        lax.all_gather(query_key_value, ("fsdp", "ctx", "tp"), axis=0, tiled=True),
        lax.all_gather(attn_output, ("fsdp", "ctx", "tp"), axis=0, tiled=True),
        lax.all_gather(router_weight, ("fsdp", "ctx", "tp"), axis=1, tiled=True),
        lax.all_gather(norm_gains, ("fsdp", "ctx", "tp"), axis=1, tiled=True),
    )
    expert_in_full, expert_out_full = (
        lax.all_gather(expert_in, ("fsdp", "ctx"), axis=2, tiled=True),
        lax.all_gather(expert_out, ("fsdp", "ctx"), axis=1, tiled=True),
    )
    gain_rows = gain_full.astype(jnp.float32)
    inputs = tokens.astype(jnp.float32).reshape(row_count, model_width)
    inverse_first = lax.rsqrt(jnp.mean(inputs * inputs, axis=1, keepdims=True) + EPS)
    normed_first = inputs * inverse_first
    first_low = (normed_first * gain_rows[0]).astype(jnp.bfloat16)
    projected = times_transposed(first_low, inward_full).reshape(
        local_seqs, local_positions, KV_HEADS, 4, head_size
    )
    positions = lax.axis_index("ctx") * local_positions + jnp.arange(
        local_positions, dtype=jnp.int32
    )
    cosine_table, sine_table = angle_tables(positions, head_size)
    cosine_rows = cosine_table[None, :, None, None, :]
    sine_rows = sine_table[None, :, None, None, :]
    turned = jnp.concatenate(
        [rotary(projected[:, :, :, :3], cosine_rows, sine_rows), projected[:, :, :, 3:]], axis=3
    )
    sent_heads = turned.astype(jnp.bfloat16).reshape(
        local_seqs, local_positions, KV_HEADS, 4 * head_size
    )
    head_rows = lax.all_to_all(sent_heads, "ctx", split_axis=2, concat_axis=1, tiled=True)
    queries = head_rows[..., : 2 * head_size].reshape(
        local_seqs, length, local_groups, 2, head_size
    )
    key_rows = head_rows[..., 2 * head_size : 3 * head_size]
    value_rows = head_rows[..., 3 * head_size :]
    block_rows = min(512, length)
    key_index = jnp.arange(length)
    attended = []
    log_totals = []
    for offset in range(0, length, block_rows):
        limit_row = offset + block_rows
        scores = (
            jnp.einsum(
                "sqgjd,skgd->sgjqk",
                queries[:, offset:limit_row],
                key_rows[:, :limit_row],
                preferred_element_type=jnp.float32,
            )
            * score_scale
        )
        visible = (offset + jnp.arange(block_rows))[:, None] >= key_index[None, :limit_row]
        scores = jnp.where(visible, scores, NEG)
        top_score = jnp.max(scores, axis=-1, keepdims=True)
        exponent = jnp.exp(scores - top_score)
        denominator = jnp.sum(exponent, axis=-1, keepdims=True)
        weights = exponent / denominator
        attended.append(
            jnp.einsum(
                "sgjqk,skgd->sqgjd",
                weights.astype(jnp.bfloat16),
                value_rows[:, :limit_row],
                preferred_element_type=jnp.float32,
            )
        )
        log_totals.append(top_score + jnp.log(denominator))
    head_output = (
        jnp.concatenate(attended, axis=1)
        .astype(jnp.bfloat16)
        .reshape(local_seqs, length, local_groups, 2 * head_size)
    )
    merged = lax.all_to_all(head_output, "ctx", split_axis=1, concat_axis=2, tiled=True).reshape(
        row_count, HEADS * head_size
    )
    hidden = inputs + times_transposed(merged, output_full)
    inverse_second = lax.rsqrt(jnp.mean(hidden * hidden, axis=1, keepdims=True) + EPS)
    normed_second = hidden * inverse_second
    second_low = (normed_second * gain_rows[1]).astype(jnp.bfloat16)
    group_rows = lax.all_gather(
        second_low.reshape(local_seqs, local_positions, model_width), "tp", axis=0, tiled=True
    ).reshape(-1, model_width)
    group_count = group_rows.shape[0]
    segments = group_count // local_positions
    group_seg = group_rows.reshape(segments, local_positions, model_width)
    chances = jax.nn.softmax(times_transposed(group_rows, router_full), axis=-1)
    route_rows = routes.reshape(group_count, TOP)
    chosen_any = jnp.sum(
        (route_rows[:, :, None] == jnp.arange(EXPERTS, dtype=jnp.int32)[None, None, :]).astype(
            jnp.float32
        ),
        axis=1,
    )
    gate_table = chances * chosen_any
    earlier = (jnp.arange(local_positions)[:, None] > jnp.arange(local_positions)[None, :]).astype(
        jnp.float32
    )
    rank_table = jnp.einsum(
        "tu,sue->ste",
        earlier,
        chosen_any.reshape(segments, local_positions, EXPERTS),
        precision=HIGH,
    ).astype(jnp.int32)
    expert_step = 4
    step_count = EXPERTS // expert_step
    hidden_units = expert_in_full.shape[-1]

    def by_step(table):
        return table.reshape(segments, local_positions, step_count, expert_step).transpose(
            2, 0, 3, 1
        )

    mask_steps = by_step(chosen_any)
    rank_steps = by_step(rank_table)
    gate_steps = by_step(gate_table)
    slot_index = jnp.arange(capacity, dtype=jnp.int32)

    def dispatch(mask_block, rank_block):
        return jnp.where(
            (rank_block[:, :, None, :] == slot_index[None, None, :, None])
            & (mask_block[:, :, None, :] > 0.5),
            1.0,
            0.0,
        )

    stacked_in = expert_in_full.reshape(step_count, expert_step, 2, model_width, hidden_units)
    stacked_out = expert_out_full.reshape(step_count, expert_step, model_width, hidden_units)

    def expert_forward(running, pieces):
        mask_block, rank_block, gate_block, weight_in, weight_out = pieces
        table = dispatch(mask_block, rank_block)
        rows_in = jnp.einsum(
            "sect,std->secd",
            table.astype(jnp.bfloat16),
            group_seg,
            preferred_element_type=jnp.float32,
        ).astype(jnp.bfloat16)
        pre_gate = jnp.einsum(
            "secd,edf->secf", rows_in, weight_in[:, 0], preferred_element_type=jnp.float32
        )
        pre_up = jnp.einsum(
            "secd,edf->secf", rows_in, weight_in[:, 1], preferred_element_type=jnp.float32
        )
        hidden_rows = (jax.nn.silu(pre_gate) * pre_up).astype(jnp.bfloat16)
        expert_rows = jnp.einsum(
            "secf,edf->secd", hidden_rows, weight_out, preferred_element_type=jnp.float32
        )
        running = running + jnp.einsum(
            "sect,secd->std", table * gate_block[:, :, None, :], expert_rows, precision=HIGH
        )
        return (running, (pre_gate, pre_up))

    partial_moe, (kept_gate, kept_up) = lax.scan(
        expert_forward,
        jnp.zeros((segments, local_positions, model_width), jnp.float32),
        (mask_steps, rank_steps, gate_steps, stacked_in, stacked_out),
    )
    moe_rows = (
        lax.psum_scatter(partial_moe.astype(jnp.bfloat16), "tp", scatter_dimension=0, tiled=True)
        .astype(jnp.float32)
        .reshape(row_count, model_width)
    )
    output = (hidden + moe_rows).astype(jnp.bfloat16).reshape(tokens.shape)
    inward_full, output_full, router_full, gain_full = (
        lax.all_gather(query_key_value, ("fsdp", "ctx", "tp"), axis=0, tiled=True),
        lax.all_gather(attn_output, ("fsdp", "ctx", "tp"), axis=0, tiled=True),
        lax.all_gather(router_weight, ("fsdp", "ctx", "tp"), axis=1, tiled=True),
        lax.all_gather(norm_gains, ("fsdp", "ctx", "tp"), axis=1, tiled=True),
    )
    expert_in_full, expert_out_full = (
        lax.all_gather(expert_in, ("fsdp", "ctx"), axis=2, tiled=True),
        lax.all_gather(expert_out, ("fsdp", "ctx"), axis=1, tiled=True),
    )
    back_in = expert_in_full.reshape(step_count, expert_step, 2, model_width, hidden_units)
    back_out = expert_out_full.reshape(step_count, expert_step, model_width, hidden_units)
    grad_group = lax.all_gather(cotangent, "tp", axis=0, tiled=True)

    def expert_backward(running, pieces):
        mask_block, rank_block, gate_block, weight_in, weight_out, pre_gate, pre_up = pieces
        table = dispatch(mask_block, rank_block)
        table_low = table.astype(jnp.bfloat16)
        rows_in = jnp.einsum(
            "sect,std->secd", table_low, group_seg, preferred_element_type=jnp.float32
        ).astype(jnp.bfloat16)
        rows_grad = jnp.einsum(
            "sect,std->secd", table_low, grad_group, preferred_element_type=jnp.float32
        ).astype(jnp.bfloat16)
        slot_gate = jnp.sum(table * gate_block[:, :, None, :], axis=-1)
        sigmoid_gate = jax.nn.sigmoid(pre_gate)
        swish_gate = pre_gate * sigmoid_gate
        hidden_rows = (swish_gate * pre_up).astype(jnp.bfloat16)
        scaled = (slot_gate[..., None] * rows_grad.astype(jnp.float32)).astype(jnp.bfloat16)
        grad_hidden_rows = jnp.einsum(
            "secd,edf->secf", scaled, weight_out, preferred_element_type=jnp.float32
        )
        probe_rows = jnp.einsum(
            "secd,edf->secf", rows_grad, weight_out, preferred_element_type=jnp.float32
        )
        grad_gates = jnp.sum(probe_rows * hidden_rows.astype(jnp.float32), axis=-1)
        grad_choice = jnp.sum(table * grad_gates[..., None], axis=2)
        grad_out_block = jnp.einsum(
            "secd,secf->edf", scaled, hidden_rows, preferred_element_type=jnp.float32
        )
        grad_pre_gate = (
            grad_hidden_rows * pre_up * sigmoid_gate * (1.0 + pre_gate * (1.0 - sigmoid_gate))
        ).astype(jnp.bfloat16)
        grad_pre_up = (grad_hidden_rows * swish_gate).astype(jnp.bfloat16)
        grad_in_block = jnp.stack(
            [
                jnp.einsum(
                    "secd,secf->edf", rows_in, grad_pre_gate, preferred_element_type=jnp.float32
                ),
                jnp.einsum(
                    "secd,secf->edf", rows_in, grad_pre_up, preferred_element_type=jnp.float32
                ),
            ],
            axis=1,
        )
        back_rows = jnp.einsum(
            "secf,edf->secd", grad_pre_gate, weight_in[:, 0], preferred_element_type=jnp.float32
        ) + jnp.einsum(
            "secf,edf->secd", grad_pre_up, weight_in[:, 1], preferred_element_type=jnp.float32
        )
        running = running + jnp.einsum("sect,secd->std", table, back_rows, precision=HIGH)
        return (running, (grad_choice, grad_in_block, grad_out_block))

    back_moe, (grad_choice_steps, grad_in_steps, grad_out_steps) = lax.scan(
        expert_backward,
        jnp.zeros((segments, local_positions, model_width), jnp.float32),
        (mask_steps, rank_steps, gate_steps, back_in, back_out, kept_gate, kept_up),
    )
    grad_chances = grad_choice_steps.transpose(1, 3, 0, 2).reshape(group_count, EXPERTS)
    grad_logits = chances * (grad_chances - jnp.sum(grad_chances * chances, axis=-1, keepdims=True))
    router_rows = router_full.astype(jnp.float32)
    grad_router = jnp.dot(grad_logits.T, group_rows.astype(jnp.float32), precision=HIGH)
    back_group = back_moe.reshape(group_count, model_width) + jnp.dot(
        grad_logits, router_rows, precision=HIGH
    )
    grad_second = (
        lax.psum_scatter(
            back_group.reshape(segments, local_positions, model_width).astype(jnp.bfloat16),
            "tp",
            scatter_dimension=0,
            tiled=True,
        )
        .astype(jnp.float32)
        .reshape(row_count, model_width)
    )
    gain_rows = gain_full.astype(jnp.float32)
    grad_gain_second = jnp.sum(grad_second * normed_second, axis=0)
    grad_hidden = cotangent.astype(jnp.float32).reshape(row_count, model_width) + rms_back(
        grad_second, normed_second, inverse_second, gain_rows[1]
    )
    grad_attn = grad_hidden.astype(jnp.bfloat16)
    grad_output_weight = transposed_times(grad_attn, merged)
    grad_merged = (
        jnp.dot(grad_attn, output_full, preferred_element_type=jnp.float32)
        .astype(jnp.bfloat16)
        .reshape(local_seqs, local_positions, KV_HEADS, 2 * head_size)
    )
    grad_heads = lax.all_to_all(grad_merged, "ctx", split_axis=2, concat_axis=1, tiled=True)
    grad_keys = jnp.zeros((local_seqs, length, local_groups, head_size), jnp.float32)
    grad_values = jnp.zeros((local_seqs, length, local_groups, head_size), jnp.float32)
    grad_query_blocks = []
    for offset, log_total in zip(range(0, length, block_rows), log_totals):
        limit_row = offset + block_rows
        query_block = queries[:, offset:limit_row]
        key_part = key_rows[:, :limit_row]
        value_part = value_rows[:, :limit_row]
        scores = (
            jnp.einsum(
                "sqgjd,skgd->sgjqk", query_block, key_part, preferred_element_type=jnp.float32
            )
            * score_scale
        )
        visible = (offset + jnp.arange(block_rows))[:, None] >= key_index[None, :limit_row]
        scores = jnp.where(visible, scores, NEG)
        weights = jnp.exp(scores - log_total)
        grad_block = grad_heads[:, offset:limit_row].reshape(
            local_seqs, block_rows, local_groups, 2, head_size
        )
        grad_values = grad_values.at[:, :limit_row].add(
            jnp.einsum(
                "sgjqk,sqgjd->skgd",
                weights.astype(jnp.bfloat16),
                grad_block,
                preferred_element_type=jnp.float32,
            )
        )
        grad_weights = jnp.einsum(
            "sqgjd,skgd->sgjqk", grad_block, value_part, preferred_element_type=jnp.float32
        )
        grad_scores = (
            weights * (grad_weights - jnp.sum(weights * grad_weights, axis=-1, keepdims=True))
        ).astype(jnp.bfloat16)
        grad_query_blocks.append(
            jnp.einsum(
                "sgjqk,skgd->sqgjd", grad_scores, key_part, preferred_element_type=jnp.float32
            )
            * score_scale
        )
        grad_keys = grad_keys.at[:, :limit_row].add(
            jnp.einsum(
                "sgjqk,sqgjd->skgd", grad_scores, query_block, preferred_element_type=jnp.float32
            )
            * score_scale
        )
    grad_queries = jnp.concatenate(grad_query_blocks, axis=1).reshape(
        local_seqs, length, local_groups, 2 * head_size
    )
    grad_head_rows = jnp.concatenate([grad_queries, grad_keys, grad_values], axis=-1).astype(
        jnp.bfloat16
    )
    grad_turned = (
        lax.all_to_all(grad_head_rows, "ctx", split_axis=1, concat_axis=2, tiled=True)
        .astype(jnp.float32)
        .reshape(local_seqs, local_positions, KV_HEADS, 4, head_size)
    )
    grad_projected = (
        jnp.concatenate(
            [
                rotary_back(grad_turned[:, :, :, :3], cosine_rows, sine_rows),
                grad_turned[:, :, :, 3:],
            ],
            axis=3,
        )
        .astype(jnp.bfloat16)
        .reshape(row_count, -1)
    )
    grad_inward = transposed_times(grad_projected, first_low)
    grad_first = jnp.dot(grad_projected, inward_full, preferred_element_type=jnp.float32)
    grad_gain_first = jnp.sum(grad_first * normed_first, axis=0)
    grad_inputs = grad_hidden + rms_back(grad_first, normed_first, inverse_first, gain_rows[0])
    grad_gains = jnp.stack([grad_gain_first, grad_gain_second])
    dense_sums = (
        lax.psum_scatter(grad_inward, ("fsdp", "ctx", "tp"), scatter_dimension=0, tiled=True),
        lax.psum_scatter(
            grad_output_weight, ("fsdp", "ctx", "tp"), scatter_dimension=0, tiled=True
        ),
        lax.psum_scatter(grad_router, ("fsdp", "ctx", "tp"), scatter_dimension=1, tiled=True),
        lax.psum_scatter(grad_gains, ("fsdp", "ctx", "tp"), scatter_dimension=1, tiled=True),
    )
    expert_in_terms = grad_in_steps.reshape(EXPERTS, 2, model_width, hidden_units)
    expert_out_terms = grad_out_steps.reshape(EXPERTS, model_width, hidden_units)
    expert_sums = (
        lax.psum_scatter(expert_in_terms, ("fsdp", "ctx"), scatter_dimension=2, tiled=True),
        lax.psum_scatter(expert_out_terms, ("fsdp", "ctx"), scatter_dimension=1, tiled=True),
    )
    return (
        output,
        grad_inputs.reshape(tokens.shape),
        dense_sums[3],
        dense_sums[0],
        dense_sums[1],
        dense_sums[2],
        expert_sums[0],
        expert_sums[1],
    )


def solution(mesh):
    placed = (
        P(("fsdp", "tp"), "ctx", None),
        P("fsdp", "ctx", None),
        P(("fsdp", "tp"), "ctx", None),
        P(None, ("fsdp", "ctx", "tp")),
        P(("fsdp", "ctx", "tp"), None),
        P(("fsdp", "ctx", "tp"), None),
        P(None, ("fsdp", "ctx", "tp")),
        P(None, None, ("fsdp", "ctx"), "tp"),
        P(None, ("fsdp", "ctx"), "tp"),
    )
    return jax.shard_map(
        per_device,
        mesh=mesh,
        in_specs=placed,
        out_specs=(
            P(("fsdp", "tp"), "ctx", None),
            P(("fsdp", "tp"), "ctx", None),
            P(None, ("fsdp", "ctx", "tp")),
            P(("fsdp", "ctx", "tp"), None),
            P(("fsdp", "ctx", "tp"), None),
            P(None, ("fsdp", "ctx", "tp")),
            P(None, None, ("fsdp", "ctx"), "tp"),
            P(None, ("fsdp", "ctx"), "tp"),
        ),
        check_vma=False,
    )
```

profile of v0, /device:TPU:0, one launch (start us, length us, event | category | flops | bytes accessed | tf_op | source)
XLA Modules:
  0.0 3076.1 jit_solution(2374678237478736761)
XLA Ops:
  7.9 43.3 %all-gather.1 = bf16[32,32,2]{1,2,0:T(2,128)(2,1)S(1)} all-gather(bf16[1,32,2]{1,2,0:T(2,128)(2,1)} %bitcast.660), channel_id=1, replica_groups=mesh['fsdp'=4,'ctx'=2,'tp'=4] {'fsdp','ctx','tp'}, dimensions={0}, use_global_device_ids=true | all-gather | bytes 4224 | tf_op jit(solution)/shard_map/all_gather | solution.py:85
  53.2 22.4 all-gather.9.cloned.1.call-done
  75.6 5.1 convolution_bitcast_fusion.2
  88.0 24.5 all-to-all-done
  126.0 7.5 fusion.211
  134.6 8.1 fusion.115
  142.8 7.5 fusion.178
  152.4 16.1 all_to_all.60
  177.2 39.6 %all_gather.34 = bf16[32,1024]{0,1:T(8,128)(2,1)S(1)} all-gather(bf16[32,32]{0,1:T(8,128)(2,1)S(1)} %copy.251), channel_id=1, replica_groups=mesh['fsdp'=4,'ctx'=2,'tp'=4] {'fsdp','ctx','tp'}, dimensions={1}, use_global_device_ids=true | all-gather | bytes 67584 | tf_op jit(solution)/shard_map/all_gather | solution.py:84
  226.0 213.6 %all-gather.15.cloned.1.call-done = bf16[32,2,1024,128]{3,2,1,0:T(8,128)(2,1)} async-done(((bf16[32,2,128,128]{3,2,1,0:T(8,128)(2,1)}), bf16[32,2,1024,128]{3,2,1,0:T(8,128)(2,1)}) %all-gather.15.cloned.1.call-update) | async-done | bytes 16777232 | tf_op jit(solution)/shard_map/all_gather | solution.py:88
  439.6 14.0 copy.253
  453.6 111.2 %all-gather.13.cloned.1.call-done = bf16[32,1024,128]{2,1,0:T(8,128)(2,1)} async-done(((bf16[32,128,128]{2,1,0:T(8,128)(2,1)}), bf16[32,1024,128]{2,1,0:T(8,128)(2,1)}) %all-gather.13.cloned.1.call-update) | async-done | bytes 8388624 | tf_op jit(solution)/shard_map/all_gather | solution.py:89
  564.8 333.1 %while.38 = (s32[]{:T(128)}, f32[4,512,1024]{2,1,0:T(8,128)}, f32[8,4,4,192,128]{4,3,1,2,0:T(8,128)}, f32[8,4,4,192,128]{4,3,1,2,0:T(8,128)}, s32[8,4,4,512]{3,2...) while((s32[]{:T(128)}, f32[4,512,1024]{2,1,0:T(8,128)}, ...), condition=%wide.region_10.11_spmd.clone, body=%wide.region_9.10_spmd.clone.sunk | while | flops 24986787840 | bytes 159146256 | solution.py:232
  581.2 21.8 bitcast_add_fusion.5
  622.7 21.8 bitcast_add_fusion.5
  664.3 21.8 bitcast_add_fusion.5
  705.9 21.8 bitcast_add_fusion.5
  747.5 21.8 bitcast_add_fusion.5
  789.1 21.8 bitcast_add_fusion.5
  830.6 21.8 bitcast_add_fusion.5
  872.2 21.8 bitcast_add_fusion.5
  897.8 572.8 %while.39 = (s32[]{:T(128)}, f32[4,512,1024]{2,1,0:T(8,128)}, f32[8,4,4,512]{3,2,1,0:T(4,128)}, f32[8,4,2,1024,128]{4,3,2,1,0:T(8,128)}, f32[8,4,1024,128]{3,2,1...) while((s32[]{:T(128)}, f32[4,512,1024]{2,1,0:T(8,128)}, ...), condition=%wide.region_16.17_spmd.clone, body=%wide.region_12.16_spmd.clone.sunk | while | flops 31477458944 | bytes 223638832 | solution.py:306
  932.3 4.6 fusion.295
  946.6 6.8 bitcast_dynamic-update-slice_fusion.11
  957.0 22.9 bitcast_add_fusion.6
  1000.3 4.6 fusion.295
  1014.6 6.8 bitcast_dynamic-update-slice_fusion.11
  1025.0 24.6 bitcast_add_fusion.6
  1084.4 6.7 bitcast_dynamic-update-slice_fusion.11
  1094.7 24.6 bitcast_add_fusion.6
  1139.8 4.6 fusion.295
  1154.1 6.8 bitcast_dynamic-update-slice_fusion.11
  1164.5 24.6 bitcast_add_fusion.6
  1223.8 6.7 bitcast_dynamic-update-slice_fusion.11
  1234.1 24.6 bitcast_add_fusion.6
  1293.4 6.9 bitcast_dynamic-update-slice_fusion.11
  1303.9 24.6 bitcast_add_fusion.6
  1348.9 4.6 fusion.295
  1363.3 6.7 bitcast_dynamic-update-slice_fusion.11
  1373.6 24.6 bitcast_add_fusion.6
  1433.0 6.7 bitcast_dynamic-update-slice_fusion.11
  1443.3 24.6 bitcast_add_fusion.6
  1471.9 7.5 fusion.124
  1479.4 6.1 convert_element_type.195
  1485.6 36.6 %reduce-scatter.15.cloned.1.call-done = bf16[1,512,1024]{2,1,0:T(8,128)(2,1)} async-done(((bf16[4,512,1024]{2,1,0:T(8,128)(2,1)}), bf16[1,512,1024]{2,1,0:T(8,128)(2,1)}) %reduce-scatter.15.cloned.1.call-update) | async-done | bytes 1048592 | tf_op jit(solution)/shard_map/reduce_scatter | solution.py:319
  1524.2 45.3 %reduce-scatter.13.cloned.1.call-done = bf16[1,512,1024]{2,1,0:T(8,128)(2,1)} async-done(((bf16[4,512,1024]{2,1,0:T(8,128)(2,1)}), bf16[1,512,1024]{2,1,0:T(8,128)(2,1)}) %reduce-scatter.13.cloned.1.call-update) | async-done | bytes 1048592 | tf_op jit(solution)/shard_map/reduce_scatter | solution.py:238
  1581.1 13.9 all-to-all-done.2
  1603.4 5.7 fusion.183
  1609.1 8.5 fusion.121
  1617.7 4.8 fusion.133
  1629.2 10.5 fusion.112
  1639.7 4.8 fusion.169
  1646.8 12.2 fusion.120
  1673.9 4.8 all-to-all-start.3
  1678.7 7.5 convolution_bitcast_fusion.4
  1686.3 16.9 all-to-all-done.3
  1707.5 5.5 copy.268
  1727.4 7.6 fusion.191
  1736.3 84.7 %reduce-scatter.27.cloned.1.call-done = f32[32,32]{1,0:T(8,128)} async-done(((f32[1024,32]{1,0:T(8,128)}), f32[32,32]{1,0:T(8,128)}) %reduce-scatter.27.cloned.1.call-update) | async-done | bytes 4112
  1826.2 126.8 %reduce-scatter.25.cloned.1.call-done = f32[32,2]{1,0:T(8,128)} async-done(((f32[1024,2]{1,0:T(8,128)}), f32[32,2]{1,0:T(8,128)}) %reduce-scatter.25.cloned.1.call-update) | async-done | bytes 272
  1954.4 138.4 %reduce-scatter.19.cloned.1.call-done = f32[32,1024]{1,0:T(8,128)} async-done(((f32[1024,1024]{1,0:T(8,128)}), f32[32,1024]{1,0:T(8,128)}) %reduce-scatter.19.cloned.1.call-update) | async-done | bytes 131088 | tf_op jit(solution)/shard_map/reduce_scatter | solution.py:416
  2092.8 147.5 %reduce-scatter.17.cloned.1.call-done = f32[64,1024]{1,0:T(8,128)} async-done(((f32[2048,1024]{1,0:T(8,128)}), f32[64,1024]{1,0:T(8,128)}) %reduce-scatter.17.cloned.1.call-update) | async-done | bytes 262160 | tf_op jit(solution)/shard_map/reduce_scatter | solution.py:415
  2240.3 282.2 %reduce-scatter.23.cloned.1.call-done = f32[32,128,128]{2,1,0:T(8,128)} async-done(((f32[32,1024,128]{2,1,0:T(8,128)}), f32[32,128,128]{2,1,0:T(8,128)}) %reduce-scatter.23.cloned.1.call-update) | async-done | bytes 2097168 | tf_op jit(solution)/shard_map/reduce_scatter | solution.py:426
  2522.5 546.8 %reduce-scatter.21.cloned.1.call-done = f32[32,2,128,128]{3,2,1,0:T(8,128)} async-done(((f32[32,2,1024,128]{3,2,1,0:T(8,128)}), f32[32,2,128,128]{3,2,1,0:T(8,128)}) %reduce-scatter.21.cloned.1.call-update) | async-done | bytes 4194320 | tf_op jit(solution)/shard_map/reduce_scatter | solution.py:425
  (562 shorter events, 562.1 us)
Async XLA Ops:
  7.2 68.5 %all-gather.9.cloned.1.call-start = ((), (), s32[]{:S(2)}) async-start(), calls=%async_computation.12 | async-start | bytes 4325376 | tf_op jit(solution)/shard_map/all_gather | solution.py:82
  52.8 27.9 copy-start.44
  52.8 27.9 copy-start.42
  52.9 119.8 %copy-start.31 = (f32[1,1024]{1,0:T(1,128)}, f32[1,1024]{1,0:T(1,128)S(1)}, u32[]{:S(2)}) copy-start(f32[1,1024]{1,0:T(1,128)S(1)} %get-tuple-element.484) | copy-start | bytes 12292
  53.2 27.6 copy-start.21
  53.2 27.6 copy-start.23
  82.8 29.8 all-to-all-start
  86.6 82.7 %all-gather.11.cloned.1.call-start = ((), (), s32[]{:S(2)}) async-start(), calls=%async_computation.13 | async-start | bytes 2162688 | tf_op jit(solution)/shard_map/all_gather | solution.py:83
  87.3 132.0 %all-gather.19.cloned.1.call-start = ((), (), s32[]{:S(2)}) async-start(), calls=%async_computation.23 | async-start | bytes 5242880 | tf_op jit(solution)/shard_map/all_gather | solution.py:159
  119.4 23.3 copy-start.6
  133.6 9.2 copy-start.36
  150.6 18.7 copy-start.15
  174.0 42.8 %copy-start.35 = (s32[4,512,8]{1,2,0:T(8,128)S(1)}, s32[4,512,8]{1,2,0:T(8,128)}, u32[]{:S(2)}) copy-start(s32[4,512,8]{1,2,0:T(8,128)} %param.26) | copy-start | bytes 196612
  175.2 264.4 %all-gather.15.cloned.1.call-start = ((), (), s32[]{:S(2)}) async-start(), calls=%async_computation.15 | async-start | bytes 18874368 | tf_op jit(solution)/shard_map/all_gather | solution.py:88
  175.8 389.0 %all-gather.13.cloned.1.call-start = ((), (), s32[]{:S(2)}) async-start(), calls=%async_computation.14 | async-start | bytes 9437184 | tf_op jit(solution)/shard_map/all_gather | solution.py:89
  176.4 721.5 %all-gather.17.cloned.1.call-start = ((), (), s32[]{:S(2)}) async-start(), calls=%async_computation.17 | async-start | bytes 5242880 | tf_op jit(solution)/shard_map/all_gather | solution.py:255
  177.0 1345.3 %reduce-scatter.15.cloned.1.call-start = ((), (), s32[]{:S(2)}) async-start(), calls=%async_computation.18 | async-start | bytes 5242880 | tf_op jit(solution)/shard_map/reduce_scatter | solution.py:319
  216.7 8.3 copy-start.17
  573.3 7.9 slice-start.6
  614.9 7.8 slice-start.6
  656.4 7.8 slice-start.6
  698.0 7.8 slice-start.6
  739.6 7.9 slice-start.6
  781.2 7.9 slice-start.6
  822.8 7.8 slice-start.6
  864.4 7.8 slice-start.6
  897.8 573.9 %copy-start.8 = (f32[2048,32]{0,1:T(8,128)S(1)}, f32[2048,32]{0,1:T(8,128)}, u32[]{:S(2)}) copy-start(f32[2048,32]{0,1:T(8,128)} %copy-done.7) | copy-start | bytes 786436
  897.8 573.9 %copy-start.26 = (f32[2048]{0:T(1024)S(1)}, f32[2048]{0:T(1024)}, u32[]{:S(2)}) copy-start(f32[2048]{0:T(1024)} %copy-done.25) | copy-start | bytes 24580
  897.8 574.0 %copy-start.28 = (f32[2048]{0:T(1024)S(1)}, f32[2048]{0:T(1024)}, u32[]{:S(2)}) copy-start(f32[2048]{0:T(1024)} %copy-done.27) | copy-start | bytes 24580
  924.6 7.6 copy-start.50
  957.0 22.9 copy-start.1
  992.6 7.6 copy-start.50
  1025.0 24.6 copy-start.1
  1062.4 7.6 copy-start.50
  1094.7 24.6 copy-start.1
  1132.1 7.6 copy-start.50
  1164.5 24.6 copy-start.1
  1201.8 7.6 copy-start.50
  1234.1 24.6 copy-start.1
  1271.4 7.6 copy-start.50
  1303.9 24.6 copy-start.1
  1341.3 7.6 copy-start.50
  1373.6 24.6 copy-start.1
  1411.0 7.6 copy-start.50
  1443.3 24.6 copy-start.1
  1471.8 7.6 copy-start.13
  1479.4 90.1 %reduce-scatter.13.cloned.1.call-start = ((), (), s32[]{:S(2)}) async-start(), calls=%async_computation.16 | async-start | bytes 5242880 | tf_op jit(solution)/shard_map/reduce_scatter | solution.py:238
  1485.6 36.6 %copy-start.3 = (f32[512,1024]{1,0:T(8,128)S(1)}, f32[512,1024]{1,0:T(8,128)}, u32[]{:S(2)}) copy-start(f32[512,1024]{1,0:T(8,128)} %copy-done.2) | copy-start | bytes 6291460
  1485.6 36.6 %copy-start.32 = (f32[1,1024]{1,0:T(1,128)S(1)}, f32[1,1024]{1,0:T(1,128)}, u32[]{:S(2)}) copy-start(f32[1,1024]{1,0:T(1,128)} %copy-done.31) | copy-start | bytes 12292
  1485.6 36.6 %copy-start.41 = (f32[512]{0:T(512)S(1)}, f32[512]{0:T(512)}, u32[]{:S(2)}) copy-start(f32[512]{0:T(512)} %copy-done.40) | copy-start | bytes 6148
  1576.6 18.4 all-to-all-start.2
  1603.4 14.3 slice-start
  1609.1 8.5 slice-start.1
  1617.7 11.5 slice-start.2
  1617.7 11.5 slice-start.3
  1617.7 11.5 slice-start.4
  1669.3 9.4 copy-start.14
  1673.9 29.3 all-to-all-start.3
  1678.7 142.3 %reduce-scatter.27.cloned.1.call-start = ((), (), s32[]{:S(2)}) async-start(), calls=%async_computation.25 | async-start | bytes 540672
  1686.3 266.8 %reduce-scatter.25.cloned.1.call-start = ((), (), s32[]{:S(2)}) async-start(), calls=%async_computation.24 | async-start | bytes 540672
  1722.8 370.0 %reduce-scatter.19.cloned.1.call-start = ((), (), s32[]{:S(2)}) async-start(), calls=%async_computation.20 | async-start | bytes 4325376 | tf_op jit(solution)/shard_map/reduce_scatter | solution.py:416
  1727.4 512.9 %reduce-scatter.17.cloned.1.call-start = ((), (), s32[]{:S(2)}) async-start(), calls=%async_computation.19 | async-start | bytes 8650752 | tf_op jit(solution)/shard_map/reduce_scatter | solution.py:415
  1735.0 787.5 %reduce-scatter.23.cloned.1.call-start = ((), (), s32[]{:S(2)}) async-start(), calls=%async_computation.22 | async-start | bytes 18874368 | tf_op jit(solution)/shard_map/reduce_scatter | solution.py:426
  1735.8 1333.5 %reduce-scatter.21.cloned.1.call-start = ((), (), s32[]{:S(2)}) async-start(), calls=%async_computation.21 | async-start | bytes 37748736 | tf_op jit(solution)/shard_map/reduce_scatter | solution.py:425
  (68 other events, 302.2 us)
Sparse Core Ops, SparseCore 0:
  10.9 64.7 all-gather.8
  90.3 56.1 all-gather.10
  175.3 34.2 all-gather.18
  211.7 227.8 all-gather.14
  441.6 123.0 all-gather.12
  566.2 32.6 all-gather.16
  1479.5 42.6 reduce-scatter.14
  1524.9 44.5 reduce-scatter.12
  1686.4 134.5 reduce-scatter.26
  1823.2 129.8 reduce-scatter.24
  1955.9 136.8 reduce-scatter.18
  2095.5 144.7 reduce-scatter.16
  2244.6 277.8 reduce-scatter.22
  2527.2 542.0 reduce-scatter.20
where the time goes:
time: 3090 us; the launch traced here: 3080 us
  waiting for transfers between devices  1820 us (59%)
  matrix products  825 us (27%)
  local copies, waits for them, and re-layouts  152 us (5%)
  other arithmetic  137 us (4%)
  blocking collectives  99 us (3%)
    reduce_scatter x1, waiting for transfers between devices, per_device(): lax.psum_scatter(expert_in_terms, ('fsdp', 'ctx'), scatter_dimension=2, t...  547 us
    reduce_scatter x1, waiting for transfers between devices, per_device(): lax.psum_scatter(expert_out_terms, ('fsdp', 'ctx'), scatter_dimension=1,...  282 us
    unnamed x16, waiting for transfers between devices  216 us
    all_gather x1, waiting for transfers between devices, per_device(): lax.all_gather(expert_in, ('fsdp', 'ctx'), axis=2, tiled=True)  214 us
    dot_general x8, matrix products, expert_backward(): jnp.einsum('sect,secd->std', table, back_rows, precision=HIGH)  195 us
    dot_general x8, matrix products, expert_forward(): jnp.einsum('sect,secd->std', table * gate_block[:, :, None, :], expert_ro...  174 us
    reduce_scatter x1, waiting for transfers between devices, per_device(): lax.psum_scatter(grad_inward, ('fsdp', 'ctx', 'tp'), scatter_dimension=0,...  147 us
    reduce_scatter x1, waiting for transfers between devices, per_device(): lax.psum_scatter(grad_output_weight, ('fsdp', 'ctx', 'tp'), scatter_dimen...  138 us
  transfers between devices with their start and end apart: 17, of which 14 were waited for; matrix products, arithmetic and copies ran while one was open for 14% of the time, Pallas kernels for 0%

commit v1 on v0

v1 whole, which is shorter than its diff:
```python
import functools

import jax
import jax.numpy as jnp
from jax import lax
from jax.experimental import pallas as pl
from jax.experimental.pallas import tpu as pltpu
from jax.sharding import PartitionSpec as P

HEADS = 16
KV_HEADS = 8
HEAD = 64
EXPERTS = 32
TOP = 8


EPS = 1e-06
NEG = -1e30
HIGH = lax.Precision.HIGHEST
ALL_AXES = ("fsdp", "ctx", "tp")
CHUNKS = 4
TILE = 512
LANES = 128


def times_transposed(left_side, right_side):
    return lax.dot_general(
        left_side, right_side, (((1,), (1,)), ((), ())), preferred_element_type=jnp.float32
    )


def transposed_times(left_side, right_side):
    return lax.dot_general(
        left_side, right_side, (((0,), (0,)), ((), ())), preferred_element_type=jnp.float32
    )


def angle_tables(positions, head_size):
    half_size = head_size // 2
    inverse = 10000.0 ** (-jnp.arange(half_size, dtype=jnp.float32) * 2.0 / head_size)
    angles = positions.astype(jnp.float32)[:, None] * inverse[None, :]
    return (jnp.cos(angles), jnp.sin(angles))


def rotary(values, cosine_table, sine_table):
    half_size = values.shape[-1] // 2
    former = values[..., :half_size]
    latter = values[..., half_size:]
    return jnp.concatenate(
        [former * cosine_table - latter * sine_table, latter * cosine_table + former * sine_table],
        axis=-1,
    )


def rotary_back(gradient, cosine_table, sine_table):
    half_size = gradient.shape[-1] // 2
    former = gradient[..., :half_size]
    latter = gradient[..., half_size:]
    return jnp.concatenate(
        [former * cosine_table + latter * sine_table, latter * cosine_table - former * sine_table],
        axis=-1,
    )


def rms_back(grad_normed, normed, inverse, gain_row):
    scaled_grad = grad_normed * gain_row
    return inverse * (scaled_grad - normed * jnp.mean(scaled_grad * normed, axis=1, keepdims=True))


def dot_nn(left_side, right_side):
    return lax.dot_general(
        left_side, right_side, (((1,), (0,)), ((), ())), preferred_element_type=jnp.float32
    )


def pack_rows(pieces, width):
    flat = jnp.concatenate([piece.reshape(-1) for piece in pieces])
    rows = -(-flat.shape[0] // (16 * width)) * 16
    return jnp.pad(flat, (0, rows * width - flat.shape[0])).reshape(rows, width)


def expert_kernel(first, steps, base_expert, extra, places_ref, *refs):
    count = len(steps)
    weight_refs, refs = refs[:count], refs[count:]
    rows_ref, rows_turned_ref, grad_ref, grad_turned_ref, gate_ref = refs[:5]
    refs = refs[5:]
    if not first:
        moe_in_ref, back_in_ref = refs[:2]
        refs = refs[2:]
    refs = refs[extra:]
    moe_ref, back_ref, choice_ref = refs[:3]
    out_refs, refs = refs[3 : 3 + count], refs[3 + count + extra :]
    moe, back, weight_in, weight_out, hidden_rows, grad_hidden, stage, semaphores = refs
    pair = pl.program_id(0)
    token_count = rows_ref.shape[0]
    units = weight_refs[0].shape[-1]
    depth = weight_refs[0].shape[-2]
    width = 2 * units

    last = pl.num_programs(0) - 1
    tiles = token_count // TILE

    def moves(tile, inward):
        rows = pl.ds(pl.multiple_of(tile * TILE, TILE), TILE)
        if inward:
            return (
                pltpu.make_async_copy(moe_in_ref.at[rows], moe.at[rows], semaphores.at[0, tile]),
                pltpu.make_async_copy(back_in_ref.at[rows], back.at[rows], semaphores.at[1, tile]),
            )
        return (
            pltpu.make_async_copy(moe.at[rows], moe_ref.at[rows], semaphores.at[2, tile]),
            pltpu.make_async_copy(back.at[rows], back_ref.at[rows], semaphores.at[3, tile]),
        )

    if not first:

        @pl.when(pair == 0)
        def _():
            for tile in range(tiles):
                for move in moves(tile, True):
                    move.start()

    @pl.when(pair == 0)
    def _():
        choice_ref[...] = jnp.zeros_like(choice_ref)
        if first:
            moe[...] = jnp.zeros_like(moe)
            back[...] = jnp.zeros_like(back)

    def place(number, block):
        return pl.ds(
            pl.multiple_of(places_ref[number] + block * steps[number], depth), depth
        )

    for number, ref in enumerate(weight_refs):
        for block in range(ref.shape[0]):
            where = place(number, block)
            for which in range(2):
                columns = slice(which * units, (which + 1) * units)
                weight_in[where, columns] = ref[block, which, 0]
                weight_in[where, width + which * units : width + (which + 1) * units] = ref[
                    block, which, 1
                ]
                weight_out[where, columns] = ref[block, which, 2]

    expert = base_expert + 2 * pair

    def tile_step(tile, carry):
        rows = pl.ds(pl.multiple_of(tile * TILE, TILE), TILE)
        both = dot_nn(rows_ref[rows, :], weight_in[...])
        probe = dot_nn(grad_ref[rows, :], weight_out[...])
        gates = gate_ref[rows, :]
        lane = lax.broadcasted_iota(jnp.int32, gates.shape, 1)
        pre_gate = both[:, :width]
        pre_up = both[:, width:]
        gate = jnp.concatenate(
            [
                jnp.broadcast_to(
                    jnp.sum(
                        jnp.where(lane == expert + which, gates, 0.0), axis=1, keepdims=True
                    ),
                    (TILE, units),
                )
                for which in range(2)
            ],
            axis=1,
        )
        sigmoid_gate = 1.0 / (1.0 + jnp.exp(-pre_gate))
        swish_gate = pre_gate * sigmoid_gate
        hidden = (swish_gate * pre_up).astype(jnp.bfloat16).astype(jnp.float32)
        gated = (hidden * gate).astype(jnp.bfloat16)
        product = probe * hidden
        choice = choice_ref[rows, :]
        for which in range(2):
            total = jnp.sum(
                product[:, which * units : (which + 1) * units], axis=1, keepdims=True
            )
            choice = jnp.where(lane == expert + which, total, choice)
        choice_ref[rows, :] = choice
        scaled = probe * gate
        grad_gate = (
            scaled * pre_up * sigmoid_gate * (1.0 + pre_gate * (1.0 - sigmoid_gate))
        ).astype(jnp.bfloat16)
        grad_up = (scaled * swish_gate).astype(jnp.bfloat16)
        hidden_rows[rows, :] = gated
        grad_hidden[rows, :width] = grad_gate
        grad_hidden[rows, width:] = grad_up
        if not first:

            @pl.when(pair == 0)
            def _():
                for move in moves(tile, True):
                    move.wait()

        moe[rows, :] += times_transposed(gated, weight_out[...])
        back[rows, :] += times_transposed(
            jnp.concatenate([grad_gate, grad_up], axis=1), weight_in[...]
        )

        @pl.when(pair == last)
        def _():
            for move in moves(tile, False):
                move.start()

        return carry

    lax.fori_loop(0, tiles, tile_step, 0)

    slab = 256

    def weight_step(tile, carry):
        rows = pl.ds(pl.multiple_of(tile * slab, slab), slab)
        stage[rows, : 2 * width] = dot_nn(rows_turned_ref[rows, :], grad_hidden[...]).astype(
            jnp.bfloat16
        )
        stage[rows, 2 * width :] = dot_nn(grad_turned_ref[rows, :], hidden_rows[...]).astype(
            jnp.bfloat16
        )
        return carry

    lax.fori_loop(0, rows_turned_ref.shape[0] // slab, weight_step, 0)

    for number, ref in enumerate(out_refs):
        for block in range(ref.shape[0]):
            where = place(number, block)
            for which in range(2):
                for kind in range(3):
                    start = kind * width + which * units
                    ref[block, which, kind] = stage[where, start : start + units]

    @pl.when(pair == last)
    def _():
        for tile in range(tiles):
            for move in moves(tile, False):
                move.wait()


def expert_pass(
    places, steps, weights, rows, rows_turned, grads, grads_turned, gates, totals, base_expert, earlier=()
):
    first = totals is None
    token_count, model_width = rows.shape
    experts, _, depth, units = weights[0].shape[1:]

    def whole(array):
        return pl.BlockSpec(
            array.shape, lambda *_: (0,) * array.ndim, pipeline_mode=pl.Buffered(1)
        )

    weight_specs = [
        pl.BlockSpec((piece.shape[0], 2, 3, depth, units), lambda pair, _: (0, pair, 0, 0, 0))
        for piece in weights
    ]
    operands = [*weights, rows, rows_turned, grads, grads_turned, gates]
    specs = [*weight_specs, *(whole(array) for array in operands[len(weights) :])]
    aliases = {}
    if not first:
        aliases = {1 + len(operands): 0, 2 + len(operands): 1}
        operands += list(totals)
        specs += [pl.BlockSpec(memory_space=pl.ANY)] * 2
    for number, array in enumerate(earlier):
        aliases[1 + len(operands)] = 3 + len(weights) + number
        operands.append(array)
        specs.append(pl.BlockSpec(memory_space=pl.ANY))
    total_shape = jax.ShapeDtypeStruct((token_count, model_width), jnp.float32)
    products = 2 * token_count * model_width * units * experts
    return pl.pallas_call(
        functools.partial(expert_kernel, first, steps, base_expert, len(earlier)),
        grid_spec=pltpu.PrefetchScalarGridSpec(
            num_scalar_prefetch=1,
            grid=(experts // 2,),
            in_specs=specs,
            out_specs=[
                pl.BlockSpec(memory_space=pl.ANY),
                pl.BlockSpec(memory_space=pl.ANY),
                pl.BlockSpec((token_count, LANES), lambda *_: (0, 0)),
                *weight_specs,
                *([pl.BlockSpec(memory_space=pl.ANY)] * len(earlier)),
            ],
            scratch_shapes=[
                pltpu.VMEM((token_count, model_width), jnp.float32),
                pltpu.VMEM((token_count, model_width), jnp.float32),
                pltpu.VMEM((model_width, 4 * units), jnp.bfloat16),
                pltpu.VMEM((model_width, 2 * units), jnp.bfloat16),
                pltpu.VMEM((token_count, 2 * units), jnp.bfloat16),
                pltpu.VMEM((token_count, 4 * units), jnp.bfloat16),
                pltpu.VMEM((model_width, 6 * units), jnp.bfloat16),
                pltpu.SemaphoreType.DMA((4, token_count // TILE)),
            ],
        ),
        out_shape=[
            total_shape,
            total_shape,
            jax.ShapeDtypeStruct((token_count, LANES), jnp.float32),
            *(jax.ShapeDtypeStruct(piece.shape, jnp.bfloat16) for piece in weights),
            *(jax.ShapeDtypeStruct(array.shape, array.dtype) for array in earlier),
        ],
        input_output_aliases=aliases,
        compiler_params=pltpu.CompilerParams(
            dimension_semantics=("arbitrary",), vmem_limit_bytes=60 * 2**20
        ),
        cost_estimate=pl.CostEstimate(
            flops=9 * products,
            bytes_accessed=40 * 2**20,
            transcendentals=token_count * units * experts,
        ),
    )(places, *operands)


def swap_pairs(count, bit):
    return [(index, index ^ bit) for index in range(count)]


def gather_group(rows):
    count = lax.axis_size("tp")
    across = lax.ppermute(rows, "tp", swap_pairs(count, 2))
    beside = lax.ppermute(rows, "tp", swap_pairs(count, 1))
    corner = lax.ppermute(across, "tp", swap_pairs(count, 1))
    return jnp.concatenate([rows, beside, across, corner], axis=0)


def scatter_group(terms):
    count = lax.axis_size("tp")
    parts = terms.reshape(count, -1, terms.shape[-1])
    sent = lax.ppermute(
        parts[1::2].astype(jnp.bfloat16), "tp", swap_pairs(count, 1)
    ).astype(jnp.float32)
    kept = parts[0] + sent[0]
    passed = (parts[2] + sent[1]).astype(jnp.bfloat16)
    return kept + lax.ppermute(passed, "tp", swap_pairs(count, 2)).astype(jnp.float32)


def shifted(count, step):
    return [(index, (index + step) % count) for index in range(count)]


def gather_axis(piece, name):
    count = lax.axis_size(name)
    mine = lax.axis_index(name)
    found = [piece] + [
        lax.ppermute(piece, name, shifted(count, -step)) for step in range(1, count)
    ]
    return lax.dynamic_slice_in_dim(
        jnp.stack(found + found[:-1]), (count - mine) % count, count, axis=0
    )


def gather_bit(piece, bit):
    other = lax.ppermute(piece, "tp", swap_pairs(lax.axis_size("tp"), bit))
    upper = (lax.axis_index("tp") & bit) > 0
    return jnp.where(upper, jnp.stack([other, piece]), jnp.stack([piece, other]))


def gather_dense(piece):
    fsdp_count, context_count = lax.axis_size("fsdp"), lax.axis_size("ctx")
    whole = gather_bit(gather_bit(gather_axis(gather_axis(piece, "fsdp"), "ctx"), 2), 1)
    whole = whole.reshape((2, 2, context_count, fsdp_count) + piece.shape)
    return whole.transpose(3, 2, 1, 0, 4, 5).reshape((-1,) + piece.shape)


def scatter_axis(parts, name):
    count = lax.axis_size(name)
    mine = lax.axis_index(name)
    low = parts.astype(jnp.bfloat16)
    total = lax.dynamic_index_in_dim(parts, mine, 0, keepdims=False).astype(jnp.float32)
    for step in range(1, count):
        sent = lax.dynamic_index_in_dim(low, (mine + step) % count, 0, keepdims=False)
        total = total + lax.ppermute(sent, name, shifted(count, step)).astype(jnp.float32)
    return total


def scatter_bit(parts, bit):
    mine = (lax.axis_index("tp") & bit) // bit
    sent = lax.dynamic_index_in_dim(parts, 1 - mine, 0, keepdims=False).astype(jnp.bfloat16)
    kept = lax.dynamic_index_in_dim(parts, mine, 0, keepdims=False).astype(jnp.float32)
    return kept + lax.ppermute(sent, "tp", swap_pairs(lax.axis_size("tp"), bit)).astype(
        jnp.float32
    )


def scatter_dense(parts):
    fsdp_count, context_count = lax.axis_size("fsdp"), lax.axis_size("ctx")
    parts = parts.reshape((fsdp_count, context_count, 2, 2) + parts.shape[1:])
    parts = parts.transpose(3, 2, 1, 0, 4, 5)
    return scatter_axis(scatter_axis(scatter_bit(scatter_bit(parts, 1), 2), "ctx"), "fsdp")


def hold(*refs):
    pass


def together(*values):
    spec = pl.BlockSpec(memory_space=pl.ANY)
    return pl.pallas_call(
        hold,
        in_specs=[spec] * len(values),
        out_specs=[spec] * len(values),
        out_shape=[jax.ShapeDtypeStruct(value.shape, value.dtype) for value in values],
        input_output_aliases={number: number for number in range(len(values))},
    )(*values)


def after(value, *earlier):
    spec = pl.BlockSpec(memory_space=pl.ANY)
    return pl.pallas_call(
        hold,
        in_specs=[spec] * (1 + len(earlier)),
        out_specs=spec,
        out_shape=jax.ShapeDtypeStruct(value.shape, value.dtype),
        input_output_aliases={0: 0},
    )(value, *earlier)


def per_device(
    tokens,
    routes,
    cotangent,
    norm_gains,
    query_key_value,
    attn_output,
    router_weight,
    expert_in,
    expert_out,
):
    local_seqs, local_positions, model_width = tokens.shape
    context_count = lax.axis_size("ctx")
    length = local_positions * context_count
    row_count = local_seqs * local_positions
    local_groups = KV_HEADS // context_count
    head_size = HEAD
    score_scale = HEAD ** (-0.5)
    capacity = local_positions * 3 // 8
    device_count = context_count * lax.axis_size("fsdp") * lax.axis_size("tp")
    inward_count, output_count = query_key_value.size, attn_output.size
    gain_count, router_count = norm_gains.size, router_weight.size
    packed = lax.all_gather(pack_rows([query_key_value, norm_gains], model_width), ALL_AXES, axis=0)
    packed_later = gather_dense(pack_rows([attn_output, router_weight], model_width))
    inward_rows, output_rows = query_key_value.shape[0], attn_output.shape[0]
    inward_full = packed[:, :inward_rows].reshape(-1, model_width)
    gain_full = (
        packed[:, inward_rows:]
        .reshape(device_count, -1)[:, :gain_count]
        .reshape(device_count, 2, -1)
        .transpose(1, 0, 2)
        .reshape(2, model_width)
    )
    output_full = packed_later[:, :output_rows].reshape(-1, model_width)
    router_full = (
        packed_later[:, output_rows:]
        .reshape(device_count, -1)[:, :router_count]
        .reshape(device_count, EXPERTS, -1)
        .transpose(1, 0, 2)
        .reshape(EXPERTS, model_width)
    )
    paired = context_count == 2
    expert_shards = jnp.concatenate([expert_in, expert_out[:, None]], axis=1)
    shard_depth = expert_in.shape[2]
    chunk_experts = EXPERTS // CHUNKS
    my_context = lax.axis_index("ctx").astype(jnp.int32)
    if paired:
        places = jnp.stack([my_context, 1 - my_context]) * shard_depth
        steps = (2 * shard_depth, 2 * shard_depth)
    else:
        places = jnp.zeros((1,), jnp.int32)
        steps = (shard_depth,)
    expert_pieces = []
    for chunk in range(CHUNKS):
        shard = expert_shards[chunk * chunk_experts : (chunk + 1) * chunk_experts]
        if paired:
            expert_pieces.append([lax.all_gather(shard, "fsdp", axis=0)])
        else:
            expert_pieces.append([lax.all_gather(shard, ("fsdp", "ctx"), axis=0)])
    gain_rows = gain_full.astype(jnp.float32)
    inputs = tokens.astype(jnp.float32).reshape(row_count, model_width)
    inverse_first = lax.rsqrt(jnp.mean(inputs * inputs, axis=1, keepdims=True) + EPS)
    normed_first = inputs * inverse_first
    first_low = (normed_first * gain_rows[0]).astype(jnp.bfloat16)
    projected = times_transposed(first_low, inward_full).reshape(
        local_seqs, local_positions, KV_HEADS, 4, head_size
    )
    positions = lax.axis_index("ctx") * local_positions + jnp.arange(
        local_positions, dtype=jnp.int32
    )
    cosine_table, sine_table = angle_tables(positions, head_size)
    cosine_rows = cosine_table[None, :, None, None, :]
    sine_rows = sine_table[None, :, None, None, :]
    turned = jnp.concatenate(
        [rotary(projected[:, :, :, :3], cosine_rows, sine_rows), projected[:, :, :, 3:]], axis=3
    )
    sent_heads = turned.astype(jnp.bfloat16).reshape(
        local_seqs, local_positions, KV_HEADS, 4 * head_size
    )
    head_rows = lax.all_to_all(sent_heads, "ctx", split_axis=2, concat_axis=1, tiled=True)
    queries = head_rows[..., : 2 * head_size].reshape(
        local_seqs, length, local_groups, 2, head_size
    )
    key_rows = head_rows[..., 2 * head_size : 3 * head_size]
    value_rows = head_rows[..., 3 * head_size :]
    block_rows = min(512, length)
    key_index = jnp.arange(length)
    attended = []
    log_totals = []
    for offset in range(0, length, block_rows):
        limit_row = offset + block_rows
        scores = (
            jnp.einsum(
                "sqgjd,skgd->sgjqk",
                queries[:, offset:limit_row],
                key_rows[:, :limit_row],
                preferred_element_type=jnp.float32,
            )
            * score_scale
        )
        visible = (offset + jnp.arange(block_rows))[:, None] >= key_index[None, :limit_row]
        scores = jnp.where(visible, scores, NEG)
        top_score = jnp.max(scores, axis=-1, keepdims=True)
        exponent = jnp.exp(scores - top_score)
        denominator = jnp.sum(exponent, axis=-1, keepdims=True)
        weights = exponent / denominator
        attended.append(
            jnp.einsum(
                "sgjqk,skgd->sqgjd",
                weights.astype(jnp.bfloat16),
                value_rows[:, :limit_row],
                preferred_element_type=jnp.float32,
            )
        )
        log_totals.append(top_score + jnp.log(denominator))
    head_output = (
        jnp.concatenate(attended, axis=1)
        .astype(jnp.bfloat16)
        .reshape(local_seqs, length, local_groups, 2 * head_size)
    )
    merged = lax.all_to_all(head_output, "ctx", split_axis=1, concat_axis=2, tiled=True).reshape(
        row_count, HEADS * head_size
    )
    hidden = inputs + times_transposed(merged, output_full)
    inverse_second = lax.rsqrt(jnp.mean(hidden * hidden, axis=1, keepdims=True) + EPS)
    normed_second = hidden * inverse_second
    second_low = (normed_second * gain_rows[1]).astype(jnp.bfloat16)
    group_rows = gather_group(second_low)
    group_grads = gather_group(cotangent.reshape(row_count, model_width))
    group_count = group_rows.shape[0]
    chances = jax.nn.softmax(times_transposed(group_rows, router_full), axis=-1)
    group_order = jnp.bitwise_xor(
        jnp.arange(lax.axis_size("tp"), dtype=jnp.int32), lax.axis_index("tp").astype(jnp.int32)
    )
    route_rows = jnp.take(
        routes.reshape(lax.axis_size("tp"), row_count, TOP), group_order, axis=0
    ).reshape(group_count, TOP)
    chosen_any = jnp.sum(
        (route_rows[:, :, None] == jnp.arange(EXPERTS, dtype=jnp.int32)[None, None, :]).astype(
            jnp.float32
        ),
        axis=1,
    )
    gates = jnp.pad(chances * chosen_any, ((0, 0), (0, LANES - EXPERTS)))
    group_turned = group_rows.T
    grads_turned = group_grads.T
    totals = None
    choice_total = None
    chunk_sums = []
    own_sums = []
    arrivals = []
    marks = []

    def fetch(chunk):
        near = expert_pieces[chunk][0]
        if chunk > 1:
            near = after(near, marks[chunk - 2])
            expert_pieces[chunk][0] = near
        expert_pieces[chunk].append(lax.ppermute(near, "ctx", swap_pairs(2, 1)))

    if paired:
        fetch(0)
    for chunk in range(CHUNKS):
        if paired:
            if chunk + 1 < CHUNKS:
                fetch(chunk + 1)
        moe_total, back_total, choice, *grad_pieces = expert_pass(
            places,
            steps,
            expert_pieces[chunk],
            group_rows,
            group_turned,
            group_grads,
            grads_turned,
            gates,
            totals,
            chunk * chunk_experts,
            arrivals[chunk - 2 : chunk - 1] if chunk > 1 else (),
        )
        totals = (moe_total, back_total)
        marks.append(choice)
        choice_total = choice if choice_total is None else choice_total + choice
        if paired:
            if chunk > 1:
                arrivals[chunk - 2] = grad_pieces[2]
            own_sums.append(grad_pieces[0])
            arrivals.append(lax.ppermute(grad_pieces[1], "ctx", swap_pairs(2, 1)))
        else:
            chunk_sums.append(
                lax.psum_scatter(grad_pieces[0], ("fsdp", "ctx"), scatter_dimension=0)
            )
    grad_chances = choice_total[:, :EXPERTS] * chosen_any
    grad_logits = chances * (grad_chances - jnp.sum(grad_chances * chances, axis=-1, keepdims=True))
    router_rows = router_full.astype(jnp.float32)
    grad_router = jnp.dot(grad_logits.T, group_rows.astype(jnp.float32), precision=HIGH)
    back_group = totals[1] + jnp.dot(grad_logits, router_rows, precision=HIGH)
    grad_second = scatter_group(back_group)
    moe_rows = scatter_group(totals[0])
    output = (hidden + moe_rows).astype(jnp.bfloat16).reshape(tokens.shape)
    grad_gain_second = jnp.sum(grad_second * normed_second, axis=0)
    grad_hidden = cotangent.astype(jnp.float32).reshape(row_count, model_width) + rms_back(
        grad_second, normed_second, inverse_second, gain_rows[1]
    )
    grad_attn = grad_hidden.astype(jnp.bfloat16)
    grad_output_weight = transposed_times(grad_attn, merged)
    grad_merged = (
        jnp.dot(grad_attn, output_full, preferred_element_type=jnp.float32)
        .astype(jnp.bfloat16)
        .reshape(local_seqs, local_positions, KV_HEADS, 2 * head_size)
    )
    grad_heads = lax.all_to_all(grad_merged, "ctx", split_axis=2, concat_axis=1, tiled=True)
    if paired:
        grad_heads, arrivals[-2] = together(grad_heads, arrivals[-2])
    grad_keys = jnp.zeros((local_seqs, length, local_groups, head_size), jnp.float32)
    grad_values = jnp.zeros((local_seqs, length, local_groups, head_size), jnp.float32)
    grad_query_blocks = []
    for offset, log_total in zip(range(0, length, block_rows), log_totals):
        limit_row = offset + block_rows
        query_block = queries[:, offset:limit_row]
        key_part = key_rows[:, :limit_row]
        value_part = value_rows[:, :limit_row]
        scores = (
            jnp.einsum(
                "sqgjd,skgd->sgjqk", query_block, key_part, preferred_element_type=jnp.float32
            )
            * score_scale
        )
        visible = (offset + jnp.arange(block_rows))[:, None] >= key_index[None, :limit_row]
        scores = jnp.where(visible, scores, NEG)
        weights = jnp.exp(scores - log_total)
        grad_block = grad_heads[:, offset:limit_row].reshape(
            local_seqs, block_rows, local_groups, 2, head_size
        )
        grad_values = grad_values.at[:, :limit_row].add(
            jnp.einsum(
                "sgjqk,sqgjd->skgd",
                weights.astype(jnp.bfloat16),
                grad_block,
                preferred_element_type=jnp.float32,
            )
        )
        grad_weights = jnp.einsum(
            "sqgjd,skgd->sgjqk", grad_block, value_part, preferred_element_type=jnp.float32
        )
        grad_scores = (
            weights * (grad_weights - jnp.sum(weights * grad_weights, axis=-1, keepdims=True))
        ).astype(jnp.bfloat16)
        grad_query_blocks.append(
            jnp.einsum(
                "sgjqk,skgd->sqgjd", grad_scores, key_part, preferred_element_type=jnp.float32
            )
            * score_scale
        )
        grad_keys = grad_keys.at[:, :limit_row].add(
            jnp.einsum(
                "sgjqk,sqgjd->skgd", grad_scores, query_block, preferred_element_type=jnp.float32
            )
            * score_scale
        )
    grad_queries = jnp.concatenate(grad_query_blocks, axis=1).reshape(
        local_seqs, length, local_groups, 2 * head_size
    )
    grad_head_rows = jnp.concatenate([grad_queries, grad_keys, grad_values], axis=-1).astype(
        jnp.bfloat16
    )
    if paired:
        grad_head_rows, arrivals[-1] = together(grad_head_rows, arrivals[-1])
        for own, arrived in zip(own_sums, arrivals):
            joined = (own.astype(jnp.float32) + arrived.astype(jnp.float32)).astype(jnp.bfloat16)
            chunk_sums.append(lax.psum_scatter(joined, "fsdp", scatter_dimension=0))
    grad_turned = (
        lax.all_to_all(grad_head_rows, "ctx", split_axis=1, concat_axis=2, tiled=True)
        .astype(jnp.float32)
        .reshape(local_seqs, local_positions, KV_HEADS, 4, head_size)
    )
    grad_projected = (
        jnp.concatenate(
            [
                rotary_back(grad_turned[:, :, :, :3], cosine_rows, sine_rows),
                grad_turned[:, :, :, 3:],
            ],
            axis=3,
        )
        .astype(jnp.bfloat16)
        .reshape(row_count, -1)
    )
    grad_inward = transposed_times(grad_projected, first_low)
    grad_first = jnp.dot(grad_projected, inward_full, preferred_element_type=jnp.float32)
    grad_gain_first = jnp.sum(grad_first * normed_first, axis=0)
    grad_inputs = grad_hidden + rms_back(grad_first, normed_first, inverse_first, gain_rows[0])

    def by_device(array, axis):
        parts = array.reshape(
            array.shape[:axis] + (device_count, -1) + array.shape[axis + 1 :]
        )
        return jnp.moveaxis(parts, axis, 0).reshape(device_count, -1)

    def sum_dense(terms):
        flat = jnp.concatenate(terms, axis=1)
        rows = -(-flat.shape[1] // (8 * model_width)) * 8
        flat = jnp.pad(flat, ((0, 0), (0, rows * model_width - flat.shape[1])))
        return scatter_dense(flat.reshape(device_count, rows, model_width)).reshape(-1)

    half_gains = gain_count // 2
    early = sum_dense(
        [
            by_device(grad_output_weight, 0),
            by_device(grad_router, 1),
            by_device(grad_gain_second, 0),
        ]
    )
    late = sum_dense([by_device(grad_inward, 0), by_device(grad_gain_first, 0)])
    grad_gains = jnp.stack(
        [
            late[inward_count : inward_count + half_gains],
            early[output_count + router_count : output_count + router_count + half_gains],
        ]
    )
    expert_sums = jnp.concatenate(chunk_sums, axis=0).astype(jnp.float32)
    return (
        output,
        grad_inputs.reshape(tokens.shape),
        grad_gains,
        late[:inward_count].reshape(query_key_value.shape),
        early[:output_count].reshape(attn_output.shape),
        early[output_count : output_count + router_count].reshape(router_weight.shape),
        expert_sums[:, :2],
        expert_sums[:, 2],
    )


def solution(mesh):
    placed = (
        P(("fsdp", "tp"), "ctx", None),
        P("fsdp", "ctx", None),
        P(("fsdp", "tp"), "ctx", None),
        P(None, ("fsdp", "ctx", "tp")),
        P(("fsdp", "ctx", "tp"), None),
        P(("fsdp", "ctx", "tp"), None),
        P(None, ("fsdp", "ctx", "tp")),
        P(None, None, ("fsdp", "ctx"), "tp"),
        P(None, ("fsdp", "ctx"), "tp"),
    )
    return jax.shard_map(
        per_device,
        mesh=mesh,
        in_specs=placed,
        out_specs=(
            P(("fsdp", "tp"), "ctx", None),
            P(("fsdp", "tp"), "ctx", None),
            P(None, ("fsdp", "ctx", "tp")),
            P(("fsdp", "ctx", "tp"), None),
            P(("fsdp", "ctx", "tp"), None),
            P(None, ("fsdp", "ctx", "tp")),
            P(None, None, ("fsdp", "ctx"), "tp"),
            P(None, ("fsdp", "ctx"), "tp"),
        ),
        check_vma=False,
    )
```

time: 3090 us -> 1160 us (0.38)
  waiting for transfers between devices: 1820 us -> 330 us
  matrix products: 825 us -> 104 us
  Pallas kernels: 0 us -> 275 us
  blocking collectives: 99 us -> 0 us
  local copies, waits for them, and re-layouts: 152 us -> 224 us
  starting transfers between devices: 13.6 us -> 54 us
    reduce_scatter x6 -> x4, waiting for transfers between devices: 1200 us -> 0.04 us  [per_device(): chunk_sums.append(lax.psum_scatter(joined, 'fsdp', scatter_dimension=0))]
    dot_general x122 -> x2, matrix products: 728 us -> 13.1 us  [the longest x1 6.91 us: per_device(): jnp.dot(grad_logits.T, group_rows.astype(jnp.float32), precision=HIGH)]
    all_gather x6 -> x5, waiting for transfers between devices: 347 us -> 51.6 us  [the longest x1 51.5 us: per_device(): lax.all_gather(pack_rows([query_key_value, norm_gains], model_width), ALL...]
    pallas_call x0 -> x8, Pallas kernels: none -> 275 us  [the longest x4 275 us: expert_pass(): pl.pallas_call(functools.partial(expert_kernel, first, steps, base_expert...]
    ppermute x0 -> x36, waiting for transfers between devices: none -> 246 us  [the longest x4 141 us: fetch(): expert_pieces[chunk].append(lax.ppermute(near, 'ctx', swap_pairs(2, 1)))]
    unnamed x16 -> x9, waiting for transfers between devices: 216 us -> 0.81 us
    all_gather x2 -> x0, blocking collectives: 82.8 us -> none  [the longest x1 43.3 us: per_device(): lax.all_gather(norm_gains, ('fsdp', 'ctx', 'tp'), axis=1, tiled=True)]
    slice x0 -> x11, local copies, waits for them, and re-layouts: none -> 79 us  [the longest x2 69.7 us: scatter_group(): parts[1::2].astype(jnp.bfloat16)]
  transfers between devices with their start and end apart: 17 -> 49, of which waited for: 14 -> 21; matrix products, arithmetic and copies ran while one was open for 14% -> 38% of each run, Pallas kernels for 0% -> 18%
where the time goes in v1:
time: 1160 us; the launch traced here: 1150 us
  waiting for transfers between devices  330 us (28%)
  Pallas kernels  275 us (24%)
  local copies, waits for them, and re-layouts  224 us (19%)
  other arithmetic  145 us (12%)
  matrix products  104 us (9%)
  starting transfers between devices  54 us (5%)
  between operations  15.7 us (1%)
    pallas_call x4, Pallas kernels, expert_pass(): pl.pallas_call(functools.partial(expert_kernel, first, steps, base_expert...  275 us
    ppermute x4, waiting for transfers between devices, fetch(): expert_pieces[chunk].append(lax.ppermute(near, 'ctx', swap_pairs(2, 1)))  141 us
    slice x2, local copies, waits for them, and re-layouts, scatter_group(): parts[1::2].astype(jnp.bfloat16)  69.7 us
    all_gather x1, waiting for transfers between devices, per_device(): lax.all_gather(pack_rows([query_key_value, norm_gains], model_width), ALL...  51.5 us
    unnamed x181, local copies, waits for them, and re-layouts  50.5 us
    another operation x7, other arithmetic  35.1 us
    ppermute x8, waiting for transfers between devices, scatter_axis(): lax.ppermute(sent, name, shifted(count, step)).astype(jnp.float32)  23.7 us
  transfers between devices with their start and end apart: 49, of which 21 were waited for; matrix products, arithmetic and copies ran while one was open for 38% of the time, Pallas kernels for 18%

profile of v1, /device:TPU:0, one launch (start us, length us, event | category | flops | bytes accessed | tf_op | source)
XLA Modules:
  0.0 1147.7 jit_solution(17807167810298271950)
XLA Ops:
  9.8 3.7 pad_maximum_fusion.7
  22.7 4.0 collective-permute-done
  28.5 51.5 %all-gather.10.cloned.1.call-done = bf16[32,80,1024]{2,1,0:T(8,128)(2,1)} async-done(((bf16[1,80,1024]{2,1,0:T(8,128)(2,1)}), bf16[32,80,1024]{2,1,0:T(8,128)(2,1)}) %all-gather.10.cloned.1.call-update) | async-done | bytes 5242896 | tf_op jit(solution)/shard_map/all_gather | solution.py:436
  89.5 3.8 all-to-all-start
  101.0 14.5 %collective-permute-done.4 = bf16[2,4,48,1024]{3,2,0,1:T(8,128)(2,1)} collective-permute-done((bf16[2,4,48,1024]{3,2,0,1:T(8,128)(2,1)}, bf16[2,4,48,1024]{3,2,0,1:T(8,128)(2,1)}, u32[]{:S(2)}, u32[]{:S(2)}) %collective-permute-start.4) | collective-permute-done | bytes 786464 | tf_op jit(solution)/shard_map/ppermute | solution.py:349
  132.8 7.5 fusion.118
  140.4 8.0 fusion.3
  149.8 9.0 fusion.63
  161.7 4.5 all-to-all-start.1
  171.7 8.8 all-to-all-done.1
  194.2 21.8 %collective-permute-done.8 = bf16[512,1024]{0,1:T(8,128)(2,1)} collective-permute-done((bf16[512,1024]{0,1:T(8,128)(2,1)}, bf16[512,1024]{0,1:T(8,128)(2,1)}, u32[]{:S(2)}, u32[]{:S(2)}) %collective-permute-start.8) | collective-permute-done | bytes 1048608 | tf_op jit(solution)/shard_map/ppermute | solution.py:316
  218.3 5.8 fusion.111
  224.1 6.4 copy.249.refs_4_
  232.2 3.8 pad_maximum_fusion
  236.0 6.4 copy.248.refs_2_
  248.4 3.9 fusion.141.refs_3_
  252.3 12.3 %collective-permute-done.13.refs_1_ = bf16[4,8,3,128,128]{4,3,2,1,0:T(8,128)(2,1)} collective-permute-done((bf16[4,8,3,128,128]{4,3,2,1,0:T(8,128)(2,1)}, bf16[4,8,3,128,128]{4,3,2,1,0:T(8,128)(2,1)}, u32[]{:S(2)}, u32[]{:S(2)}) %collective-permute-start.13) | collective-permute-done | bytes 3145760 | tf_op jit(solution)/shard_map/ppermute | solution.py:572
  264.6 60.5 %shard_map.162 = (f32[2048,1024]{1,0:T(8,128)}, f32[2048,1024]{1,0:T(8,128)}, f32[2048,128]{1,0:T(8,128)}, bf16[4,8,3,128,128]{4,3,2,1,0:T(8,128)(2,1)}, bf16[4,8,3,128,128]{4,3,2,1,0:T(8,128)(2,1)}) custom-call(s32[2]{0:T(128)} %add_multiply_fusion.places_ref, bf16[4,8,3,128,128]{4,3,2,1,0:T(8,128)(2,1)} %bitcast.511, ...), custom_call_target="tpu_custom_call" | custom-call | flops 38654705664 | bytes 41943040 | tf_op jit(solution)/shard_map/pallas_call | solution.py:267
  327.2 4.8 collective-permute-done.6.refs_1_
  332.0 71.4 %shard_map.163 = (f32[2048,1024]{1,0:T(8,128)}, f32[2048,1024]{1,0:T(8,128)}, f32[2048,128]{1,0:T(8,128)}, bf16[4,8,3,128,128]{4,3,2,1,0:T(8,128)(2,1)}, bf16[4,8,3,128,128]{4,3,2,1,0:T(8,128)(2,1)}) custom-call(s32[2]{0:T(128)} %add_multiply_fusion.places_ref, bf16[4,8,3,128,128]{4,3,2,1,0:T(8,128)(2,1)} %bitcast.509, ...), custom_call_target="tpu_custom_call", output_to_operand_aliasing={{0}: (8, {}), {1}: (9, {})} | custom-call | flops 38654705664 | bytes 41943040 | tf_op jit(solution)/shard_map/pallas_call | solution.py:267
  405.5 61.3 %collective-permute-done.15.refs_1_ = bf16[4,8,3,128,128]{4,3,2,1,0:T(8,128)(2,1)} collective-permute-done((bf16[4,8,3,128,128]{4,3,2,1,0:T(8,128)(2,1)}, bf16[4,8,3,128,128]{4,3,2,1,0:T(8,128)(2,1)}, u32[]{:S(2)}, u32[]{:S(2)}) %collective-permute-start.15) | collective-permute-done | bytes 3145760 | tf_op jit(solution)/shard_map/ppermute | solution.py:572
  466.8 71.1 %shard_map.166 = (f32[2048,1024]{1,0:T(8,128)}, f32[2048,1024]{1,0:T(8,128)}, f32[2048,128]{1,0:T(8,128)}, bf16[4,8,3,128,128]{4,3,2,1,0:T(8,128)(2,1)}, bf16[4,...) custom-call(s32[2]{0:T(128)} %add_multiply_fusion.places_ref, ...), custom_call_target="tpu_custom_call", output_to_operand_aliasing={{0}: (8, {}), {1}: (9, {}), {5}: (10, {})} | custom-call | flops 38654705664 | bytes 41943040 | tf_op jit(solution)/shard_map/pallas_call | solution.py:267
  538.0 62.8 %collective-permute-done.14.refs_1_ = bf16[4,8,3,128,128]{4,3,2,1,0:T(8,128)(2,1)} collective-permute-done((bf16[4,8,3,128,128]{4,3,2,1,0:T(8,128)(2,1)}, bf16[4,8,3,128,128]{4,3,2,1,0:T(8,128)(2,1)}, u32[]{:S(2)}, u32[]{:S(2)}) %collective-permute-start.14) | collective-permute-done | bytes 3145760 | tf_op jit(solution)/shard_map/ppermute | solution.py:572
  600.8 71.5 %shard_map.167 = (f32[2048,1024]{1,0:T(8,128)}, f32[2048,1024]{1,0:T(8,128)}, f32[2048,128]{1,0:T(8,128)}, bf16[4,8,3,128,128]{4,3,2,1,0:T(8,128)(2,1)}, bf16[4,...) custom-call(s32[2]{0:T(128)} %add_multiply_fusion.places_ref, ...), custom_call_target="tpu_custom_call", output_to_operand_aliasing={{0}: (8, {}), {1}: (9, {}), {5}: (10, {})} | custom-call | flops 38654705664 | bytes 41943040 | tf_op jit(solution)/shard_map/pallas_call | solution.py:267
  672.4 5.4 add_convert_fusion.2
  677.9 9.3 copy.258
  691.0 6.2 fusion.105
  697.2 13.4 %fusion.115 = (bf16[2048,1024]{0,1:T(8,128)(2,1)}, f32[2048,1024]{0,1:T(8,128)}) fusion(f32[2048,1024]{0,1:T(8,128)} %copy.258, f32[2048,1024]{0,1:T(8,128)} %fusion.105), kind=kLoop, calls=%fused_computation.241 | loop fusion | flops 4194304 | bytes 29360128 | tf_op jit(solution)/shard_map/convert.22
  710.6 7.9 reshape.855
  718.5 68.2 %slice.296 = bf16[2,512,1024]{1,0,2:T(2,128)(2,1)} slice(bf16[4,512,1024]{1,0,2:T(4,128)(2,1)} %reshape.855), slice={[1:4:2], [0:512:1], [0:1024:1]} | slice | bytes 4194304 | tf_op jit(solution)/shard_map/slice | solution.py:326
  790.0 4.0 convert.69
  795.5 3.9 copy.306
  808.0 9.5 copy.254
  829.2 4.0 collective-permute-done.21
  833.3 4.4 multiply_reduce_fusion
  837.7 17.2 %collective-permute-done.19 = bf16[512,1024]{0,1:T(8,128)(2,1)} collective-permute-done((bf16[512,1024]{0,1:T(8,128)(2,1)}, bf16[512,1024]{0,1:T(8,128)(2,1)}, u32[]{:S(2)}, u32[]{:S(2)}) %collective-permute-start.19) | collective-permute-done | bytes 1048608 | tf_op jit(solution)/shard_map/ppermute | solution.py:330
  854.9 4.4 multiply_add_fusion
  867.7 22.3 %all-to-all-done.2 = bf16[1,512,8,128]{3,1,0,2:T(8,128)(2,1)S(1)} async-done(((bf16[1,512,8,128]{3,1,0,2:T(8,128)(2,1)}), bf16[1,512,8,128]{3,1,0,2:T(8,128)(2,1)S(1)}, u32[]{:S(2)}, u32[]{:S(2)}) %all-to-all-start.2) | async-done | bytes 1048608 | tf_op jit(solution)/shard_map/all_to_all | solution.py:624
  893.7 4.8 fusion.68
  900.2 9.6 fusion.53
  912.6 5.3 fusion.9
  918.0 4.7 fusion.20
  927.4 4.0 fusion.67
  931.5 4.9 add_convert_fusion.1
  936.4 10.3 fusion
  946.7 8.3 fusion.8
  961.8 7.1 fusion.56
  978.5 5.0 all-to-all-start.3
  983.5 6.9 fusion.104
  991.3 5.2 fusion.87
  996.4 5.1 reshape_reshape.14
  1001.5 4.9 add_convert_fusion
  1012.2 5.9 fusion.76
  1018.1 4.0 fusion.36
  1022.1 7.9 reshape_reshape.12
  1030.0 4.0 select_maximum_fusion
  1034.0 5.5 copy.316
  1058.3 3.9 bitcast_add_fusion
  1066.1 8.4 collective-permute-done.31
  1081.1 4.1 collective-permute-done.32
  1091.2 7.7 collective-permute-done.25
  1108.2 8.1 collective-permute-done.26
  1122.2 4.6 collective-permute-done.27
  1127.4 6.3 collective-permute-done.28
  (402 shorter events, 216.4 us)
Async XLA Ops:
  7.2 186.4 %copy-start = (s32[4,512,8]{1,2,0:T(8,128)S(1)}, s32[4,512,8]{1,2,0:T(8,128)}, u32[]{:S(2)}) copy-start(s32[4,512,8]{1,2,0:T(8,128)} %param.22) | copy-start | bytes 196612
  7.2 72.9 %all-gather.10.cloned.1.call-start = ((), (), s32[]{:S(2)}) async-start(), calls=%async_computation.8 | async-start | bytes 5406720 | tf_op jit(solution)/shard_map/all_gather | solution.py:436
  9.7 183.6 %all-gather.16.cloned.1.call-start = ((), (), s32[]{:S(2)}) async-start(), calls=%async_computation.15 | async-start | bytes 3932160 | tf_op jit(solution)/shard_map/all_gather | solution.py:470
  9.8 11.7 %copy-start.48 = (bf16[1,512,1024]{2,1,0:T(8,128)(2,1)S(1)}, bf16[1,512,1024]{2,1,0:T(8,128)(2,1)}, u32[]{:S(2)}) copy-start(bf16[1,512,1024]{2,1,0:T(8,128)(2,1)} %param.21) | copy-start | bytes 3145732
  13.4 218.4 %all-gather.14.cloned.1.call-start = ((), (), s32[]{:S(2)}) async-start(), calls=%async_computation.14 | async-start | bytes 3932160 | tf_op jit(solution)/shard_map/all_gather | solution.py:470
  14.4 12.4 %collective-permute-start.2 = (bf16[48,1024]{1,0:T(8,128)(2,1)S(1)}, bf16[48,1024]{1,0:T(8,128)(2,1)S(1)}, u32[]{:S(2)}, u32[]{:S(2)}) collective-permute-start(bf16[48,1024]{1,0:T(8,128)(2,1)S(1)} %reshape.845), channel_id=1, source_target_pairs={{0,8},{8,16},{16,24},{24,0},{1,9},{9,17},{17,25},{25,1},{2,10},{10... | collective-permute-start | bytes 294920 | tf_op jit(solution)/shard_map/ppermute | solution.py:341
  17.4 9.3 collective-permute-start.1
  20.0 6.7 collective-permute-start
  22.0 62.9 %copy-start.21 = (bf16[1,512,1024]{1,2,0:T(8,128)(2,1)}, bf16[1,512,1024]{1,2,0:T(8,128)(2,1)S(1)}, u32[]{:S(2)}) copy-start(bf16[1,512,1024]{1,2,0:T(8,128)(2,1)S(1)} %copy.230) | copy-start | bytes 3145732
  22.3 62.5 %copy-start.75 = (f32[512]{0:T(512)}, f32[512]{0:T(512)S(1)}, u32[]{:S(2)}) copy-start(f32[512]{0:T(512)S(1)} %add_rsqrt_fusion.1) | copy-start | bytes 6148
  22.7 64.8 %copy-start.51 = (f32[512,32]{0,1:T(8,128)}, f32[512,32]{0,1:T(8,128)S(1)}, u32[]{:S(2)}) copy-start(f32[512,32]{0,1:T(8,128)S(1)} %get-tuple-element.199) | copy-start | bytes 196612
  22.7 64.8 %copy-start.53 = (f32[512,32]{0,1:T(8,128)}, f32[512,32]{0,1:T(8,128)S(1)}, u32[]{:S(2)}) copy-start(f32[512,32]{0,1:T(8,128)S(1)} %get-tuple-element.200) | copy-start | bytes 196612
  26.9 66.6 %collective-permute-start.3 = (bf16[4,48,1024]{2,1,0:T(8,128)(2,1)S(1)}, bf16[4,48,1024]{2,1,0:T(8,128)(2,1)S(1)}, u32[]{:S(2)}, u32[]{:S(2)}) collective-permute-start(bf16[4,48,1024]{2,1,0:T(8,128)(2,1)S(1)} %constant_dynamic-slice_fusion), channel_id=1, source_target_pairs={{0,4},{4,0},{1,5},{5,1},{2,6},{6,2},{3,7},{7,3},{8,12},{12,8},{9,1... | collective-permute-start | bytes 1179656 | tf_op jit(solution)/shard_map/ppermute | solution.py:341
  89.5 29.3 %all-to-all-start = ((bf16[1,512,8,256]{1,3,0,2:T(8,128)(2,1)}), bf16[1,512,8,256]{1,3,0,2:T(8,128)(2,1)S(1)}, u32[]{:S(2)}, u32[]{:S(2)}) async-start(bf16[1,512,8,256]{1,3,0,2:T(8,128)(2,1)} %bitcast.445), calls=%async_computation | async-start | bytes 4194304 | tf_op jit(solution)/shard_map/all_to_all | solution.py:493
  93.3 231.9 %all-gather.18.cloned.1.call-start = ((), (), s32[]{:S(2)}) async-start(), calls=%async_computation.16 | async-start | bytes 3932160 | tf_op jit(solution)/shard_map/all_gather | solution.py:470
  94.8 20.7 %collective-permute-start.4 = (bf16[2,4,48,1024]{3,2,0,1:T(8,128)(2,1)}, bf16[2,4,48,1024]{3,2,0,1:T(8,128)(2,1)}, u32[]{:S(2)}, u32[]{:S(2)}) collective-permute-start(bf16[2,4,48,1024]{3,2,0,1:T(8,128)(2,1)} %fusion.81), channel_id=1, source_target_pairs={{0,2},{1,3},{2,0},{3,1},{4,6},{5,7},{6,4},{7,5},{8,10},{9,11},{10,... | collective-permute-start | bytes 2359304 | tf_op jit(solution)/shard_map/ppermute | solution.py:349
  98.5 94.2 %collective-permute-start.11 = (bf16[512,1024]{0,1:T(8,128)(2,1)}, bf16[512,1024]{0,1:T(8,128)(2,1)}, u32[]{:S(2)}, u32[]{:S(2)}) collective-permute-start(bf16[512,1024]{0,1:T(8,128)(2,1)} %bitcast.59), channel_id=1, source_target_pairs={{0,2},{1,3},{2,0},{3,1},{4,6},{5,7},{6,4},{7,5},{8,10},{9,11},{10,... | collective-permute-start | bytes 3145736 | tf_op jit(solution)/shard_map/ppermute | solution.py:316
  118.3 50.0 %collective-permute-start.5 = (bf16[2,2,4,48,1024]{4,3,1,2,0:T(8,128)(2,1)}, bf16[2,2,4,48,1024]{4,3,1,2,0:T(8,128)(2,1)}, u32[]{:S(2)}, u32[]{:S(2)}) collective-permute-start(bf16[2,2,4,48,1024]{4,3,1,2,0:T(8,128)(2,1)} %maximum_select_fusion.1), channel_id=1, source_target_pairs={{0,1},{1,0},{2,3},{3,2},{4,5},{5,4},{6,7},{7,6},{8,9},{9,8},{10,11... | collective-permute-start | bytes 4718600 | tf_op jit(solution)/shard_map/ppermute | solution.py:349
  125.5 24.2 %copy-start.18 = (bf16[1,1024,4,256]{1,3,2,0:T(8,128)(2,1)}, bf16[1,1024,4,256]{1,3,2,0:T(8,128)(2,1)S(1)}, u32[]{:S(2)}) copy-start(bf16[1,1024,4,256]{1,3,2,0:T(8,128)(2,1)S(1)} %all_to_all.47) | copy-start | bytes 6291460
  161.7 18.8 %all-to-all-start.1 = ((bf16[1,1024,4,128]{3,2,0,1:T(4,128)(2,1)}), bf16[1,1024,4,128]{3,2,0,1:T(4,128)(2,1)}, u32[]{:S(2)}, u32[]{:S(2)}) async-start(bf16[1,1024,4,128]{3,2,0,1:T(4,128)(2,1)} %pad_maximum_fusion.5), calls=%async_computation.1 | async-start | bytes 2097152 | tf_op jit(solution)/shard_map/all_to_all | solution.py:534
  166.2 237.3 %all-gather.12.cloned.1.call-start = ((), (), s32[]{:S(2)}) async-start(), calls=%async_computation.13 | async-start | bytes 3932160 | tf_op jit(solution)/shard_map/all_gather | solution.py:470
  171.7 16.9 %copy-start.62 = (f32[1024]{0:T(1024)}, f32[1024]{0:T(1024)S(1)}, u32[]{:S(2)}) copy-start(f32[1024]{0:T(1024)S(1)} %mul.297) | copy-start | bytes 12292
  191.2 24.8 %collective-permute-start.8 = (bf16[512,1024]{0,1:T(8,128)(2,1)}, bf16[512,1024]{0,1:T(8,128)(2,1)}, u32[]{:S(2)}, u32[]{:S(2)}) collective-permute-start(bf16[512,1024]{0,1:T(8,128)(2,1)} %multiply_convert_fusion), channel_id=1, source_target_pairs={{0,2},{1,3},{2,0},{3,1},{4,6},{5,7},{6,4},{7,5},{8,10},{9,11},{10,... | collective-permute-start | bytes 3145736 | tf_op jit(solution)/shard_map/ppermute | solution.py:316
  192.6 25.6 %collective-permute-start.10 = (bf16[512,1024]{0,1:T(8,128)(2,1)}, bf16[512,1024]{0,1:T(8,128)(2,1)}, u32[]{:S(2)}, u32[]{:S(2)}) collective-permute-start(bf16[512,1024]{0,1:T(8,128)(2,1)} %bitcast.59), channel_id=1, source_target_pairs={{0,1},{1,0},{2,3},{3,2},{4,5},{5,4},{6,7},{7,6},{8,9},{9,8},{10,11... | collective-permute-start | bytes 3145736 | tf_op jit(solution)/shard_map/ppermute | solution.py:317
  192.7 942.5 %reduce-scatter.7.cloned.1.call-start = ((), (), s32[]{:S(2)}) async-start(), calls=%async_computation.10 | async-start | bytes 3932160 | tf_op jit(solution)/shard_map/reduce_scatter | solution.py:683
  192.7 25.5 %collective-permute-start.12 = (bf16[512,1024]{0,1:T(8,128)(2,1)}, bf16[512,1024]{0,1:T(8,128)(2,1)}, u32[]{:S(2)}, u32[]{:S(2)}) collective-permute-start(bf16[512,1024]{0,1:T(8,128)(2,1)} %collective-permute-done.11), channel_id=1, source_target_pairs={{0,1},{1,0},{2,3},{3,2},{4,5},{5,4},{6,7},{7,6},{8,9},{9,8},{10,11... | collective-permute-start | bytes 3145736 | tf_op jit(solution)/shard_map/ppermute | solution.py:318
  193.3 71.3 %collective-permute-start.13 = (bf16[4,8,3,128,128]{4,3,2,1,0:T(8,128)(2,1)}, bf16[4,8,3,128,128]{4,3,2,1,0:T(8,128)(2,1)}, u32[]{:S(2)}, u32[]{:S(2)}) collective-permute-start(bf16[4,8,3,128,128]{4,3,2,1,0:T(8,128)(2,1)} %bitcast.510), channel_id=1, source_target_pairs={{0,4},{4,0},{1,5},{5,1},{2,6},{6,2},{3,7},{7,3},{8,12},{12,8},{9,1... | collective-permute-start | bytes 9437192 | tf_op jit(solution)/shard_map/ppermute | solution.py:572
  194.1 38.1 %collective-permute-start.7 = (bf16[512,1024]{0,1:T(8,128)(2,1)}, bf16[512,1024]{0,1:T(8,128)(2,1)}, u32[]{:S(2)}, u32[]{:S(2)}) collective-permute-start(bf16[512,1024]{0,1:T(8,128)(2,1)} %multiply_convert_fusion), channel_id=1, source_target_pairs={{0,1},{1,0},{2,3},{3,2},{4,5},{5,4},{6,7},{7,6},{8,9},{9,8},{10,11... | collective-permute-start | bytes 3145736 | tf_op jit(solution)/shard_map/ppermute | solution.py:317
  216.0 16.2 %collective-permute-start.9 = (bf16[512,1024]{0,1:T(8,128)(2,1)}, bf16[512,1024]{0,1:T(8,128)(2,1)}, u32[]{:S(2)}, u32[]{:S(2)}) collective-permute-start(bf16[512,1024]{0,1:T(8,128)(2,1)} %collective-permute-done.8), channel_id=1, source_target_pairs={{0,1},{1,0},{2,3},{3,2},{4,5},{5,4},{6,7},{7,6},{8,9},{9,8},{10,11... | collective-permute-start | bytes 3145736 | tf_op jit(solution)/shard_map/ppermute | solution.py:318
  231.8 100.2 %collective-permute-start.6 = (bf16[4,8,3,128,128]{4,3,2,1,0:T(8,128)(2,1)}, bf16[4,8,3,128,128]{4,3,2,1,0:T(8,128)(2,1)}, u32[]{:S(2)}, u32[]{:S(2)}) collective-permute-start(bf16[4,8,3,128,128]{4,3,2,1,0:T(8,128)(2,1)} %bitcast.508), channel_id=1, source_target_pairs={{0,4},{4,0},{1,5},{5,1},{2,6},{6,2},{3,7},{7,3},{8,12},{12,8},{9,1... | collective-permute-start | bytes 9437192 | tf_op jit(solution)/shard_map/ppermute | solution.py:572
  325.1 80.4 %collective-permute-start.16 = (bf16[4,8,3,128,128]{4,3,2,1,0:T(8,128)(2,1)}, bf16[4,8,3,128,128]{4,3,2,1,0:T(8,128)(2,1)S(1)}, u32[]{:S(2)}, u32[]{:S(2)}) collective-permute-start(bf16[4,8,3,128,128]{4,3,2,1,0:T(8,128)(2,1)} %get-tuple-element.104), channel_id=1, source_target_pairs={{0,4},{4,0},{1,5},{5,1},{2,6},{6,2},{3,7},{7,3},{8,12},{12,8},{9,1... | collective-permute-start | bytes 9437192 | tf_op jit(solution)/shard_map/ppermute | solution.py:600
  325.2 141.6 %collective-permute-start.15 = (bf16[4,8,3,128,128]{4,3,2,1,0:T(8,128)(2,1)}, bf16[4,8,3,128,128]{4,3,2,1,0:T(8,128)(2,1)}, u32[]{:S(2)}, u32[]{:S(2)}) collective-permute-start(bf16[4,8,3,128,128]{4,3,2,1,0:T(8,128)(2,1)} %shard_map.165.refs_0_), channel_id=1, source_target_pairs={{0,4},{4,0},{1,5},{5,1},{2,6},{6,2},{3,7},{7,3},{8,12},{12,8},{9,1... | collective-permute-start | bytes 9437192 | tf_op jit(solution)/shard_map/ppermute | solution.py:572
  403.4 134.6 %collective-permute-start.17 = (bf16[4,8,3,128,128]{4,3,2,1,0:T(8,128)(2,1)}, bf16[4,8,3,128,128]{4,3,2,1,0:T(8,128)(2,1)}, u32[]{:S(2)}, u32[]{:S(2)}) collective-permute-start(bf16[4,8,3,128,128]{4,3,2,1,0:T(8,128)(2,1)} %get-tuple-element.107), channel_id=1, source_target_pairs={{0,4},{4,0},{1,5},{5,1},{2,6},{6,2},{3,7},{7,3},{8,12},{12,8},{9,1... | collective-permute-start | bytes 9437192 | tf_op jit(solution)/shard_map/ppermute | solution.py:600
  403.5 197.3 %collective-permute-start.14 = (bf16[4,8,3,128,128]{4,3,2,1,0:T(8,128)(2,1)}, bf16[4,8,3,128,128]{4,3,2,1,0:T(8,128)(2,1)}, u32[]{:S(2)}, u32[]{:S(2)}) collective-permute-start(bf16[4,8,3,128,128]{4,3,2,1,0:T(8,128)(2,1)} %shard_map.164.refs_0_), channel_id=1, source_target_pairs={{0,4},{4,0},{1,5},{5,1},{2,6},{6,2},{3,7},{7,3},{8,12},{12,8},{9,1... | collective-permute-start | bytes 9437192 | tf_op jit(solution)/shard_map/ppermute | solution.py:572
  405.5 61.4 %copy-start.43 = (bf16[4,8,3,128,128]{4,3,2,1,0:T(8,128)(2,1)}, bf16[4,8,3,128,128]{4,3,2,1,0:T(8,128)(2,1)S(1)}, u32[]{:S(2)}) copy-start(bf16[4,8,3,128,128]{4,3,2,1,0:T(8,128)(2,1)S(1)} %collective-permute-done.16.refs_9_) | copy-start | bytes 9437188
  600.8 71.6 %copy-start.42 = (bf16[4,8,3,128,128]{4,3,2,1,0:T(8,128)(2,1)S(1)}, bf16[4,8,3,128,128]{4,3,2,1,0:T(8,128)(2,1)}, u32[]{:S(2)}) copy-start(bf16[4,8,3,128,128]{4,3,2,1,0:T(8,128)(2,1)} %get-tuple-element.118) | copy-start | bytes 9437188
  677.8 457.3 %reduce-scatter.5.cloned.1.call-start = ((), (), s32[]{:S(2)}) async-start(), calls=%async_computation.9 | async-start | bytes 3932160 | tf_op jit(solution)/shard_map/reduce_scatter | solution.py:683
  790.0 10.0 collective-permute-start.20
  799.4 18.0 %collective-permute-start.18 = (bf16[2,512,1024]{1,2,0:T(8,128)(2,1)}, bf16[2,512,1024]{1,2,0:T(8,128)(2,1)}, u32[]{:S(2)}, u32[]{:S(2)}) collective-permute-start(bf16[2,512,1024]{1,2,0:T(8,128)(2,1)} %copy.306), channel_id=1, source_target_pairs={{0,1},{1,0},{2,3},{3,2},{4,5},{5,4},{6,7},{7,6},{8,9},{9,8},{10,11... | collective-permute-start | bytes 6291464 | tf_op jit(solution)/shard_map/ppermute | solution.py:325
  807.0 26.2 %collective-permute-start.21 = (bf16[512,1024]{0,1:T(8,128)(2,1)}, bf16[512,1024]{0,1:T(8,128)(2,1)S(1)}, u32[]{:S(2)}, u32[]{:S(2)}) collective-permute-start(bf16[512,1024]{0,1:T(8,128)(2,1)} %fusion.41), channel_id=1, source_target_pairs={{0,2},{1,3},{2,0},{3,1},{4,6},{5,7},{6,4},{7,5},{8,10},{9,11},{10,... | collective-permute-start | bytes 3145736 | tf_op jit(solution)/shard_map/ppermute | solution.py:330
  807.6 84.2 %collective-permute-start.22 = (bf16[4,8,3,128,128]{4,3,2,1,0:T(8,128)(2,1)}, bf16[4,8,3,128,128]{4,3,2,1,0:T(8,128)(2,1)}, u32[]{:S(2)}, u32[]{:S(2)}) collective-permute-start(bf16[4,8,3,128,128]{4,3,2,1,0:T(8,128)(2,1)} %get-tuple-element.112), channel_id=1, source_target_pairs={{0,4},{4,0},{1,5},{5,1},{2,6},{6,2},{3,7},{7,3},{8,12},{12,8},{9,1... | collective-permute-start | bytes 9437192 | tf_op jit(solution)/shard_map/ppermute | solution.py:600
  824.9 30.0 %collective-permute-start.19 = (bf16[512,1024]{0,1:T(8,128)(2,1)}, bf16[512,1024]{0,1:T(8,128)(2,1)}, u32[]{:S(2)}, u32[]{:S(2)}) collective-permute-start(bf16[512,1024]{0,1:T(8,128)(2,1)} %fusion.45), channel_id=1, source_target_pairs={{0,2},{1,3},{2,0},{3,1},{4,6},{5,7},{6,4},{7,5},{8,10},{9,11},{10,... | collective-permute-start | bytes 3145736 | tf_op jit(solution)/shard_map/ppermute | solution.py:330
  829.2 25.7 %copy-start.11 = (f32[512,1024]{0,1:T(8,128)S(1)}, f32[512,1024]{0,1:T(8,128)}, u32[]{:S(2)}) copy-start(f32[512,1024]{0,1:T(8,128)} %copy-done.10) | copy-start | bytes 6291460
  829.2 25.6 %copy-start.15 = (f32[2,512,1024]{1,2,0:T(8,128)S(1)}, f32[2,512,1024]{1,2,0:T(8,128)}, u32[]{:S(2)}) copy-start(f32[2,512,1024]{1,2,0:T(8,128)} %copy-done.14) | copy-start | bytes 12582916
  862.0 28.1 %all-to-all-start.2 = ((bf16[1,512,8,128]{3,1,0,2:T(8,128)(2,1)}), bf16[1,512,8,128]{3,1,0,2:T(8,128)(2,1)S(1)}, u32[]{:S(2)}, u32[]{:S(2)}) async-start(bf16[1,512,8,128]{3,1,0,2:T(8,128)(2,1)} %copy.261), calls=%async_computation.2 | async-start | bytes 2097152 | tf_op jit(solution)/shard_map/all_to_all | solution.py:624
  865.6 269.6 %reduce-scatter.9.cloned.1.call-start = ((), (), s32[]{:S(2)}) async-start(), calls=%async_computation.11 | async-start | bytes 3932160 | tf_op jit(solution)/shard_map/reduce_scatter | solution.py:683
  865.7 112.8 %collective-permute-start.23 = (bf16[4,8,3,128,128]{4,3,2,1,0:T(8,128)(2,1)}, bf16[4,8,3,128,128]{4,3,2,1,0:T(8,128)(2,1)}, u32[]{:S(2)}, u32[]{:S(2)}) collective-permute-start(bf16[4,8,3,128,128]{4,3,2,1,0:T(8,128)(2,1)} %get-tuple-element.114), channel_id=1, source_target_pairs={{0,4},{4,0},{1,5},{5,1},{2,6},{6,2},{3,7},{7,3},{8,12},{12,8},{9,1... | collective-permute-start | bytes 9437192 | tf_op jit(solution)/shard_map/ppermute | solution.py:600
  978.5 28.0 %all-to-all-start.3 = ((bf16[1,1024,4,256]{3,2,0,1:T(4,128)(2,1)}), bf16[1,1024,4,256]{3,2,0,1:T(4,128)(2,1)}, u32[]{:S(2)}, u32[]{:S(2)}) async-start(bf16[1,1024,4,256]{3,2,0,1:T(4,128)(2,1)} %bitcast.431), calls=%async_computation.3 | async-start | bytes 4194304 | tf_op jit(solution)/shard_map/all_to_all | solution.py:685
  983.5 151.7 %reduce-scatter.11.cloned.1.call-start = ((), (), s32[]{:S(2)}) async-start(), calls=%async_computation.12 | async-start | bytes 3932160 | tf_op jit(solution)/shard_map/reduce_scatter | solution.py:683
  1041.4 16.9 %collective-permute-start.24 = (bf16[2,2,4,72,1024]{4,3,0,1,2:T(8,128)(2,1)}, bf16[2,2,4,72,1024]{4,3,0,1,2:T(8,128)(2,1)}, u32[]{:S(2)}, u32[]{:S(2)}) collective-permute-start(bf16[2,2,4,72,1024]{4,3,0,1,2:T(8,128)(2,1)} %fusion.30), channel_id=1, source_target_pairs={{0,1},{1,0},{2,3},{3,2},{4,5},{5,4},{6,7},{7,6},{8,9},{9,8},{10,11... | collective-permute-start | bytes 7077896 | tf_op jit(solution)/shard_map/ppermute | solution.py:376
  1050.9 3.2 collective-permute-start.30
  1056.7 17.7 %collective-permute-start.31 = (bf16[2,4,40,1024]{3,2,0,1:T(8,128)(2,1)S(1)}, bf16[2,4,40,1024]{3,2,0,1:T(8,128)(2,1)}, u32[]{:S(2)}, u32[]{:S(2)}) collective-permute-start(bf16[2,4,40,1024]{3,2,0,1:T(8,128)(2,1)S(1)} %fusion.85), channel_id=1, source_target_pairs={{0,2},{1,3},{2,0},{3,1},{4,6},{5,7},{6,4},{7,5},{8,10},{9,11},{10,... | collective-permute-start | bytes 1966088 | tf_op jit(solution)/shard_map/ppermute | solution.py:376
  1065.5 33.5 %collective-permute-start.25 = (bf16[2,4,72,1024]{3,2,0,1:T(8,128)(2,1)}, bf16[2,4,72,1024]{3,2,0,1:T(8,128)(2,1)}, u32[]{:S(2)}, u32[]{:S(2)}) collective-permute-start(bf16[2,4,72,1024]{3,2,0,1:T(8,128)(2,1)} %fusion.72), channel_id=1, source_target_pairs={{0,2},{1,3},{2,0},{3,1},{4,6},{5,7},{6,4},{7,5},{8,10},{9,11},{10,... | collective-permute-start | bytes 3538952 | tf_op jit(solution)/shard_map/ppermute | solution.py:376
  1076.9 8.4 collective-permute-start.32
  1087.1 18.7 %collective-permute-start.33 = (bf16[40,1024]{1,0:T(8,128)(2,1)}, bf16[40,1024]{1,0:T(8,128)(2,1)}, u32[]{:S(2)}, u32[]{:S(2)}) collective-permute-start(bf16[40,1024]{1,0:T(8,128)(2,1)} %get-tuple-element.196), channel_id=1, source_target_pairs={{0,8},{8,16},{16,24},{24,0},{1,9},{9,17},{17,25},{25,1},{2,10},{10... | collective-permute-start | bytes 245768 | tf_op jit(solution)/shard_map/ppermute | solution.py:368
  1089.2 16.6 %collective-permute-start.35 = (bf16[40,1024]{1,0:T(8,128)(2,1)}, bf16[40,1024]{1,0:T(8,128)(2,1)}, u32[]{:S(2)}, u32[]{:S(2)}) collective-permute-start(bf16[40,1024]{1,0:T(8,128)(2,1)} %get-tuple-element.197), channel_id=1, source_target_pairs={{0,24},{8,0},{16,8},{24,16},{1,25},{9,1},{17,9},{25,17},{2,26},{10... | collective-permute-start | bytes 245768 | tf_op jit(solution)/shard_map/ppermute | solution.py:368
  1090.9 12.5 %copy-start.8 = (f32[512,1024]{0,1:T(8,128)S(1)}, f32[512,1024]{0,1:T(8,128)}, u32[]{:S(2)}) copy-start(f32[512,1024]{0,1:T(8,128)} %copy-done.7) | copy-start | bytes 6291460
  1090.9 12.5 %copy-start.23 = (bf16[1,512,1024]{1,2,0:T(8,128)(2,1)S(1)}, bf16[1,512,1024]{1,2,0:T(8,128)(2,1)}, u32[]{:S(2)}) copy-start(bf16[1,512,1024]{1,2,0:T(8,128)(2,1)} %copy-done.21) | copy-start | bytes 3145732
  1090.9 12.5 %copy-start.47 = (f32[512,1024]{0,1:T(8,128)S(1)}, f32[512,1024]{0,1:T(8,128)}, u32[]{:S(2)}) copy-start(f32[512,1024]{0,1:T(8,128)} %get-tuple-element.213) | copy-start | bytes 6291460
  1091.0 14.8 %collective-permute-start.34 = (bf16[40,1024]{1,0:T(8,128)(2,1)S(1)}, bf16[40,1024]{1,0:T(8,128)(2,1)}, u32[]{:S(2)}, u32[]{:S(2)}) collective-permute-start(bf16[40,1024]{1,0:T(8,128)(2,1)S(1)} %get-tuple-element.198), channel_id=1, source_target_pairs={{0,16},{8,24},{16,0},{24,8},{1,17},{9,25},{17,1},{25,9},{2,18},{10... | collective-permute-start | bytes 245768 | tf_op jit(solution)/shard_map/ppermute | solution.py:368
  1101.5 14.9 %collective-permute-start.26 = (bf16[4,72,1024]{2,1,0:T(8,128)(2,1)S(1)}, bf16[4,72,1024]{2,1,0:T(8,128)(2,1)}, u32[]{:S(2)}, u32[]{:S(2)}) collective-permute-start(bf16[4,72,1024]{2,1,0:T(8,128)(2,1)S(1)} %fusion.86), channel_id=1, source_target_pairs={{0,4},{4,0},{1,5},{5,1},{2,6},{6,2},{3,7},{7,3},{8,12},{12,8},{9,1... | collective-permute-start | bytes 1769480 | tf_op jit(solution)/shard_map/ppermute | solution.py:368
  1118.1 8.7 collective-permute-start.27
  1120.2 7.2 collective-permute-start.29
  1121.9 11.8 %collective-permute-start.28 = (bf16[72,1024]{1,0:T(8,128)(2,1)S(1)}, bf16[72,1024]{1,0:T(8,128)(2,1)S(1)}, u32[]{:S(2)}, u32[]{:S(2)}) collective-permute-start(bf16[72,1024]{1,0:T(8,128)(2,1)S(1)} %get-tuple-element.195), channel_id=1, source_target_pairs={{0,16},{8,24},{16,0},{24,8},{1,17},{9,25},{17,1},{25,9},{2,18},{10... | collective-permute-start | bytes 442376 | tf_op jit(solution)/shard_map/ppermute | solution.py:368
  (63 other events, 268.0 us)
Sparse Core Ops, SparseCore 0:
  11.5 68.5 all-gather.9
  82.2 62.3 all-gather.15
  146.2 62.1 all-gather.13
  209.8 62.1 all-gather.17
  273.4 62.1 all-gather.11
  678.0 58.3 reduce-scatter.6
  829.3 59.5 reduce-scatter.4
  936.5 59.1 reduce-scatter.8
  1006.6 60.1 reduce-scatter.10

commit v2 on v1

--- a/solution.py
+++ b/solution.py
@@ -4,6 +4,7 @@
 import jax.numpy as jnp
 from jax import lax
 from jax.experimental import pallas as pl
+from jax.experimental.layout import Layout, with_layout_constraint
 from jax.experimental.pallas import tpu as pltpu
 from jax.sharding import PartitionSpec as P
 
@@ -65,6 +66,10 @@
 def rms_back(grad_normed, normed, inverse, gain_row):
     scaled_grad = grad_normed * gain_row
     return inverse * (scaled_grad - normed * jnp.mean(scaled_grad * normed, axis=1, keepdims=True))
+
+
+def by_rows(array):
+    return with_layout_constraint(array, Layout(tuple(range(array.ndim))))
 
 
 def dot_nn(left_side, right_side):
@@ -322,12 +327,14 @@
 def scatter_group(terms):
     count = lax.axis_size("tp")
     parts = terms.reshape(count, -1, terms.shape[-1])
-    sent = lax.ppermute(
-        parts[1::2].astype(jnp.bfloat16), "tp", swap_pairs(count, 1)
-    ).astype(jnp.float32)
-    kept = parts[0] + sent[0]
-    passed = (parts[2] + sent[1]).astype(jnp.bfloat16)
-    return kept + lax.ppermute(passed, "tp", swap_pairs(count, 2)).astype(jnp.float32)
+    first, second = (
+        lax.ppermute(parts[which].astype(jnp.bfloat16), "tp", swap_pairs(count, 1)).astype(
+            jnp.float32
+        )
+        for which in (3, 1)
+    )
+    passed = lax.ppermute((parts[2] + first).astype(jnp.bfloat16), "tp", swap_pairs(count, 2))
+    return parts[0] + second + passed.astype(jnp.float32)
 
 
 def shifted(count, step):
@@ -369,10 +376,10 @@
     return total
 
 
-def scatter_bit(parts, bit):
+def scatter_bit(parts, bit, axis):
     mine = (lax.axis_index("tp") & bit) // bit
-    sent = lax.dynamic_index_in_dim(parts, 1 - mine, 0, keepdims=False).astype(jnp.bfloat16)
-    kept = lax.dynamic_index_in_dim(parts, mine, 0, keepdims=False).astype(jnp.float32)
+    sent = lax.dynamic_index_in_dim(parts, 1 - mine, axis, keepdims=False).astype(jnp.bfloat16)
+    kept = lax.dynamic_index_in_dim(parts, mine, axis, keepdims=False).astype(jnp.float32)
     return kept + lax.ppermute(sent, "tp", swap_pairs(lax.axis_size("tp"), bit)).astype(
         jnp.float32
     )
@@ -381,8 +388,8 @@
 def scatter_dense(parts):
     fsdp_count, context_count = lax.axis_size("fsdp"), lax.axis_size("ctx")
     parts = parts.reshape((fsdp_count, context_count, 2, 2) + parts.shape[1:])
-    parts = parts.transpose(3, 2, 1, 0, 4, 5)
-    return scatter_axis(scatter_axis(scatter_bit(scatter_bit(parts, 1), 2), "ctx"), "fsdp")
+    parts = scatter_bit(scatter_bit(parts, 1, 3), 2, 2)
+    return scatter_axis(scatter_axis(jnp.moveaxis(parts, 1, 0), "ctx"), "fsdp")
 
 
 def hold(*refs):
@@ -430,10 +437,12 @@
     head_size = HEAD
     score_scale = HEAD ** (-0.5)
     capacity = local_positions * 3 // 8
+    group_grads = by_rows(gather_group(cotangent.reshape(row_count, model_width)))
+    grads_turned = by_rows(group_grads.T)
     device_count = context_count * lax.axis_size("fsdp") * lax.axis_size("tp")
-    inward_count, output_count = query_key_value.size, attn_output.size
     gain_count, router_count = norm_gains.size, router_weight.size
     packed = lax.all_gather(pack_rows([query_key_value, norm_gains], model_width), ALL_AXES, axis=0)
+    packed = after(packed, grads_turned)
     packed_later = gather_dense(pack_rows([attn_output, router_weight], model_width))
     inward_rows, output_rows = query_key_value.shape[0], attn_output.shape[0]
     inward_full = packed[:, :inward_rows].reshape(-1, model_width)
@@ -468,6 +477,9 @@
         shard = expert_shards[chunk * chunk_experts : (chunk + 1) * chunk_experts]
         if paired:
             expert_pieces.append([lax.all_gather(shard, "fsdp", axis=0)])
+            if chunk == CHUNKS - 1:
+                other = lax.ppermute(shard, "ctx", swap_pairs(2, 1))
+                expert_pieces[chunk].append(lax.all_gather(other, "fsdp", axis=0))
         else:
             expert_pieces.append([lax.all_gather(shard, ("fsdp", "ctx"), axis=0)])
     gain_rows = gain_full.astype(jnp.float32)
@@ -538,8 +550,7 @@
     inverse_second = lax.rsqrt(jnp.mean(hidden * hidden, axis=1, keepdims=True) + EPS)
     normed_second = hidden * inverse_second
     second_low = (normed_second * gain_rows[1]).astype(jnp.bfloat16)
-    group_rows = gather_group(second_low)
-    group_grads = gather_group(cotangent.reshape(row_count, model_width))
+    group_rows = by_rows(gather_group(by_rows(second_low)))
     group_count = group_rows.shape[0]
     chances = jax.nn.softmax(times_transposed(group_rows, router_full), axis=-1)
     group_order = jnp.bitwise_xor(
@@ -555,12 +566,12 @@
         axis=1,
     )
     gates = jnp.pad(chances * chosen_any, ((0, 0), (0, LANES - EXPERTS)))
-    group_turned = group_rows.T
-    grads_turned = group_grads.T
+    group_turned = by_rows(group_rows.T)
     totals = None
     choice_total = None
     chunk_sums = []
     own_sums = []
+    far_sums = []
     arrivals = []
     marks = []
 
@@ -575,7 +586,7 @@
         fetch(0)
     for chunk in range(CHUNKS):
         if paired:
-            if chunk + 1 < CHUNKS:
+            if chunk + 2 < CHUNKS:
                 fetch(chunk + 1)
         moe_total, back_total, choice, *grad_pieces = expert_pass(
             places,
@@ -588,42 +599,47 @@
             gates,
             totals,
             chunk * chunk_experts,
-            arrivals[chunk - 2 : chunk - 1] if chunk > 1 else (),
         )
         totals = (moe_total, back_total)
         marks.append(choice)
         choice_total = choice if choice_total is None else choice_total + choice
         if paired:
-            if chunk > 1:
-                arrivals[chunk - 2] = grad_pieces[2]
             own_sums.append(grad_pieces[0])
-            arrivals.append(lax.ppermute(grad_pieces[1], "ctx", swap_pairs(2, 1)))
+            far_sums.append(grad_pieces[1])
         else:
             chunk_sums.append(
                 lax.psum_scatter(grad_pieces[0], ("fsdp", "ctx"), scatter_dimension=0)
             )
+    if paired:
+        for chunk in range(CHUNKS - 1):
+            held = after(far_sums[chunk], marks[min(chunk + 1, CHUNKS - 1)])
+            arrivals.append(lax.ppermute(held, "ctx", swap_pairs(2, 1)))
+        last_sums = [
+            lax.psum_scatter(part, "fsdp", scatter_dimension=0)
+            for part in (far_sums[-1], own_sums[-1])
+        ]
     grad_chances = choice_total[:, :EXPERTS] * chosen_any
     grad_logits = chances * (grad_chances - jnp.sum(grad_chances * chances, axis=-1, keepdims=True))
     router_rows = router_full.astype(jnp.float32)
     grad_router = jnp.dot(grad_logits.T, group_rows.astype(jnp.float32), precision=HIGH)
-    back_group = totals[1] + jnp.dot(grad_logits, router_rows, precision=HIGH)
-    grad_second = scatter_group(back_group)
-    moe_rows = scatter_group(totals[0])
+    back_group = by_rows(totals[1] + jnp.dot(grad_logits, router_rows, precision=HIGH))
+    grad_second = by_rows(scatter_group(back_group))
+    moe_rows = by_rows(scatter_group(totals[0]))
     output = (hidden + moe_rows).astype(jnp.bfloat16).reshape(tokens.shape)
     grad_gain_second = jnp.sum(grad_second * normed_second, axis=0)
     grad_hidden = cotangent.astype(jnp.float32).reshape(row_count, model_width) + rms_back(
         grad_second, normed_second, inverse_second, gain_rows[1]
     )
-    grad_attn = grad_hidden.astype(jnp.bfloat16)
+    grad_attn = by_rows(grad_hidden.astype(jnp.bfloat16))
+    if paired:
+        grad_attn, arrivals[0] = together(grad_attn, arrivals[0])
     grad_output_weight = transposed_times(grad_attn, merged)
     grad_merged = (
         jnp.dot(grad_attn, output_full, preferred_element_type=jnp.float32)
         .astype(jnp.bfloat16)
         .reshape(local_seqs, local_positions, KV_HEADS, 2 * head_size)
     )
-    grad_heads = lax.all_to_all(grad_merged, "ctx", split_axis=2, concat_axis=1, tiled=True)
-    if paired:
-        grad_heads, arrivals[-2] = together(grad_heads, arrivals[-2])
+    grad_heads = lax.all_to_all(by_rows(grad_merged), "ctx", split_axis=2, concat_axis=1, tiled=True)
     grad_keys = jnp.zeros((local_seqs, length, local_groups, head_size), jnp.float32)
     grad_values = jnp.zeros((local_seqs, length, local_groups, head_size), jnp.float32)
     grad_query_blocks = []
@@ -677,10 +693,12 @@
         jnp.bfloat16
     )
     if paired:
-        grad_head_rows, arrivals[-1] = together(grad_head_rows, arrivals[-1])
+        grad_head_rows, arrivals[1] = together(grad_head_rows, arrivals[1])
         for own, arrived in zip(own_sums, arrivals):
             joined = (own.astype(jnp.float32) + arrived.astype(jnp.float32)).astype(jnp.bfloat16)
             chunk_sums.append(lax.psum_scatter(joined, "fsdp", scatter_dimension=0))
+        far = lax.ppermute(last_sums[0], "ctx", swap_pairs(2, 1))
+        chunk_sums.append(last_sums[1].astype(jnp.float32) + far.astype(jnp.float32))
     grad_turned = (
         lax.all_to_all(grad_head_rows, "ctx", split_axis=1, concat_axis=2, tiled=True)
         .astype(jnp.float32)
@@ -701,6 +719,7 @@
     grad_first = jnp.dot(grad_projected, inward_full, preferred_element_type=jnp.float32)
     grad_gain_first = jnp.sum(grad_first * normed_first, axis=0)
     grad_inputs = grad_hidden + rms_back(grad_first, normed_first, inverse_first, gain_rows[0])
+    grad_gains = jnp.stack([grad_gain_first, grad_gain_second])
 
     def by_device(array, axis):
         parts = array.reshape(
@@ -708,35 +727,25 @@
         )
         return jnp.moveaxis(parts, axis, 0).reshape(device_count, -1)
 
-    def sum_dense(terms):
-        flat = jnp.concatenate(terms, axis=1)
-        rows = -(-flat.shape[1] // (8 * model_width)) * 8
-        flat = jnp.pad(flat, ((0, 0), (0, rows * model_width - flat.shape[1])))
-        return scatter_dense(flat.reshape(device_count, rows, model_width)).reshape(-1)
-
-    half_gains = gain_count // 2
-    early = sum_dense(
-        [
-            by_device(grad_output_weight, 0),
-            by_device(grad_router, 1),
-            by_device(grad_gain_second, 0),
-        ]
-    )
-    late = sum_dense([by_device(grad_inward, 0), by_device(grad_gain_first, 0)])
-    grad_gains = jnp.stack(
-        [
-            late[inward_count : inward_count + half_gains],
-            early[output_count + router_count : output_count + router_count + half_gains],
-        ]
-    )
-    expert_sums = jnp.concatenate(chunk_sums, axis=0).astype(jnp.float32)
+    inward_sum = scatter_dense(
+        grad_inward.astype(jnp.bfloat16).reshape((device_count,) + query_key_value.shape)
+    )
+    output_sum = scatter_dense(
+        grad_output_weight.astype(jnp.bfloat16).reshape((device_count,) + attn_output.shape)
+    )
+    small = jnp.concatenate([by_device(grad_router, 1), by_device(grad_gains, 1)], axis=1)
+    small_count = small.shape[1]
+    small_rows = -(-small_count // (16 * LANES)) * 16
+    small = jnp.pad(small, ((0, 0), (0, small_rows * LANES - small_count)))
+    small_sum = scatter_dense(small.reshape(device_count, small_rows, LANES)).reshape(-1)
+    expert_sums = jnp.concatenate([part.astype(jnp.float32) for part in chunk_sums], axis=0)
     return (
         output,
         grad_inputs.reshape(tokens.shape),
-        grad_gains,
-        late[:inward_count].reshape(query_key_value.shape),
-        early[:output_count].reshape(attn_output.shape),
-        early[output_count : output_count + router_count].reshape(router_weight.shape),
+        small_sum[router_count:small_count].reshape(norm_gains.shape),
+        inward_sum,
+        output_sum,
+        small_sum[:router_count].reshape(router_weight.shape),
         expert_sums[:, :2],
         expert_sums[:, 2],
     )

time: 1160 us -> 1010 us (0.87)
  local copies, waits for them, and re-layouts: 224 us -> 91.5 us
  waiting for transfers between devices: 330 us -> 306 us
    ppermute x4 -> x3, waiting for transfers between devices: 141 us -> 0.01 us  [fetch(): expert_pieces[chunk].append(lax.ppermute(near, 'ctx', swap_pairs(2, 1)))]
    ppermute x8 -> x11, waiting for transfers between devices: 21.2 us -> 156 us  [the longest x1 60 us: per_device(): other = lax.ppermute(shard, 'ctx', swap_pairs(2, 1))]
    slice x5, local copies, waits for them, and re-layouts: 71.1 us -> 3.49 us  [the longest x2 2.86 us: scatter_group(): parts[which].astype(jnp.bfloat16)]
    all_gather x1, waiting for transfers between devices: 51.5 us -> 17.8 us  [per_device(): lax.all_gather(pack_rows([query_key_value, norm_gains], model_width), ALL...]
    unnamed x181 -> x172, local copies, waits for them, and re-layouts: 50.5 us -> 23 us
    ppermute x2, waiting for transfers between devices: 21.8 us -> 45.2 us  [gather_group(): across = lax.ppermute(rows, 'tp', swap_pairs(count, 2))]
    pallas_call x2 -> x0, local copies, waits for them, and re-layouts: 18.8 us -> none  [expert_pass(): pl.pallas_call(functools.partial(expert_kernel, first, steps, base_expert...]
    all_to_all x1, waiting for transfers between devices: 22.3 us -> 8.12 us  [per_device(): lax.all_to_all(by_rows(grad_merged), 'ctx', split_axis=2, concat_axis=1,...]
  transfers between devices with their start and end apart: 49 -> 59, of which waited for: 21 -> 22; matrix products, arithmetic and copies ran while one was open for 38% -> 32% of each run, Pallas kernels for 18% -> 20%
where the time goes in v2:
time: 1010 us; the launch traced here: 999 us
  waiting for transfers between devices  306 us (30%)
  Pallas kernels  274 us (27%)
  other arithmetic  142 us (14%)
  matrix products  111 us (11%)
  local copies, waits for them, and re-layouts  91.5 us (9%)
  starting transfers between devices  58.6 us (6%)
  between operations  15.9 us (2%)
    pallas_call x4, Pallas kernels, expert_pass(): pl.pallas_call(functools.partial(expert_kernel, first, steps, base_expert...  274 us
    ppermute x1, waiting for transfers between devices, per_device(): other = lax.ppermute(shard, 'ctx', swap_pairs(2, 1))  60 us
    ppermute x3, waiting for transfers between devices, per_device(): arrivals.append(lax.ppermute(held, 'ctx', swap_pairs(2, 1)))  51.4 us
    ppermute x2, waiting for transfers between devices, gather_group(): across = lax.ppermute(rows, 'tp', swap_pairs(count, 2))  45.2 us
    ppermute x2, waiting for transfers between devices, scatter_group(): lax.ppermute((parts[2] + first).astype(jnp.bfloat16), 'tp', swap_pairs(co...  44.4 us
    another operation x7, other arithmetic  35.8 us
    ppermute x12, waiting for transfers between devices, scatter_axis(): lax.ppermute(sent, name, shifted(count, step)).astype(jnp.float32)  34.6 us
    unnamed x172, local copies, waits for them, and re-layouts  23 us
  transfers between devices with their start and end apart: 59, of which 22 were waited for; matrix products, arithmetic and copies ran while one was open for 32% of the time, Pallas kernels for 20%

profile of v2, /device:TPU:0, one launch (start us, length us, event | category | flops | bytes accessed | tf_op | source)
XLA Modules:
  0.0 998.9 jit_solution(3773381225612883531)
XLA Ops:
  9.8 3.6 pad_maximum_fusion.8
  24.2 4.0 collective-permute-done.3
  28.3 23.7 %collective-permute-done.1 = bf16[512,1024]{1,0:T(8,128)(2,1)} collective-permute-done((bf16[512,1024]{1,0:T(8,128)(2,1)S(1)}, bf16[512,1024]{1,0:T(8,128)(2,1)}, u32[]{:S(2)}, u32[]{:S(2)}) %collective-permute-start.1) | collective-permute-done | bytes 1048608 | tf_op jit(solution)/shard_map/ppermute | solution.py:321
  54.8 3.4 pad_maximum_fusion.1.refs_4_
  58.2 6.5 copy.168
  64.8 17.8 %all-gather.12.cloned.1.call-done.refs_0_ = bf16[32,80,1024]{2,1,0:T(8,128)(2,1)} async-done(((bf16[1,80,1024]{2,1,0:T(8,128)(2,1)}), bf16[32,80,1024]{2,1,0:T(8,128)(2,1)}) %all-gather.12.cloned.1.call-update) | async-done | bytes 5242896 | tf_op jit(solution)/shard_map/all_gather | solution.py:444
  83.9 4.9 slice.305
  89.6 5.0 convolution_bitcast_fusion
  96.8 3.8 all-to-all-start
  105.2 16.7 %collective-permute-done.7 = bf16[2,4,48,1024]{3,2,0,1:T(8,128)(2,1)} collective-permute-done((bf16[2,4,48,1024]{3,2,0,1:T(8,128)(2,1)}, bf16[2,4,48,1024]{3,2,0,1:T(8,128)(2,1)}, u32[]{:S(2)}, u32[]{:S(2)}) %collective-permute-start.7) | collective-permute-done | bytes 786464 | tf_op jit(solution)/shard_map/ppermute | solution.py:356
  126.1 3.5 copy.230
  129.6 3.6 all_to_all.47
  133.3 4.9 fusion.118
  138.2 7.4 fusion.117
  145.5 8.2 fusion.3
  153.8 8.7 fusion.53
  170.5 4.4 all-to-all-start.1
  178.5 11.2 %maximum_select_fusion = bf16[2,2,2,4,48,1024]{5,4,0,1,2,3:T(8,128)(2,1)S(1)} fusion(bf16[1,2,2,4,48,1024]{5,4,0,1,2,3:T(8,128)(2,1)S(1)} %maximum_select_fusion.2, bf16[1,2,2,4,48,1024]{5,4,0,1,2,3:T(8,128)(2,1)S(1)} %bitcast.446, pred[]{:T(512)S(6)} %gt.6), kind=kLoop, calls=%fused_computation.49 | loop fusion | flops 4718592 | bytes 6291457 | tf_op jit(solution)/shard_map/jit(_where)/select_n | solution.py:358
  196.0 3.6 multiply_reduce_fusion.2
  205.7 21.5 %collective-permute-done.11 = bf16[512,1024]{1,0:T(8,128)(2,1)} collective-permute-done((bf16[512,1024]{1,0:T(8,128)(2,1)}, bf16[512,1024]{1,0:T(8,128)(2,1)}, u32[]{:S(2)}, u32[]{:S(2)}) %collective-permute-start.11) | collective-permute-done | bytes 1048608 | tf_op jit(solution)/shard_map/ppermute | solution.py:321
  230.2 60.0 %collective-permute-done.9 = bf16[8,3,128,128]{3,2,1,0:T(8,128)(2,1)} collective-permute-done((bf16[8,3,128,128]{3,2,1,0:T(8,128)(2,1)}, bf16[8,3,128,128]{3,2,1,0:T(8,128)(2,1)}, u32[]{:S(2)}, u32[]{:S(2)}) %collective-permute-start.9) | collective-permute-done | bytes 786464 | tf_op jit(solution)/shard_map/ppermute | solution.py:481
  293.3 3.7 pad_maximum_fusion.2.refs_2_
  297.1 6.5 copy.178
  303.6 3.7 fusion.119
  310.0 60.6 %shard_map.163 = (f32[2048,1024]{1,0:T(8,128)}, f32[2048,1024]{1,0:T(8,128)}, f32[2048,128]{1,0:T(8,128)}, bf16[4,8,3,128,128]{4,3,2,1,0:T(8,128)(2,1)}, bf16[4,8,3,128,128]{4,3,2,1,0:T(8,128)(2,1)}) custom-call(s32[2]{0:T(128)} %add_multiply_fusion.places_ref, bf16[4,8,3,128,128]{4,3,2,1,0:T(8,128)(2,1)} %bitcast.509, ...), custom_call_target="tpu_custom_call" | custom-call | flops 38654705664 | bytes 41943040 | tf_op jit(solution)/shard_map/pallas_call | solution.py:272
  371.1 71.3 %shard_map.165 = (f32[2048,1024]{1,0:T(8,128)}, f32[2048,1024]{1,0:T(8,128)}, f32[2048,128]{1,0:T(8,128)}, bf16[4,8,3,128,128]{4,3,2,1,0:T(8,128)(2,1)}, bf16[4,8,3,128,128]{4,3,2,1,0:T(8,128)(2,1)}) custom-call(s32[2]{0:T(128)} %add_multiply_fusion.places_ref, bf16[4,8,3,128,128]{4,3,2,1,0:T(8,128)(2,1)} %bitcast.507, ...), custom_call_target="tpu_custom_call", output_to_operand_aliasing={{0}: (8, {}), {1}: (9, {})} | custom-call | flops 38654705664 | bytes 41943040 | tf_op jit(solution)/shard_map/pallas_call | solution.py:272
  444.1 71.4 %shard_map.166 = (f32[2048,1024]{1,0:T(8,128)}, f32[2048,1024]{1,0:T(8,128)}, f32[2048,128]{1,0:T(8,128)}, bf16[4,8,3,128,128]{4,3,2,1,0:T(8,128)(2,1)}, bf16[4,8,3,128,128]{4,3,2,1,0:T(8,128)(2,1)}) custom-call(s32[2]{0:T(128)} %add_multiply_fusion.places_ref, ...), custom_call_target="tpu_custom_call", output_to_operand_aliasing={{0}: (8, {}), {1}: (9, {})} | custom-call | flops 38654705664 | bytes 41943040 | tf_op jit(solution)/shard_map/pallas_call | solution.py:272
  515.5 71.1 %shard_map.167 = (f32[2048,1024]{1,0:T(8,128)}, f32[2048,1024]{1,0:T(8,128)}, f32[2048,128]{1,0:T(8,128)}, bf16[4,8,3,128,128]{4,3,2,1,0:T(8,128)(2,1)}, bf16[4,8,3,128,128]{4,3,2,1,0:T(8,128)(2,1)}) custom-call(s32[2]{0:T(128)} %add_multiply_fusion.places_ref, bf16[4,8,3,128,128]{4,3,2,1,0:T(8,128)(2,1)} %bitcast.510, ...), custom_call_target="tpu_custom_call", output_to_operand_aliasing={{0}: (8, {}), {1}: (9, {})} | custom-call | flops 38654705664 | bytes 41943040 | tf_op jit(solution)/shard_map/pallas_call | solution.py:272
  591.4 5.9 fusion.90
  597.3 13.7 %fusion.112 = (bf16[2048,1024]{1,0:T(8,128)(2,1)}, f32[2048,1024]{1,0:T(8,128)}) fusion(f32[2048,1024]{1,0:T(8,128)} %get-tuple-element.104, f32[2048,1024]{1,0:T(8,128)} %fusion.90), kind=kLoop, calls=%fused_computation.249 | loop fusion | flops 4194304 | bytes 29360128 | tf_op jit(solution)/shard_map/convert.28
  615.4 4.2 convert.75
  626.1 23.5 %collective-permute-done.21 = bf16[512,1024]{1,0:T(8,128)(2,1)S(1)} collective-permute-done((bf16[512,1024]{1,0:T(8,128)(2,1)S(1)}, bf16[512,1024]{1,0:T(8,128)(2,1)S(1)}, u32[]{:S(2)}, u32[]{:S(2)}) %collective-permute-start.21) | collective-permute-done | bytes 1048608 | tf_op jit(solution)/shard_map/ppermute | solution.py:336
  650.5 20.9 %collective-permute-done.18 = bf16[512,1024]{1,0:T(8,128)(2,1)S(1)} collective-permute-done((bf16[512,1024]{1,0:T(8,128)(2,1)S(1)}, bf16[512,1024]{1,0:T(8,128)(2,1)S(1)}, u32[]{:S(2)}, u32[]{:S(2)}) %collective-permute-start.18) | collective-permute-done | bytes 1048608 | tf_op jit(solution)/shard_map/ppermute | solution.py:336
  674.2 10.4 %collective-permute-done.22.refs_1_ = bf16[4,8,3,128,128]{4,3,2,1,0:T(8,128)(2,1)} collective-permute-done((bf16[4,8,3,128,128]{4,3,2,1,0:T(8,128)(2,1)}, bf16[4,8,3,128,128]{4,3,2,1,0:T(8,128)(2,1)}, u32[]{:S(2)}, u32[]{:S(2)}) %collective-permute-start.22) | collective-permute-done | bytes 3145760 | tf_op jit(solution)/shard_map/ppermute | solution.py:616
  684.6 6.5 add_convert_fusion.2
  696.6 3.6 all-to-all-start.2
  707.1 8.1 all-to-all-done.2
  715.6 5.4 fusion.58
  722.6 9.7 fusion.44
  735.0 5.3 fusion.9
  740.3 4.7 fusion.20
  749.7 33.0 %collective-permute-done.42 = bf16[4,8,3,128,128]{4,3,2,1,0:T(8,128)(2,1)} collective-permute-done((bf16[4,8,3,128,128]{4,3,2,1,0:T(8,128)(2,1)}, bf16[4,8,3,128,128]{4,3,2,1,0:T(8,128)(2,1)}, u32[]{:S(2)}, u32[]{:S(2)}) %collective-permute-start.42) | collective-permute-done | bytes 3145760 | tf_op jit(solution)/shard_map/ppermute | solution.py:616
  782.7 6.5 add_convert_fusion
  789.2 4.1 fusion.57
  793.3 15.2 %fusion = (f32[4,2,512]{2,1,0:T(2,128)S(1)}, f32[4,1024,512,2]{2,1,3,0:T(8,128)}) fusion(f32[1,4,2,512,1024]{3,4,2,1,0:T(8,128)} %get-tuple-element.165, f32[4,2,512]{2,1,0:T(2,128)S(1)} %bitcast.495, bf16[512,4,2,64]{0,3,2,1:T(8,128)(2,1)} %bitcast.448, bf16[1,1024,4,256]{1,3,2,0:T(8,128)(2,1)} %copy-done.10), kind=kOutput, calls=%fused_computation.4 | convolution fusion | flops 549449728 | bytes 34635776 | tf_op jit(solution)/shard_map/sqgjd,skgd->sgjqk/dot_general | solution.py:671
  808.5 8.3 fusion.8
  824.1 7.0 fusion.47
  834.0 3.7 fusion.41
  837.6 3.2 pad_maximum_fusion.4.refs_0_
  840.8 8.1 collective-permute-done.23.refs_1_
  848.9 4.8 all-to-all-start.3
  857.7 6.4 add_convert_fusion.1
  864.1 5.8 collective-permute-done.37
  874.3 5.8 all-to-all-done.3
  880.1 4.3 copy.199
  901.6 6.7 fusion.35
  913.7 3.2 convert_add_fusion
  920.6 7.2 collective-permute-done.40
  928.6 3.7 collective-permute-done.26
  932.4 4.0 collective-permute-start.29
  936.4 7.3 collective-permute-done.31
  950.1 16.2 %collective-permute-done.32 = bf16[4,64,1024]{2,1,0:T(8,128)(2,1)} collective-permute-done((bf16[4,64,1024]{2,1,0:T(8,128)(2,1)}, bf16[4,64,1024]{2,1,0:T(8,128)(2,1)}, u32[]{:S(2)}, u32[]{:S(2)}) %collective-permute-start.32) | collective-permute-done | bytes 524320 | tf_op jit(solution)/shard_map/ppermute | solution.py:375
  968.3 3.3 collective-permute-start.35
  975.8 5.5 collective-permute-done.34
  (423 shorter events, 173.3 us)
Async XLA Ops:
  7.2 220.1 %copy-start = (s32[4,512,8]{1,2,0:T(8,128)S(1)}, s32[4,512,8]{1,2,0:T(8,128)}, u32[]{:S(2)}) copy-start(s32[4,512,8]{1,2,0:T(8,128)} %param.22) | copy-start | bytes 196612
  7.2 75.4 %all-gather.12.cloned.1.call-start = ((), (), s32[]{:S(2)}) async-start(), calls=%async_computation.9 | async-start | bytes 5406720 | tf_op jit(solution)/shard_map/all_gather | solution.py:444
  9.7 193.9 %all-gather.20.cloned.1.call-start = ((), (), s32[]{:S(2)}) async-start(), calls=%async_computation.18 | async-start | bytes 3932160 | tf_op jit(solution)/shard_map/all_gather | solution.py:479
  13.4 278.2 %all-gather.22.cloned.1.call-start = ((), (), s32[]{:S(2)}) async-start(), calls=%async_computation.19 | async-start | bytes 3932160 | tf_op jit(solution)/shard_map/all_gather | solution.py:479
  14.2 356.5 %all-gather.18.cloned.1.call-start = ((), (), s32[]{:S(2)}) async-start(), calls=%async_computation.17 | async-start | bytes 3932160 | tf_op jit(solution)/shard_map/all_gather | solution.py:479
  14.9 37.0 %collective-permute-start.5 = (bf16[48,1024]{1,0:T(8,128)(2,1)S(1)}, bf16[48,1024]{1,0:T(8,128)(2,1)S(1)}, u32[]{:S(2)}, u32[]{:S(2)}) collective-permute-start(bf16[48,1024]{1,0:T(8,128)(2,1)S(1)} %reshape.866), channel_id=1, source_target_pairs={{0,8},{8,16},{16,24},{24,0},{1,9},{9,17},{17,25},{25,1},{2,10},{10... | collective-permute-start | bytes 294920 | tf_op jit(solution)/shard_map/ppermute | solution.py:348
  18.0 33.9 %collective-permute-start.4 = (bf16[48,1024]{1,0:T(8,128)(2,1)S(1)}, bf16[48,1024]{1,0:T(8,128)(2,1)S(1)}, u32[]{:S(2)}, u32[]{:S(2)}) collective-permute-start(bf16[48,1024]{1,0:T(8,128)(2,1)S(1)} %reshape.866), channel_id=1, source_target_pairs={{0,16},{8,24},{16,0},{24,8},{1,17},{9,25},{17,1},{25,9},{2,18},{10... | collective-permute-start | bytes 294920 | tf_op jit(solution)/shard_map/ppermute | solution.py:348
  20.6 7.6 collective-permute-start.3
  22.0 30.0 %collective-permute-start.1 = (bf16[512,1024]{1,0:T(8,128)(2,1)S(1)}, bf16[512,1024]{1,0:T(8,128)(2,1)}, u32[]{:S(2)}, u32[]{:S(2)}) collective-permute-start(bf16[512,1024]{1,0:T(8,128)(2,1)S(1)} %bitcast.464), channel_id=1, source_target_pairs={{0,2},{1,3},{2,0},{3,1},{4,6},{5,7},{6,4},{7,5},{8,10},{9,11},{10,... | collective-permute-start | bytes 3145736 | tf_op jit(solution)/shard_map/ppermute | solution.py:321
  23.4 30.3 %collective-permute-start = (bf16[512,1024]{1,0:T(8,128)(2,1)S(1)}, bf16[512,1024]{1,0:T(8,128)(2,1)}, u32[]{:S(2)}, u32[]{:S(2)}) collective-permute-start(bf16[512,1024]{1,0:T(8,128)(2,1)S(1)} %bitcast.465), channel_id=1, source_target_pairs={{0,1},{1,0},{2,3},{3,2},{4,5},{5,4},{6,7},{7,6},{8,9},{9,8},{10,11... | collective-permute-start | bytes 3145736 | tf_op jit(solution)/shard_map/ppermute | solution.py:322
  23.8 65.8 %copy-start.64 = (f32[512]{0:T(512)}, f32[512]{0:T(512)S(1)}, u32[]{:S(2)}) copy-start(f32[512]{0:T(512)S(1)} %add_rsqrt_fusion.1) | copy-start | bytes 6148
  24.2 70.6 %copy-start.40 = (f32[512,32]{0,1:T(8,128)}, f32[512,32]{0,1:T(8,128)S(1)}, u32[]{:S(2)}) copy-start(f32[512,32]{0,1:T(8,128)S(1)} %get-tuple-element.162) | copy-start | bytes 196612
  24.2 70.6 %copy-start.42 = (f32[512,32]{0,1:T(8,128)}, f32[512,32]{0,1:T(8,128)S(1)}, u32[]{:S(2)}) copy-start(f32[512,32]{0,1:T(8,128)S(1)} %get-tuple-element.163) | copy-start | bytes 196612
  52.0 2.9 collective-permute-start.2
  52.1 48.5 %collective-permute-start.6 = (bf16[4,48,1024]{2,1,0:T(8,128)(2,1)S(1)}, bf16[4,48,1024]{2,1,0:T(8,128)(2,1)S(1)}, u32[]{:S(2)}, u32[]{:S(2)}) collective-permute-start(bf16[4,48,1024]{2,1,0:T(8,128)(2,1)S(1)} %constant_dynamic-slice_fusion.4), channel_id=1, source_target_pairs={{0,4},{4,0},{1,5},{5,1},{2,6},{6,2},{3,7},{7,3},{8,12},{12,8},{9,1... | collective-permute-start | bytes 1179656 | tf_op jit(solution)/shard_map/ppermute | solution.py:348
  96.8 29.3 %all-to-all-start = ((bf16[1,512,8,256]{1,3,0,2:T(8,128)(2,1)}), bf16[1,512,8,256]{1,3,0,2:T(8,128)(2,1)S(1)}, u32[]{:S(2)}, u32[]{:S(2)}) async-start(bf16[1,512,8,256]{1,3,0,2:T(8,128)(2,1)} %bitcast.442), calls=%async_computation | async-start | bytes 4194304 | tf_op jit(solution)/shard_map/all_to_all | solution.py:505
  100.6 414.9 %all-gather.14.cloned.1.call-start = ((), (), s32[]{:S(2)}) async-start(), calls=%async_computation.15 | async-start | bytes 3932160 | tf_op jit(solution)/shard_map/all_gather | solution.py:479
  101.9 20.0 %collective-permute-start.7 = (bf16[2,4,48,1024]{3,2,0,1:T(8,128)(2,1)}, bf16[2,4,48,1024]{3,2,0,1:T(8,128)(2,1)}, u32[]{:S(2)}, u32[]{:S(2)}) collective-permute-start(bf16[2,4,48,1024]{3,2,0,1:T(8,128)(2,1)} %fusion.70), channel_id=1, source_target_pairs={{0,2},{1,3},{2,0},{3,1},{4,6},{5,7},{6,4},{7,5},{8,10},{9,11},{10,... | collective-permute-start | bytes 2359304 | tf_op jit(solution)/shard_map/ppermute | solution.py:356
  124.7 52.2 %collective-permute-start.8 = (bf16[2,2,4,48,1024]{4,3,1,2,0:T(8,128)(2,1)}, bf16[2,2,4,48,1024]{4,3,1,2,0:T(8,128)(2,1)}, u32[]{:S(2)}, u32[]{:S(2)}) collective-permute-start(bf16[2,2,4,48,1024]{4,3,1,2,0:T(8,128)(2,1)} %maximum_select_fusion.1), channel_id=1, source_target_pairs={{0,1},{1,0},{2,3},{3,2},{4,5},{5,4},{6,7},{7,6},{8,9},{9,8},{10,11... | collective-permute-start | bytes 4718600 | tf_op jit(solution)/shard_map/ppermute | solution.py:356
  170.5 20.8 %all-to-all-start.1 = ((bf16[1,1024,4,128]{3,2,0,1:T(4,128)(2,1)}), bf16[1,1024,4,128]{3,2,0,1:T(4,128)(2,1)}, u32[]{:S(2)}, u32[]{:S(2)}) async-start(bf16[1,1024,4,128]{3,2,0,1:T(4,128)(2,1)} %pad_maximum_fusion.6), calls=%async_computation.1 | async-start | bytes 2097152 | tf_op jit(solution)/shard_map/all_to_all | solution.py:546
  174.9 340.6 %all-gather.16.cloned.1.call-start = ((), (), s32[]{:S(2)}) async-start(), calls=%async_computation.16 | async-start | bytes 3932160 | tf_op jit(solution)/shard_map/all_gather | solution.py:482
  202.1 25.1 %collective-permute-start.11 = (bf16[512,1024]{1,0:T(8,128)(2,1)}, bf16[512,1024]{1,0:T(8,128)(2,1)}, u32[]{:S(2)}, u32[]{:S(2)}) collective-permute-start(bf16[512,1024]{1,0:T(8,128)(2,1)} %multiply_convert_fusion), channel_id=1, source_target_pairs={{0,2},{1,3},{2,0},{3,1},{4,6},{5,7},{6,4},{7,5},{8,10},{9,11},{10,... | collective-permute-start | bytes 3145736 | tf_op jit(solution)/shard_map/ppermute | solution.py:321
  203.6 106.4 %collective-permute-start.13 = (bf16[4,8,3,128,128]{4,3,2,1,0:T(8,128)(2,1)}, bf16[4,8,3,128,128]{4,3,2,1,0:T(8,128)(2,1)}, u32[]{:S(2)}, u32[]{:S(2)}) collective-permute-start(bf16[4,8,3,128,128]{4,3,2,1,0:T(8,128)(2,1)} %bitcast.508), channel_id=1, source_target_pairs={{0,4},{4,0},{1,5},{5,1},{2,6},{6,2},{3,7},{7,3},{8,12},{12,8},{9,1... | collective-permute-start | bytes 9437192 | tf_op jit(solution)/shard_map/ppermute | solution.py:583
  205.6 84.6 %collective-permute-start.9 = (bf16[8,3,128,128]{3,2,1,0:T(8,128)(2,1)}, bf16[8,3,128,128]{3,2,1,0:T(8,128)(2,1)}, u32[]{:S(2)}, u32[]{:S(2)}) collective-permute-start(bf16[8,3,128,128]{3,2,1,0:T(8,128)(2,1)} %get-tuple-element.147), channel_id=1, source_target_pairs={{0,4},{4,0},{1,5},{5,1},{2,6},{6,2},{3,7},{7,3},{8,12},{12,8},{9,1... | collective-permute-start | bytes 2359304 | tf_op jit(solution)/shard_map/ppermute | solution.py:481
  205.7 87.7 %collective-permute-start.10 = (bf16[512,1024]{1,0:T(8,128)(2,1)}, bf16[512,1024]{1,0:T(8,128)(2,1)}, u32[]{:S(2)}, u32[]{:S(2)}) collective-permute-start(bf16[512,1024]{1,0:T(8,128)(2,1)} %multiply_convert_fusion), channel_id=1, source_target_pairs={{0,1},{1,0},{2,3},{3,2},{4,5},{5,4},{6,7},{7,6},{8,9},{9,8},{10,11... | collective-permute-start | bytes 3145736 | tf_op jit(solution)/shard_map/ppermute | solution.py:322
  227.2 66.2 %collective-permute-start.12 = (bf16[512,1024]{1,0:T(8,128)(2,1)}, bf16[512,1024]{1,0:T(8,128)(2,1)}, u32[]{:S(2)}, u32[]{:S(2)}) collective-permute-start(bf16[512,1024]{1,0:T(8,128)(2,1)} %collective-permute-done.11), channel_id=1, source_target_pairs={{0,1},{1,0},{2,3},{3,2},{4,5},{5,4},{6,7},{7,6},{8,9},{9,8},{10,11... | collective-permute-start | bytes 3145736 | tf_op jit(solution)/shard_map/ppermute | solution.py:323
  290.2 646.1 %reduce-scatter.14.cloned.1.call-start = ((), (), s32[]{:S(2)}) async-start(), calls=%async_computation.14 | async-start | bytes 3932160 | tf_op jit(solution)/shard_map/reduce_scatter | solution.py:618
  291.6 79.5 %collective-permute-start.15 = (bf16[4,8,3,128,128]{4,3,2,1,0:T(8,128)(2,1)}, bf16[4,8,3,128,128]{4,3,2,1,0:T(8,128)(2,1)}, u32[]{:S(2)}, u32[]{:S(2)}) collective-permute-start(bf16[4,8,3,128,128]{4,3,2,1,0:T(8,128)(2,1)} %bitcast.506), channel_id=1, source_target_pairs={{0,4},{4,0},{1,5},{5,1},{2,6},{6,2},{3,7},{7,3},{8,12},{12,8},{9,1... | collective-permute-start | bytes 9437192 | tf_op jit(solution)/shard_map/ppermute | solution.py:583
  308.2 62.4 %copy-start.49 = (f32[2048]{0:T(1024)}, f32[2048]{0:T(1024)S(1)}, u32[]{:S(2)}) copy-start(f32[2048]{0:T(1024)S(1)} %fusion.68) | copy-start | bytes 24580
  370.7 71.7 %collective-permute-start.14 = (bf16[4,8,3,128,128]{4,3,2,1,0:T(8,128)(2,1)}, bf16[4,8,3,128,128]{4,3,2,1,0:T(8,128)(2,1)S(1)}, u32[]{:S(2)}, u32[]{:S(2)}) collective-permute-start(bf16[4,8,3,128,128]{4,3,2,1,0:T(8,128)(2,1)} %shard_map.164.refs_0_), channel_id=1, source_target_pairs={{0,4},{4,0},{1,5},{5,1},{2,6},{6,2},{3,7},{7,3},{8,12},{12,8},{9,1... | collective-permute-start | bytes 9437192 | tf_op jit(solution)/shard_map/ppermute | solution.py:583
  586.7 385.6 %reduce-scatter.12.cloned.1.call-start = ((), (), s32[]{:S(2)}) async-start(), calls=%async_computation.13 | async-start | bytes 3932160 | tf_op jit(solution)/shard_map/reduce_scatter | solution.py:618
  587.5 394.6 %reduce-scatter.6.cloned.1.call-start = ((), (), s32[]{:S(2)}) async-start(), calls=%async_computation.10 | async-start | bytes 3932160 | tf_op jit(solution)/shard_map/reduce_scatter | solution.py:699
  613.7 6.7 collective-permute-start.20
  613.7 70.8 %collective-permute-start.22 = (bf16[4,8,3,128,128]{4,3,2,1,0:T(8,128)(2,1)}, bf16[4,8,3,128,128]{4,3,2,1,0:T(8,128)(2,1)}, u32[]{:S(2)}, u32[]{:S(2)}) collective-permute-start(bf16[4,8,3,128,128]{4,3,2,1,0:T(8,128)(2,1)} %shard_map.168), channel_id=1, source_target_pairs={{0,4},{4,0},{1,5},{5,1},{2,6},{6,2},{3,7},{7,3},{8,12},{12,8},{9,1... | collective-permute-start | bytes 9437192 | tf_op jit(solution)/shard_map/ppermute | solution.py:616
  619.8 4.2 collective-permute-start.17
  620.2 5.9 collective-permute-start.19
  623.5 26.1 %collective-permute-start.21 = (bf16[512,1024]{1,0:T(8,128)(2,1)S(1)}, bf16[512,1024]{1,0:T(8,128)(2,1)S(1)}, u32[]{:S(2)}, u32[]{:S(2)}) collective-permute-start(bf16[512,1024]{1,0:T(8,128)(2,1)S(1)} %fusion.39), channel_id=1, source_target_pairs={{0,2},{1,3},{2,0},{3,1},{4,6},{5,7},{6,4},{7,5},{8,10},{9,11},{10,... | collective-permute-start | bytes 3145736 | tf_op jit(solution)/shard_map/ppermute | solution.py:336
  624.0 26.5 %collective-permute-start.16 = (bf16[512,1024]{1,0:T(8,128)(2,1)S(1)}, bf16[512,1024]{1,0:T(8,128)(2,1)S(1)}, u32[]{:S(2)}, u32[]{:S(2)}) collective-permute-start(bf16[512,1024]{1,0:T(8,128)(2,1)S(1)} %get-tuple-element.144), channel_id=1, source_target_pairs={{0,1},{1,0},{2,3},{3,2},{4,5},{5,4},{6,7},{7,6},{8,9},{9,8},{10,11... | collective-permute-start | bytes 3145736 | tf_op jit(solution)/shard_map/ppermute | solution.py:331
  624.4 47.0 %collective-permute-start.18 = (bf16[512,1024]{1,0:T(8,128)(2,1)S(1)}, bf16[512,1024]{1,0:T(8,128)(2,1)S(1)}, u32[]{:S(2)}, u32[]{:S(2)}) collective-permute-start(bf16[512,1024]{1,0:T(8,128)(2,1)S(1)} %add_convert_fusion.4), channel_id=1, source_target_pairs={{0,2},{1,3},{2,0},{3,1},{4,6},{5,7},{6,4},{7,5},{8,10},{9,11},{10,... | collective-permute-start | bytes 3145736 | tf_op jit(solution)/shard_map/ppermute | solution.py:336
  696.6 18.6 %all-to-all-start.2 = ((bf16[1,512,8,128]{3,1,0,2:T(8,128)(2,1)}), bf16[1,512,8,128]{3,1,0,2:T(8,128)(2,1)S(1)}, u32[]{:S(2)}, u32[]{:S(2)}) async-start(bf16[1,512,8,128]{3,1,0,2:T(8,128)(2,1)} %copy.183), calls=%async_computation.2 | async-start | bytes 2097152 | tf_op jit(solution)/shard_map/all_to_all | solution.py:642
  700.2 283.2 %reduce-scatter.10.cloned.1.call-start = ((), (), s32[]{:S(2)}) async-start(), calls=%async_computation.12 | async-start | bytes 3932160 | tf_op jit(solution)/shard_map/reduce_scatter | solution.py:699
  700.5 82.2 %collective-permute-start.42 = (bf16[4,8,3,128,128]{4,3,2,1,0:T(8,128)(2,1)}, bf16[4,8,3,128,128]{4,3,2,1,0:T(8,128)(2,1)}, u32[]{:S(2)}, u32[]{:S(2)}) collective-permute-start(bf16[4,8,3,128,128]{4,3,2,1,0:T(8,128)(2,1)} %shard_map.172), channel_id=1, source_target_pairs={{0,4},{4,0},{1,5},{5,1},{2,6},{6,2},{3,7},{7,3},{8,12},{12,8},{9,1... | collective-permute-start | bytes 9437192 | tf_op jit(solution)/shard_map/ppermute | solution.py:616
  702.5 146.4 %collective-permute-start.23 = (bf16[4,8,3,128,128]{4,3,2,1,0:T(8,128)(2,1)}, bf16[4,8,3,128,128]{4,3,2,1,0:T(8,128)(2,1)}, u32[]{:S(2)}, u32[]{:S(2)}) collective-permute-start(bf16[4,8,3,128,128]{4,3,2,1,0:T(8,128)(2,1)} %shard_map.170), channel_id=1, source_target_pairs={{0,4},{4,0},{1,5},{5,1},{2,6},{6,2},{3,7},{7,3},{8,12},{12,8},{9,1... | collective-permute-start | bytes 9437192 | tf_op jit(solution)/shard_map/ppermute | solution.py:616
  707.1 146.7 %collective-permute-start.36 = (bf16[4,2,2,32,1024]{4,3,2,1,0:T(8,128)(2,1)}, bf16[4,2,2,32,1024]{4,3,2,1,0:T(8,128)(2,1)}, u32[]{:S(2)}, u32[]{:S(2)}) collective-permute-start(bf16[4,2,2,32,1024]{4,3,2,1,0:T(8,128)(2,1)} %dynamic-slice_bitcast_fusion.1), channel_id=1, source_target_pairs={{0,1},{1,0},{2,3},{3,2},{4,5},{5,4},{6,7},{7,6},{8,9},{9,8},{10,11... | collective-permute-start | bytes 3145736 | tf_op jit(solution)/shard_map/ppermute | solution.py:383
  848.9 31.2 %all-to-all-start.3 = ((bf16[1,1024,4,256]{3,2,0,1:T(4,128)(2,1)}), bf16[1,1024,4,256]{3,2,0,1:T(4,128)(2,1)}, u32[]{:S(2)}, u32[]{:S(2)}) async-start(bf16[1,1024,4,256]{3,2,0,1:T(4,128)(2,1)} %bitcast.427), calls=%async_computation.3 | async-start | bytes 4194304 | tf_op jit(solution)/shard_map/all_to_all | solution.py:703
  853.7 132.2 %reduce-scatter.8.cloned.1.call-start = ((), (), s32[]{:S(2)}) async-start(), calls=%async_computation.11 | async-start | bytes 3932160 | tf_op jit(solution)/shard_map/reduce_scatter | solution.py:699
  857.1 12.8 %collective-permute-start.37 = (bf16[4,2,32,1024]{3,2,1,0:T(8,128)(2,1)S(1)}, bf16[4,2,32,1024]{3,2,1,0:T(8,128)(2,1)S(1)}, u32[]{:S(2)}, u32[]{:S(2)}) collective-permute-start(bf16[4,2,32,1024]{3,2,1,0:T(8,128)(2,1)S(1)} %fusion.74), channel_id=1, source_target_pairs={{0,2},{1,3},{2,0},{3,1},{4,6},{5,7},{6,4},{7,5},{8,10},{9,11},{10,... | collective-permute-start | bytes 1572872 | tf_op jit(solution)/shard_map/ppermute | solution.py:383
  872.6 27.8 %collective-permute-start.38 = (bf16[4,32,1024]{2,1,0:T(8,128)(2,1)S(1)}, bf16[4,32,1024]{2,1,0:T(8,128)(2,1)}, u32[]{:S(2)}, u32[]{:S(2)}) collective-permute-start(bf16[4,32,1024]{2,1,0:T(8,128)(2,1)S(1)} %fusion.81), channel_id=1, source_target_pairs={{0,4},{4,0},{1,5},{5,1},{2,6},{6,2},{3,7},{7,3},{8,12},{12,8},{9,1... | collective-permute-start | bytes 786440 | tf_op jit(solution)/shard_map/ppermute | solution.py:375
  895.8 17.9 %collective-permute-start.30 = (bf16[4,2,2,64,1024]{4,3,2,1,0:T(8,128)(2,1)}, bf16[4,2,2,64,1024]{4,3,2,1,0:T(8,128)(2,1)}, u32[]{:S(2)}, u32[]{:S(2)}) collective-permute-start(bf16[4,2,2,64,1024]{4,3,2,1,0:T(8,128)(2,1)} %dynamic-slice_bitcast_fusion), channel_id=1, source_target_pairs={{0,1},{1,0},{2,3},{3,2},{4,5},{5,4},{6,7},{7,6},{8,9},{9,8},{10,11... | collective-permute-start | bytes 6291464 | tf_op jit(solution)/shard_map/ppermute | solution.py:383
  908.7 4.3 collective-permute-start.24
  908.8 11.8 %collective-permute-start.39 = (bf16[32,1024]{1,0:T(8,128)(2,1)S(1)}, bf16[32,1024]{1,0:T(8,128)(2,1)S(1)}, u32[]{:S(2)}, u32[]{:S(2)}) collective-permute-start(bf16[32,1024]{1,0:T(8,128)(2,1)S(1)} %get-tuple-element.156), channel_id=1, source_target_pairs={{0,8},{8,16},{16,24},{24,0},{1,9},{9,17},{17,25},{25,1},{2,10},{10... | collective-permute-start | bytes 196616 | tf_op jit(solution)/shard_map/ppermute | solution.py:375
  910.7 9.9 collective-permute-start.41
  912.6 15.1 %collective-permute-start.40 = (bf16[32,1024]{1,0:T(8,128)(2,1)S(1)}, bf16[32,1024]{1,0:T(8,128)(2,1)S(1)}, u32[]{:S(2)}, u32[]{:S(2)}) collective-permute-start(bf16[32,1024]{1,0:T(8,128)(2,1)S(1)} %get-tuple-element.158), channel_id=1, source_target_pairs={{0,16},{8,24},{16,0},{24,8},{1,17},{9,25},{17,1},{25,9},{2,18},{10... | collective-permute-start | bytes 196616 | tf_op jit(solution)/shard_map/ppermute | solution.py:375
  913.0 15.4 %collective-permute-start.25 = (bf16[4,2,16,128]{3,2,1,0:T(8,128)(2,1)S(1)}, bf16[4,2,16,128]{3,2,1,0:T(8,128)(2,1)S(1)}, u32[]{:S(2)}, u32[]{:S(2)}) collective-permute-start(bf16[4,2,16,128]{3,2,1,0:T(8,128)(2,1)S(1)} %fusion.95), channel_id=1, source_target_pairs={{0,2},{1,3},{2,0},{3,1},{4,6},{5,7},{6,4},{7,5},{8,10},{9,11},{10,... | collective-permute-start | bytes 98312 | tf_op jit(solution)/shard_map/ppermute | solution.py:383
  919.1 24.6 %collective-permute-start.31 = (bf16[4,2,64,1024]{3,2,1,0:T(8,128)(2,1)S(1)}, bf16[4,2,64,1024]{3,2,1,0:T(8,128)(2,1)}, u32[]{:S(2)}, u32[]{:S(2)}) collective-permute-start(bf16[4,2,64,1024]{3,2,1,0:T(8,128)(2,1)S(1)} %fusion.63), channel_id=1, source_target_pairs={{0,2},{1,3},{2,0},{3,1},{4,6},{5,7},{6,4},{7,5},{8,10},{9,11},{10,... | collective-permute-start | bytes 3145736 | tf_op jit(solution)/shard_map/ppermute | solution.py:383
  928.5 3.8 collective-permute-start.26
  932.3 16.4 %collective-permute-start.27 = (bf16[16,128]{1,0:T(8,128)(2,1)S(1)}, bf16[16,128]{1,0:T(8,128)(2,1)S(1)}, u32[]{:S(2)}, u32[]{:S(2)}) collective-permute-start(bf16[16,128]{1,0:T(8,128)(2,1)S(1)} %get-tuple-element.159), channel_id=1, source_target_pairs={{0,8},{8,16},{16,24},{24,0},{1,9},{9,17},{17,25},{25,1},{2,10},{10... | collective-permute-start | bytes 12296 | tf_op jit(solution)/shard_map/ppermute | solution.py:375
  932.4 16.4 %collective-permute-start.29 = (bf16[16,128]{1,0:T(8,128)(2,1)S(1)}, bf16[16,128]{1,0:T(8,128)(2,1)S(1)}, u32[]{:S(2)}, u32[]{:S(2)}) collective-permute-start(bf16[16,128]{1,0:T(8,128)(2,1)S(1)} %get-tuple-element.160), channel_id=1, source_target_pairs={{0,24},{8,0},{16,8},{24,16},{1,25},{9,1},{17,9},{25,17},{2,26},{10... | collective-permute-start | bytes 12296 | tf_op jit(solution)/shard_map/ppermute | solution.py:375
  936.3 12.4 %collective-permute-start.28 = (bf16[16,128]{1,0:T(8,128)(2,1)S(1)}, bf16[16,128]{1,0:T(8,128)(2,1)S(1)}, u32[]{:S(2)}, u32[]{:S(2)}) collective-permute-start(bf16[16,128]{1,0:T(8,128)(2,1)S(1)} %get-tuple-element.161), channel_id=1, source_target_pairs={{0,16},{8,24},{16,0},{24,8},{1,17},{9,25},{17,1},{25,9},{2,18},{10... | collective-permute-start | bytes 12296 | tf_op jit(solution)/shard_map/ppermute | solution.py:375
  936.4 36.0 %collective-permute-start.43 = (bf16[8,3,128,128]{3,2,1,0:T(8,128)(2,1)}, bf16[8,3,128,128]{3,2,1,0:T(8,128)(2,1)}, u32[]{:S(2)}, u32[]{:S(2)}) collective-permute-start(bf16[8,3,128,128]{3,2,1,0:T(8,128)(2,1)} %bitcast.512), channel_id=1, source_target_pairs={{0,4},{4,0},{1,5},{5,1},{2,6},{6,2},{3,7},{7,3},{8,12},{12,8},{9,1... | collective-permute-start | bytes 2359304 | tf_op jit(solution)/shard_map/ppermute | solution.py:700
  946.8 19.5 %collective-permute-start.32 = (bf16[4,64,1024]{2,1,0:T(8,128)(2,1)}, bf16[4,64,1024]{2,1,0:T(8,128)(2,1)}, u32[]{:S(2)}, u32[]{:S(2)}) collective-permute-start(bf16[4,64,1024]{2,1,0:T(8,128)(2,1)} %fusion.75), channel_id=1, source_target_pairs={{0,4},{4,0},{1,5},{5,1},{2,6},{6,2},{3,7},{7,3},{8,12},{12,8},{9,1... | collective-permute-start | bytes 1572872 | tf_op jit(solution)/shard_map/ppermute | solution.py:375
  967.6 8.2 collective-permute-start.33
  968.3 7.5 collective-permute-start.35
  971.5 9.8 collective-permute-start.34
  (73 other events, 690.4 us)
Sparse Core Ops, SparseCore 0:
  11.5 71.1 all-gather.11
  84.2 62.3 all-gather.19
  148.1 62.1 all-gather.21
  211.7 62.1 all-gather.17
  275.3 62.1 all-gather.13
  339.0 62.1 all-gather.15
  586.8 59.4 reduce-scatter.13
  648.6 60.2 reduce-scatter.11
  711.3 60.2 reduce-scatter.5
  789.3 58.4 reduce-scatter.9
  864.2 64.8 reduce-scatter.7

commit v3 on v2

--- a/solution.py
+++ b/solution.py
@@ -209,9 +209,9 @@
 
         return carry
 
-    lax.fori_loop(0, tiles, tile_step, 0)
-
-    slab = 256
+    lax.fori_loop(0, tiles, tile_step, 0, unroll=True)
+
+    slab = 512
 
     def weight_step(tile, carry):
         rows = pl.ds(pl.multiple_of(tile * slab, slab), slab)
@@ -312,6 +312,105 @@
     )(places, *operands)
 
 
+def visible_mask(first_row, first_key, row_count, key_count):
+    rows = first_row + lax.broadcasted_iota(jnp.int32, (row_count, key_count), 0)
+    keys = first_key + lax.broadcasted_iota(jnp.int32, (row_count, key_count), 1)
+    return rows >= keys
+
+
+def attend_kernel(block, heads_ref, out_ref, log_ref):
+    length = heads_ref.shape[1]
+    keys = heads_ref[0, :, 2 * HEAD : 3 * HEAD]
+    values = heads_ref[0, :, 3 * HEAD :]
+    for offset in range(0, length, block):
+        limit = offset + block
+        mask = visible_mask(offset, 0, block, limit)
+        for which in range(2):
+            lanes = slice(which * HEAD, (which + 1) * HEAD)
+            query = heads_ref[0, offset:limit, lanes]
+            scores = times_transposed(query, keys[:limit]) * HEAD ** (-0.5)
+            scores = jnp.where(mask, scores, NEG)
+            top_score = jnp.max(scores, axis=1, keepdims=True)
+            exponent = jnp.exp(scores - top_score)
+            denominator = jnp.sum(exponent, axis=1, keepdims=True)
+            weights = (exponent * (1.0 / denominator)).astype(jnp.bfloat16)
+            out_ref[0, offset:limit, lanes] = dot_nn(weights, values[:limit]).astype(jnp.bfloat16)
+            log_ref[0, 0, offset:limit, which : which + 1] = top_score + jnp.log(denominator)
+
+
+def attend_back_kernel(block, heads_ref, grad_ref, log_ref, out_ref, grad_keys, grad_values):
+    length = heads_ref.shape[1]
+    grad_keys[...] = jnp.zeros_like(grad_keys)
+    grad_values[...] = jnp.zeros_like(grad_values)
+    keys = heads_ref[0, :, 2 * HEAD : 3 * HEAD]
+    values = heads_ref[0, :, 3 * HEAD :]
+    for offset in range(0, length, block):
+        limit = offset + block
+        mask = visible_mask(offset, 0, block, limit)
+        for which in range(2):
+            lanes = slice(which * HEAD, (which + 1) * HEAD)
+            query = heads_ref[0, offset:limit, lanes]
+            grad = grad_ref[0, offset:limit, lanes]
+            scores = times_transposed(query, keys[:limit]) * HEAD ** (-0.5)
+            log_total = log_ref[0, 0, offset:limit, which : which + 1]
+            weights = jnp.where(mask, jnp.exp(jnp.where(mask, scores, NEG) - log_total), 0.0)
+            grad_weights = times_transposed(grad, values[:limit])
+            middle = jnp.sum(weights * grad_weights, axis=1, keepdims=True)
+            grad_scores = (weights * (grad_weights - middle)).astype(jnp.bfloat16)
+            grad_values[:limit, :] += transposed_times(weights.astype(jnp.bfloat16), grad)
+            grad_keys[:limit, :] += transposed_times(grad_scores, query)
+            out_ref[0, offset:limit, lanes] = (
+                dot_nn(grad_scores, keys[:limit]) * HEAD ** (-0.5)
+            ).astype(jnp.bfloat16)
+    out_ref[0, :, 2 * HEAD : 3 * HEAD] = (grad_keys[...] * HEAD ** (-0.5)).astype(jnp.bfloat16)
+    out_ref[0, :, 3 * HEAD :] = grad_values[...].astype(jnp.bfloat16)
+
+
+def attend(head_rows, grad_rows=None, log_totals=None):
+    sequences, length, width = head_rows.shape
+    groups = width // (4 * HEAD)
+    block = min(256, length)
+
+    def per_group(lane_count):
+        return pl.BlockSpec((1, length, lane_count), lambda s, g: (s, 0, g))
+
+    logs = pl.BlockSpec((1, 1, length, 2), lambda s, g: (s, g, 0, 0))
+    work = sequences * groups * length * length * HEAD * 2
+    params = pltpu.CompilerParams(
+        dimension_semantics=("arbitrary", "arbitrary"), vmem_limit_bytes=48 * 2**20
+    )
+    if grad_rows is None:
+        return pl.pallas_call(
+            functools.partial(attend_kernel, block),
+            grid=(sequences, groups),
+            in_specs=[per_group(4 * HEAD)],
+            out_specs=[per_group(2 * HEAD), logs],
+            out_shape=[
+                jax.ShapeDtypeStruct((sequences, length, groups * 2 * HEAD), jnp.bfloat16),
+                jax.ShapeDtypeStruct((sequences, groups, length, 2), jnp.float32),
+            ],
+            compiler_params=params,
+            cost_estimate=pl.CostEstimate(
+                flops=16 * work, bytes_accessed=8 * 2**20, transcendentals=work // HEAD
+            ),
+        )(head_rows)
+    return pl.pallas_call(
+        functools.partial(attend_back_kernel, block),
+        grid=(sequences, groups),
+        in_specs=[per_group(4 * HEAD), per_group(2 * HEAD), logs],
+        out_specs=per_group(4 * HEAD),
+        out_shape=jax.ShapeDtypeStruct((sequences, length, width), jnp.bfloat16),
+        scratch_shapes=[
+            pltpu.VMEM((length, HEAD), jnp.float32),
+            pltpu.VMEM((length, HEAD), jnp.float32),
+        ],
+        compiler_params=params,
+        cost_estimate=pl.CostEstimate(
+            flops=36 * work, bytes_accessed=8 * 2**20, transcendentals=work // HEAD
+        ),
+    )(head_rows, grad_rows, log_totals)
+
+
 def swap_pairs(count, bit):
     return [(index, index ^ bit) for index in range(count)]
 
@@ -442,7 +541,17 @@
     device_count = context_count * lax.axis_size("fsdp") * lax.axis_size("tp")
     gain_count, router_count = norm_gains.size, router_weight.size
     packed = lax.all_gather(pack_rows([query_key_value, norm_gains], model_width), ALL_AXES, axis=0)
-    packed = after(packed, grads_turned)
+    shard_depth = expert_in.shape[2]
+    chunk_experts = EXPERTS // CHUNKS
+    paired = context_count == 2
+    expert_shards = jnp.concatenate([expert_in, expert_out[:, None]], axis=1)
+    if paired:
+        last_other = lax.ppermute(
+            expert_shards[EXPERTS - chunk_experts :], "ctx", swap_pairs(2, 1)
+        )
+        packed, last_other = together(after(packed, grads_turned), last_other)
+    else:
+        packed = after(packed, grads_turned)
     packed_later = gather_dense(pack_rows([attn_output, router_weight], model_width))
     inward_rows, output_rows = query_key_value.shape[0], attn_output.shape[0]
     inward_full = packed[:, :inward_rows].reshape(-1, model_width)
@@ -461,10 +570,6 @@
         .transpose(1, 0, 2)
         .reshape(EXPERTS, model_width)
     )
-    paired = context_count == 2
-    expert_shards = jnp.concatenate([expert_in, expert_out[:, None]], axis=1)
-    shard_depth = expert_in.shape[2]
-    chunk_experts = EXPERTS // CHUNKS
     my_context = lax.axis_index("ctx").astype(jnp.int32)
     if paired:
         places = jnp.stack([my_context, 1 - my_context]) * shard_depth
@@ -478,8 +583,7 @@
         if paired:
             expert_pieces.append([lax.all_gather(shard, "fsdp", axis=0)])
             if chunk == CHUNKS - 1:
-                other = lax.ppermute(shard, "ctx", swap_pairs(2, 1))
-                expert_pieces[chunk].append(lax.all_gather(other, "fsdp", axis=0))
+                expert_pieces[chunk].append(lax.all_gather(last_other, "fsdp", axis=0))
         else:
             expert_pieces.append([lax.all_gather(shard, ("fsdp", "ctx"), axis=0)])
     gain_rows = gain_full.astype(jnp.float32)
@@ -503,46 +607,9 @@
         local_seqs, local_positions, KV_HEADS, 4 * head_size
     )
     head_rows = lax.all_to_all(sent_heads, "ctx", split_axis=2, concat_axis=1, tiled=True)
-    queries = head_rows[..., : 2 * head_size].reshape(
-        local_seqs, length, local_groups, 2, head_size
-    )
-    key_rows = head_rows[..., 2 * head_size : 3 * head_size]
-    value_rows = head_rows[..., 3 * head_size :]
-    block_rows = min(512, length)
-    key_index = jnp.arange(length)
-    attended = []
-    log_totals = []
-    for offset in range(0, length, block_rows):
-        limit_row = offset + block_rows
-        scores = (
-            jnp.einsum(
-                "sqgjd,skgd->sgjqk",
-                queries[:, offset:limit_row],
-                key_rows[:, :limit_row],
-                preferred_element_type=jnp.float32,
-            )
-            * score_scale
-        )
-        visible = (offset + jnp.arange(block_rows))[:, None] >= key_index[None, :limit_row]
-        scores = jnp.where(visible, scores, NEG)
-        top_score = jnp.max(scores, axis=-1, keepdims=True)
-        exponent = jnp.exp(scores - top_score)
-        denominator = jnp.sum(exponent, axis=-1, keepdims=True)
-        weights = exponent / denominator
-        attended.append(
-            jnp.einsum(
-                "sgjqk,skgd->sqgjd",
-                weights.astype(jnp.bfloat16),
-                value_rows[:, :limit_row],
-                preferred_element_type=jnp.float32,
-            )
-        )
-        log_totals.append(top_score + jnp.log(denominator))
-    head_output = (
-        jnp.concatenate(attended, axis=1)
-        .astype(jnp.bfloat16)
-        .reshape(local_seqs, length, local_groups, 2 * head_size)
-    )
+    head_rows = head_rows.reshape(local_seqs, length, -1)
+    head_output, log_totals = attend(head_rows)
+    head_output = head_output.reshape(local_seqs, length, local_groups, 2 * head_size)
     merged = lax.all_to_all(head_output, "ctx", split_axis=1, concat_axis=2, tiled=True).reshape(
         row_count, HEADS * head_size
     )
@@ -581,6 +648,10 @@
             near = after(near, marks[chunk - 2])
             expert_pieces[chunk][0] = near
         expert_pieces[chunk].append(lax.ppermute(near, "ctx", swap_pairs(2, 1)))
+
+    def cross(chunk):
+        held = after(far_sums[chunk], marks[chunk + 1])
+        arrivals.append(lax.ppermute(held, "ctx", swap_pairs(2, 1)))
 
     if paired:
         fetch(0)
@@ -599,6 +670,7 @@
             gates,
             totals,
             chunk * chunk_experts,
+            arrivals if paired and chunk == CHUNKS - 1 else (),
         )
         totals = (moe_total, back_total)
         marks.append(choice)
@@ -606,14 +678,17 @@
         if paired:
             own_sums.append(grad_pieces[0])
             far_sums.append(grad_pieces[1])
+            if chunk == 1:
+                cross(0)
+            elif chunk == CHUNKS - 1:
+                arrivals[0] = grad_pieces[2]
         else:
             chunk_sums.append(
                 lax.psum_scatter(grad_pieces[0], ("fsdp", "ctx"), scatter_dimension=0)
             )
     if paired:
-        for chunk in range(CHUNKS - 1):
-            held = after(far_sums[chunk], marks[min(chunk + 1, CHUNKS - 1)])
-            arrivals.append(lax.ppermute(held, "ctx", swap_pairs(2, 1)))
+        for chunk in range(1, CHUNKS - 1):
+            cross(chunk)
         last_sums = [
             lax.psum_scatter(part, "fsdp", scatter_dimension=0)
             for part in (far_sums[-1], own_sums[-1])
@@ -632,7 +707,7 @@
     )
     grad_attn = by_rows(grad_hidden.astype(jnp.bfloat16))
     if paired:
-        grad_attn, arrivals[0] = together(grad_attn, arrivals[0])
+        grad_attn, arrivals[1] = together(grad_attn, arrivals[1])
     grad_output_weight = transposed_times(grad_attn, merged)
     grad_merged = (
         jnp.dot(grad_attn, output_full, preferred_element_type=jnp.float32)
@@ -640,60 +715,11 @@
         .reshape(local_seqs, local_positions, KV_HEADS, 2 * head_size)
     )
     grad_heads = lax.all_to_all(by_rows(grad_merged), "ctx", split_axis=2, concat_axis=1, tiled=True)
-    grad_keys = jnp.zeros((local_seqs, length, local_groups, head_size), jnp.float32)
-    grad_values = jnp.zeros((local_seqs, length, local_groups, head_size), jnp.float32)
-    grad_query_blocks = []
-    for offset, log_total in zip(range(0, length, block_rows), log_totals):
-        limit_row = offset + block_rows
-        query_block = queries[:, offset:limit_row]
-        key_part = key_rows[:, :limit_row]
-        value_part = value_rows[:, :limit_row]
-        scores = (
-            jnp.einsum(
-                "sqgjd,skgd->sgjqk", query_block, key_part, preferred_element_type=jnp.float32
-            )
-            * score_scale
-        )
-        visible = (offset + jnp.arange(block_rows))[:, None] >= key_index[None, :limit_row]
-        scores = jnp.where(visible, scores, NEG)
-        weights = jnp.exp(scores - log_total)
-        grad_block = grad_heads[:, offset:limit_row].reshape(
-            local_seqs, block_rows, local_groups, 2, head_size
-        )
-        grad_values = grad_values.at[:, :limit_row].add(
-            jnp.einsum(
-                "sgjqk,sqgjd->skgd",
-                weights.astype(jnp.bfloat16),
-                grad_block,
-                preferred_element_type=jnp.float32,
-            )
-        )
-        grad_weights = jnp.einsum(
-            "sqgjd,skgd->sgjqk", grad_block, value_part, preferred_element_type=jnp.float32
-        )
-        grad_scores = (
-            weights * (grad_weights - jnp.sum(weights * grad_weights, axis=-1, keepdims=True))
-        ).astype(jnp.bfloat16)
-        grad_query_blocks.append(
-            jnp.einsum(
-                "sgjqk,skgd->sqgjd", grad_scores, key_part, preferred_element_type=jnp.float32
-            )
-            * score_scale
-        )
-        grad_keys = grad_keys.at[:, :limit_row].add(
-            jnp.einsum(
-                "sgjqk,sqgjd->skgd", grad_scores, query_block, preferred_element_type=jnp.float32
-            )
-            * score_scale
-        )
-    grad_queries = jnp.concatenate(grad_query_blocks, axis=1).reshape(
-        local_seqs, length, local_groups, 2 * head_size
-    )
-    grad_head_rows = jnp.concatenate([grad_queries, grad_keys, grad_values], axis=-1).astype(
-        jnp.bfloat16
-    )
+    grad_head_rows = attend(
+        head_rows, grad_heads.reshape(local_seqs, length, -1), log_totals
+    ).reshape(local_seqs, length, local_groups, 4 * head_size)
     if paired:
-        grad_head_rows, arrivals[1] = together(grad_head_rows, arrivals[1])
+        grad_head_rows, arrivals[2] = together(grad_head_rows, arrivals[2])
         for own, arrived in zip(own_sums, arrivals):
             joined = (own.astype(jnp.float32) + arrived.astype(jnp.float32)).astype(jnp.bfloat16)
             chunk_sums.append(lax.psum_scatter(joined, "fsdp", scatter_dimension=0))

time: 1010 us -> 888 us (0.88)
  matrix products: 111 us -> 35.6 us
  other arithmetic: 142 us -> 95 us
  Pallas kernels: 274 us -> 286 us
    ppermute x4, waiting for transfers between devices: 111 us -> 13.5 us  [the longest x3 13.5 us: cross(): arrivals.append(lax.ppermute(held, 'ctx', swap_pairs(2, 1)))]
    dot_general x12 -> x0, matrix products: 74.4 us -> none  [the longest x2 20.5 us: per_device(): jnp.einsum('sqgjd,skgd->sgjqk', grad_block, value_part, preferred_element...]
    all_to_all x1, waiting for transfers between devices: 8.12 us -> 67.1 us  [per_device(): lax.all_to_all(by_rows(grad_merged), 'ctx', split_axis=2, concat_axis=1,...]
    pallas_call x0 -> x2, Pallas kernels: none -> 42.9 us  [the longest x1 24.9 us: attend(): pl.pallas_call(functools.partial(attend_back_kernel, block), grid=(sequen...]
    ppermute x3, waiting for transfers between devices: 0.01 us -> 36.8 us  [fetch(): expert_pieces[chunk].append(lax.ppermute(near, 'ctx', swap_pairs(2, 1)))]
    pallas_call x4, Pallas kernels: 274 us -> 243 us  [expert_pass(): pl.pallas_call(functools.partial(expert_kernel, first, steps, base_expert...]
    ppermute x12, waiting for transfers between devices: 34.6 us -> 9.37 us  [scatter_axis(): lax.ppermute(sent, name, shifted(count, step)).astype(jnp.float32)]
    all_to_all x1, waiting for transfers between devices: 1.34 us -> 21.4 us  [per_device(): lax.all_to_all(sent_heads, 'ctx', split_axis=2, concat_axis=1, tiled=True)]
  transfers between devices with their start and end apart: 59 -> 59, of which waited for: 22 -> 21; matrix products, arithmetic and copies ran while one was open for 32% -> 22% of each run, Pallas kernels for 20% -> 25%
where the time goes in v3:
time: 888 us; the launch traced here: 880 us
  waiting for transfers between devices  303 us (34%)
  Pallas kernels  286 us (32%)
  other arithmetic  95 us (11%)
  local copies, waits for them, and re-layouts  86.4 us (10%)
  starting transfers between devices  58.2 us (7%)
  matrix products  35.6 us (4%)
  between operations  15.7 us (2%)
    pallas_call x4, Pallas kernels, expert_pass(): pl.pallas_call(functools.partial(expert_kernel, first, steps, base_expert...  243 us
    all_to_all x1, waiting for transfers between devices, per_device(): lax.all_to_all(by_rows(grad_merged), 'ctx', split_axis=2, concat_axis=1,...  67.1 us
    ppermute x2, waiting for transfers between devices, gather_group(): across = lax.ppermute(rows, 'tp', swap_pairs(count, 2))  44.4 us
    ppermute x2, waiting for transfers between devices, scatter_group(): lax.ppermute((parts[2] + first).astype(jnp.bfloat16), 'tp', swap_pairs(co...  42.6 us
    ppermute x3, waiting for transfers between devices, fetch(): expert_pieces[chunk].append(lax.ppermute(near, 'ctx', swap_pairs(2, 1)))  36.8 us
    pallas_call x1, Pallas kernels, attend(): pl.pallas_call(functools.partial(attend_back_kernel, block), grid=(sequen...  24.9 us
    all_to_all x1, waiting for transfers between devices, per_device(): lax.all_to_all(sent_heads, 'ctx', split_axis=2, concat_axis=1, tiled=True)  21.4 us
    convert_element_type x3, other arithmetic, per_device(): (own.astype(jnp.float32) + arrived.astype(jnp.float32)).astype(jnp.bfloat16)  19.2 us
  transfers between devices with their start and end apart: 59, of which 21 were waited for; matrix products, arithmetic and copies ran while one was open for 22% of the time, Pallas kernels for 25%

profile of v3, /device:TPU:0, one launch (start us, length us, event | category | flops | bytes accessed | tf_op | source)
XLA Modules:
  0.0 880.4 jit_solution(14016482912825176715)
XLA Ops:
  9.8 3.7 pad_maximum_fusion.5
  14.4 5.1 collective-permute-start.4
  24.3 5.2 collective-permute-done.5
  29.6 21.0 %collective-permute-done.1 = bf16[512,1024]{1,0:T(8,128)(2,1)} collective-permute-done((bf16[512,1024]{1,0:T(8,128)(2,1)S(1)}, bf16[512,1024]{1,0:T(8,128)(2,1)}, u32[]{:S(2)}, u32[]{:S(2)}) %collective-permute-start.1) | collective-permute-done | bytes 1048608 | tf_op jit(solution)/shard_map/ppermute | solution.py:420
  54.4 8.6 collective-permute-done.7
  65.8 3.5 pad_maximum_fusion.1.refs_4_
  69.4 6.5 copy.79
  75.9 13.4 %all-gather.12.cloned.1.call-done.refs_0_ = bf16[32,80,1024]{2,1,0:T(8,128)(2,1)} async-done(((bf16[1,80,1024]{2,1,0:T(8,128)(2,1)}), bf16[32,80,1024]{2,1,0:T(8,128)(2,1)}) %all-gather.12.cloned.1.call-update) | async-done | bytes 5242896 | tf_op jit(solution)/shard_map/all_gather | solution.py:543
  90.6 5.0 slice.126
  96.4 5.0 convolution_bitcast_fusion
  104.6 3.8 all-to-all-start
  109.4 2.8 maximum_select_fusion.1
  112.5 21.4 %all-to-all-done = bf16[1,512,8,256]{3,1,0,2:T(8,128)(2,1)S(1)} async-done(((bf16[1,512,8,256]{3,1,0,2:T(8,128)(2,1)}), bf16[1,512,8,256]{3,1,0,2:T(8,128)(2,1)S(1)}, u32[]{:S(2)}, u32[]{:S(2)}) %all-to-all-start) | async-done | bytes 2097184 | tf_op jit(solution)/shard_map/all_to_all | solution.py:609
  133.9 2.9 copy.81
  136.9 3.2 reshape.478.heads_ref
  140.1 18.0 %shard_map.154 = (bf16[1,1024,512]{2,1,0:T(8,128)(2,1)S(1)}, f32[1,4,1024,2]{3,2,1,0:T(8,128)S(1)}) custom-call(bf16[1,1024,1024]{2,1,0:T(8,128)(2,1)S(1)} %reshape.478.heads_ref), custom_call_target="tpu_custom_call" | custom-call | flops 8589934592 | bytes 8388608 | tf_op jit(solution)/shard_map/pallas_call | solution.py:383
  160.5 4.6 all-to-all-start.1
  171.5 7.3 all-to-all-done.1
  181.5 3.6 multiply_reduce_fusion.2
  187.2 23.4 %collective-permute-done.11 = bf16[512,1024]{1,0:T(8,128)(2,1)} collective-permute-done((bf16[512,1024]{1,0:T(8,128)(2,1)S(1)}, bf16[512,1024]{1,0:T(8,128)(2,1)}, u32[]{:S(2)}, u32[]{:S(2)}) %collective-permute-start.11) | collective-permute-done | bytes 1048608 | tf_op jit(solution)/shard_map/ppermute | solution.py:420
  218.7 3.6 pad_maximum_fusion.2.refs_2_
  222.3 6.7 copy.86
  228.9 3.5 fusion.70
  236.4 21.8 %collective-permute-done.13.refs_1_ = bf16[4,8,3,128,128]{4,3,2,1,0:T(8,128)(2,1)} collective-permute-done((bf16[4,8,3,128,128]{4,3,2,1,0:T(8,128)(2,1)}, bf16[4,8,3,128,128]{4,3,2,1,0:T(8,128)(2,1)}, u32[]{:S(2)}, u32[]{:S(2)}) %collective-permute-start.13) | collective-permute-done | bytes 3145760 | tf_op jit(solution)/shard_map/ppermute | solution.py:650
  258.2 57.1 %shard_map.155 = (f32[2048,1024]{1,0:T(8,128)}, f32[2048,1024]{1,0:T(8,128)}, f32[2048,128]{1,0:T(8,128)}, bf16[4,8,3,128,128]{4,3,2,1,0:T(8,128)(2,1)}, bf16[4,8,3,128,128]{4,3,2,1,0:T(8,128)(2,1)}) custom-call(s32[2]{0:T(128)} %add_multiply_fusion.places_ref, bf16[4,8,3,128,128]{4,3,2,1,0:T(8,128)(2,1)} %bitcast.303, ...), custom_call_target="tpu_custom_call" | custom-call | flops 38654705664 | bytes 41943040 | tf_op jit(solution)/shard_map/pallas_call | solution.py:272
  315.7 9.9 %collective-permute-done.15.refs_1_ = bf16[4,8,3,128,128]{4,3,2,1,0:T(8,128)(2,1)} collective-permute-done((bf16[4,8,3,128,128]{4,3,2,1,0:T(8,128)(2,1)}, bf16[4,8,3,128,128]{4,3,2,1,0:T(8,128)(2,1)}, u32[]{:S(2)}, u32[]{:S(2)}) %collective-permute-start.15) | collective-permute-done | bytes 3145760 | tf_op jit(solution)/shard_map/ppermute | solution.py:650
  325.6 61.9 %shard_map.157 = (f32[2048,1024]{1,0:T(8,128)}, f32[2048,1024]{1,0:T(8,128)}, f32[2048,128]{1,0:T(8,128)}, bf16[4,8,3,128,128]{4,3,2,1,0:T(8,128)(2,1)}, bf16[4,8,3,128,128]{4,3,2,1,0:T(8,128)(2,1)}) custom-call(s32[2]{0:T(128)} %add_multiply_fusion.places_ref, bf16[4,8,3,128,128]{4,3,2,1,0:T(8,128)(2,1)} %bitcast.301, ...), custom_call_target="tpu_custom_call", output_to_operand_aliasing={{0}: (8, {}), {1}: (9, {})} | custom-call | flops 38654705664 | bytes 41943040 | tf_op jit(solution)/shard_map/pallas_call | solution.py:272
  387.9 5.1 collective-permute-done.14.refs_1_
  393.0 62.1 %shard_map.158 = (f32[2048,1024]{1,0:T(8,128)}, f32[2048,1024]{1,0:T(8,128)}, f32[2048,128]{1,0:T(8,128)}, bf16[4,8,3,128,128]{4,3,2,1,0:T(8,128)(2,1)}, bf16[4,8,3,128,128]{4,3,2,1,0:T(8,128)(2,1)}) custom-call(s32[2]{0:T(128)} %add_multiply_fusion.places_ref, ...), custom_call_target="tpu_custom_call", output_to_operand_aliasing={{0}: (8, {}), {1}: (9, {})} | custom-call | flops 38654705664 | bytes 41943040 | tf_op jit(solution)/shard_map/pallas_call | solution.py:272
  455.2 2.9 collective-permute-done.16.refs_9_
  458.1 62.0 %shard_map.160 = (f32[2048,1024]{1,0:T(8,128)}, f32[2048,1024]{1,0:T(8,128)}, f32[2048,128]{1,0:T(8,128)}, bf16[4,8,3,128,128]{4,3,2,1,0:T(8,128)(2,1)}, bf16[4,...) custom-call(s32[2]{0:T(128)} %add_multiply_fusion.places_ref, ...), custom_call_target="tpu_custom_call", output_to_operand_aliasing={{0}: (8, {}), {1}: (9, {}), {5}: (10, {})} | custom-call | flops 38654705664 | bytes 41943040 | tf_op jit(solution)/shard_map/pallas_call | solution.py:272
  520.2 6.4 add_convert_fusion.2
  527.8 3.2 multiply_reduce_fusion.3
  531.1 6.0 fusion.44
  537.1 13.7 %fusion.66 = (bf16[2048,1024]{1,0:T(8,128)(2,1)}, f32[2048,1024]{1,0:T(8,128)}) fusion(f32[2048,1024]{1,0:T(8,128)} %get-tuple-element.50, f32[2048,1024]{1,0:T(8,128)} %fusion.44), kind=kLoop, calls=%fused_computation.181 | loop fusion | flops 4194304 | bytes 29360128 | tf_op jit(solution)/shard_map/convert.18
  550.8 2.7 fusion.68
  554.2 4.3 convert.43
  559.3 2.6 fusion.15
  566.2 21.7 %collective-permute-done.22 = bf16[512,1024]{1,0:T(8,128)(2,1)S(1)} collective-permute-done((bf16[512,1024]{1,0:T(8,128)(2,1)S(1)}, bf16[512,1024]{1,0:T(8,128)(2,1)S(1)}, u32[]{:S(2)}, u32[]{:S(2)}) %collective-permute-start.22) | collective-permute-done | bytes 1048608 | tf_op jit(solution)/shard_map/ppermute | solution.py:435
  588.9 20.8 %collective-permute-done.19 = bf16[512,1024]{1,0:T(8,128)(2,1)S(1)} collective-permute-done((bf16[512,1024]{1,0:T(8,128)(2,1)S(1)}, bf16[512,1024]{1,0:T(8,128)(2,1)S(1)}, u32[]{:S(2)}, u32[]{:S(2)}) %collective-permute-start.19) | collective-permute-done | bytes 1048608 | tf_op jit(solution)/shard_map/ppermute | solution.py:435
  609.7 4.1 fusion.65
  613.8 10.6 %collective-permute-done.23.refs_1_ = bf16[4,8,3,128,128]{4,3,2,1,0:T(8,128)(2,1)} collective-permute-done((bf16[4,8,3,128,128]{4,3,2,1,0:T(8,128)(2,1)}, bf16[4,8,3,128,128]{4,3,2,1,0:T(8,128)(2,1)}, u32[]{:S(2)}, u32[]{:S(2)}) %collective-permute-start.23) | collective-permute-done | bytes 3145760 | tf_op jit(solution)/shard_map/ppermute | solution.py:654
  624.4 6.4 add_convert_fusion.1
  632.0 2.9 fusion.17
  636.3 4.0 all-to-all-start.2
  640.4 2.8 convolution_convert_fusion.1
  644.9 67.1 %all-to-all-done.2 = bf16[1,512,8,128]{3,1,0,2:T(8,128)(2,1)S(1)} async-done(((bf16[1,512,8,128]{3,1,0,2:T(8,128)(2,1)}), bf16[1,512,8,128]{3,1,0,2:T(8,128)(2,1)S(1)}, u32[]{:S(2)}, u32[]{:S(2)}) %all-to-all-start.2) | async-done | bytes 1048608 | tf_op jit(solution)/shard_map/all_to_all | solution.py:717
  715.3 24.9 %shard_map.163 = bf16[1,1024,1024]{2,1,0:T(8,128)(2,1)S(1)} custom-call(bf16[1,1024,1024]{2,1,0:T(8,128)(2,1)S(1)} %reshape.478.heads_ref, bf16[1,1024,512]{2,1,0:T(8,128)(2,1)S(1)} %reshape.492.grad_ref, f32[1,4,1024,2]{3,2,1,0:T(8,128)} %copy-done.3), custom_call_target="tpu_custom_call" | custom-call | flops 19327352832 | bytes 8388608 | tf_op jit(solution)/shard_map/pallas_call | solution.py:397
  741.5 4.5 reshape.493.refs_0_
  746.0 3.9 all-to-all-start.3
  750.0 5.5 fusion.43
  756.3 6.4 add_convert_fusion
  767.9 6.4 all-to-all-done.3
  775.6 3.1 copy.94
  781.4 2.5 convolution_convert_fusion
  788.3 3.9 fusion.11
  800.3 2.7 convert_add_fusion
  808.9 2.8 collective-permute-start.30
  811.9 15.3 %collective-permute-done.32 = bf16[4,2,64,1024]{3,2,1,0:T(8,128)(2,1)S(1)} collective-permute-done((bf16[4,2,64,1024]{3,2,1,0:T(8,128)(2,1)S(1)}, bf16[4,2,64,1024]{3,2,1,0:T(8,128)(2,1)S(1)}, u32[]{:S(2)}, u32[]{:S(2)}) %collective-permute-start.32) | collective-permute-done | bytes 1048608 | tf_op jit(solution)/shard_map/ppermute | solution.py:482
  838.5 9.3 %collective-permute-done.33 = bf16[4,64,1024]{2,1,0:T(8,128)(2,1)S(1)} collective-permute-done((bf16[4,64,1024]{2,1,0:T(8,128)(2,1)S(1)}, bf16[4,64,1024]{2,1,0:T(8,128)(2,1)S(1)}, u32[]{:S(2)}, u32[]{:S(2)}) %collective-permute-start.33) | collective-permute-done | bytes 524320 | tf_op jit(solution)/shard_map/ppermute | solution.py:474
  850.7 2.9 collective-permute-start.36
  853.6 7.9 collective-permute-done.43
  864.9 2.5 bitcast_convert_fusion.1
  871.1 2.5 slice.186
  (343 shorter events, 113.6 us)
Async XLA Ops:
  7.2 203.5 %copy-start = (s32[4,512,8]{1,2,0:T(8,128)S(1)}, s32[4,512,8]{1,2,0:T(8,128)}, u32[]{:S(2)}) copy-start(s32[4,512,8]{1,2,0:T(8,128)} %param.10) | copy-start | bytes 196612
  7.2 82.1 %all-gather.12.cloned.1.call-start = ((), (), s32[]{:S(2)}) async-start(), calls=%async_computation.9 | async-start | bytes 5406720 | tf_op jit(solution)/shard_map/all_gather | solution.py:543
  9.7 177.1 %all-gather.20.cloned.1.call-start = ((), (), s32[]{:S(2)}) async-start(), calls=%async_computation.18 | async-start | bytes 3932160 | tf_op jit(solution)/shard_map/all_gather | solution.py:584
  13.4 204.2 %all-gather.22.cloned.1.call-start = ((), (), s32[]{:S(2)}) async-start(), calls=%async_computation.19 | async-start | bytes 3932160 | tf_op jit(solution)/shard_map/all_gather | solution.py:584
  14.2 301.1 %all-gather.18.cloned.1.call-start = ((), (), s32[]{:S(2)}) async-start(), calls=%async_computation.17 | async-start | bytes 3932160 | tf_op jit(solution)/shard_map/all_gather | solution.py:584
  14.4 8.3 collective-permute-start.4
  19.5 10.0 %collective-permute-start.5 = (bf16[48,1024]{1,0:T(8,128)(2,1)S(1)}, bf16[48,1024]{1,0:T(8,128)(2,1)S(1)}, u32[]{:S(2)}, u32[]{:S(2)}) collective-permute-start(bf16[48,1024]{1,0:T(8,128)(2,1)S(1)} %reshape.483), channel_id=1, source_target_pairs={{0,16},{8,24},{16,0},{24,8},{1,17},{9,25},{17,1},{25,9},{2,18},{10... | collective-permute-start | bytes 294920 | tf_op jit(solution)/shard_map/ppermute | solution.py:447
  19.5 10.0 %collective-permute-start.6 = (bf16[48,1024]{1,0:T(8,128)(2,1)S(1)}, bf16[48,1024]{1,0:T(8,128)(2,1)S(1)}, u32[]{:S(2)}, u32[]{:S(2)}) collective-permute-start(bf16[48,1024]{1,0:T(8,128)(2,1)S(1)} %reshape.483), channel_id=1, source_target_pairs={{0,8},{8,16},{16,24},{24,0},{1,9},{9,17},{17,25},{25,1},{2,10},{10... | collective-permute-start | bytes 294920 | tf_op jit(solution)/shard_map/ppermute | solution.py:447
  20.5 30.0 %collective-permute-start.1 = (bf16[512,1024]{1,0:T(8,128)(2,1)S(1)}, bf16[512,1024]{1,0:T(8,128)(2,1)}, u32[]{:S(2)}, u32[]{:S(2)}) collective-permute-start(bf16[512,1024]{1,0:T(8,128)(2,1)S(1)} %bitcast.272), channel_id=1, source_target_pairs={{0,2},{1,3},{2,0},{3,1},{4,6},{5,7},{6,4},{7,5},{8,10},{9,11},{10,... | collective-permute-start | bytes 3145736 | tf_op jit(solution)/shard_map/ppermute | solution.py:420
  22.0 43.8 %collective-permute-start = (bf16[512,1024]{1,0:T(8,128)(2,1)S(1)}, bf16[512,1024]{1,0:T(8,128)(2,1)}, u32[]{:S(2)}, u32[]{:S(2)}) collective-permute-start(bf16[512,1024]{1,0:T(8,128)(2,1)S(1)} %bitcast.273), channel_id=1, source_target_pairs={{0,1},{1,0},{2,3},{3,2},{4,5},{5,4},{6,7},{7,6},{8,9},{9,8},{10,11... | collective-permute-start | bytes 3145736 | tf_op jit(solution)/shard_map/ppermute | solution.py:421
  22.5 79.0 %copy-start.35 = (f32[512,32]{0,1:T(8,128)}, f32[512,32]{0,1:T(8,128)S(1)}, u32[]{:S(2)}) copy-start(f32[512,32]{0,1:T(8,128)S(1)} %get-tuple-element.106) | copy-start | bytes 196612
  22.5 79.0 %copy-start.37 = (f32[512,32]{0,1:T(8,128)}, f32[512,32]{0,1:T(8,128)S(1)}, u32[]{:S(2)}) copy-start(f32[512,32]{0,1:T(8,128)S(1)} %get-tuple-element.107) | copy-start | bytes 196612
  22.7 66.6 %collective-permute-start.3 = (bf16[8,3,128,128]{3,2,1,0:T(8,128)(2,1)}, bf16[8,3,128,128]{3,2,1,0:T(8,128)(2,1)}, u32[]{:S(2)}, u32[]{:S(2)}) collective-permute-start(bf16[8,3,128,128]{3,2,1,0:T(8,128)(2,1)} %get-tuple-element.93), channel_id=1, source_target_pairs={{0,4},{4,0},{1,5},{5,1},{2,6},{6,2},{3,7},{7,3},{8,12},{12,8},{9,1... | collective-permute-start | bytes 2359304 | tf_op jit(solution)/shard_map/ppermute | solution.py:549
  50.5 15.3 %collective-permute-start.2 = (bf16[512,1024]{1,0:T(8,128)(2,1)}, bf16[512,1024]{1,0:T(8,128)(2,1)}, u32[]{:S(2)}, u32[]{:S(2)}) collective-permute-start(bf16[512,1024]{1,0:T(8,128)(2,1)} %collective-permute-done.1), channel_id=1, source_target_pairs={{0,1},{1,0},{2,3},{3,2},{4,5},{5,4},{6,7},{7,6},{8,9},{9,8},{10,11... | collective-permute-start | bytes 3145736 | tf_op jit(solution)/shard_map/ppermute | solution.py:422
  51.5 11.6 %collective-permute-start.7 = (bf16[4,48,1024]{2,1,0:T(8,128)(2,1)S(1)}, bf16[4,48,1024]{2,1,0:T(8,128)(2,1)S(1)}, u32[]{:S(2)}, u32[]{:S(2)}) collective-permute-start(bf16[4,48,1024]{2,1,0:T(8,128)(2,1)S(1)} %constant_dynamic-slice_fusion.4), channel_id=1, source_target_pairs={{0,4},{4,0},{1,5},{5,1},{2,6},{6,2},{3,7},{7,3},{8,12},{12,8},{9,1... | collective-permute-start | bytes 1179656 | tf_op jit(solution)/shard_map/ppermute | solution.py:447
  54.4 54.5 %copy-start.17 = (bf16[1,4,48,1024]{3,2,0,1:T(8,128)(2,1)}, bf16[1,4,48,1024]{3,2,0,1:T(8,128)(2,1)S(1)}, u32[]{:S(2)}) copy-start(bf16[1,4,48,1024]{3,2,0,1:T(8,128)(2,1)S(1)} %fusion.87) | copy-start | bytes 1179652
  63.0 45.9 %copy-start.28 = (bf16[4,48,1024]{2,1,0:T(8,128)(2,1)}, bf16[4,48,1024]{2,1,0:T(8,128)(2,1)S(1)}, u32[]{:S(2)}) copy-start(bf16[4,48,1024]{2,1,0:T(8,128)(2,1)S(1)} %collective-permute-done.7) | copy-start | bytes 1179652
  64.3 45.0 %collective-permute-start.8 = (bf16[2,4,48,1024]{3,2,0,1:T(8,128)(2,1)}, bf16[2,4,48,1024]{3,2,0,1:T(8,128)(2,1)}, u32[]{:S(2)}, u32[]{:S(2)}) collective-permute-start(bf16[2,4,48,1024]{3,2,0,1:T(8,128)(2,1)} %fusion.26), channel_id=1, source_target_pairs={{0,2},{1,3},{2,0},{3,1},{4,6},{5,7},{6,4},{7,5},{8,10},{9,11},{10,... | collective-permute-start | bytes 2359304 | tf_op jit(solution)/shard_map/ppermute | solution.py:455
  104.6 29.3 %all-to-all-start = ((bf16[1,512,8,256]{3,1,0,2:T(8,128)(2,1)}), bf16[1,512,8,256]{3,1,0,2:T(8,128)(2,1)S(1)}, u32[]{:S(2)}, u32[]{:S(2)}) async-start(bf16[1,512,8,256]{3,1,0,2:T(8,128)(2,1)} %copy.80), calls=%async_computation | async-start | bytes 4194304 | tf_op jit(solution)/shard_map/all_to_all | solution.py:609
  108.4 346.8 %all-gather.14.cloned.1.call-start = ((), (), s32[]{:S(2)}) async-start(), calls=%async_computation.15 | async-start | bytes 3932160 | tf_op jit(solution)/shard_map/all_gather | solution.py:584
  112.2 55.0 %collective-permute-start.9 = (bf16[2,2,4,48,1024]{4,3,1,2,0:T(8,128)(2,1)}, bf16[2,2,4,48,1024]{4,3,1,2,0:T(8,128)(2,1)}, u32[]{:S(2)}, u32[]{:S(2)}) collective-permute-start(bf16[2,2,4,48,1024]{4,3,1,2,0:T(8,128)(2,1)} %maximum_select_fusion.1), channel_id=1, source_target_pairs={{0,1},{1,0},{2,3},{3,2},{4,5},{5,4},{6,7},{7,6},{8,9},{9,8},{10,11... | collective-permute-start | bytes 4718600 | tf_op jit(solution)/shard_map/ppermute | solution.py:455
  160.5 18.3 %all-to-all-start.1 = ((bf16[1,1024,4,128]{3,2,0,1:T(4,128)(2,1)}), bf16[1,1024,4,128]{3,2,0,1:T(4,128)(2,1)}, u32[]{:S(2)}, u32[]{:S(2)}) async-start(bf16[1,1024,4,128]{3,2,0,1:T(4,128)(2,1)} %bitcast.264), calls=%async_computation.1 | async-start | bytes 2097152 | tf_op jit(solution)/shard_map/all_to_all | solution.py:613
  165.1 290.1 %all-gather.16.cloned.1.call-start = ((), (), s32[]{:S(2)}) async-start(), calls=%async_computation.16 | async-start | bytes 3932160 | tf_op jit(solution)/shard_map/all_gather | solution.py:586
  186.7 23.9 %collective-permute-start.11 = (bf16[512,1024]{1,0:T(8,128)(2,1)S(1)}, bf16[512,1024]{1,0:T(8,128)(2,1)}, u32[]{:S(2)}, u32[]{:S(2)}) collective-permute-start(bf16[512,1024]{1,0:T(8,128)(2,1)S(1)} %multiply_convert_fusion), channel_id=1, source_target_pairs={{0,2},{1,3},{2,0},{3,1},{4,6},{5,7},{6,4},{7,5},{8,10},{9,11},{10,... | collective-permute-start | bytes 3145736 | tf_op jit(solution)/shard_map/ppermute | solution.py:420
  186.8 71.4 %collective-permute-start.13 = (bf16[4,8,3,128,128]{4,3,2,1,0:T(8,128)(2,1)}, bf16[4,8,3,128,128]{4,3,2,1,0:T(8,128)(2,1)}, u32[]{:S(2)}, u32[]{:S(2)}) collective-permute-start(bf16[4,8,3,128,128]{4,3,2,1,0:T(8,128)(2,1)} %bitcast.302), channel_id=1, source_target_pairs={{0,4},{4,0},{1,5},{5,1},{2,6},{6,2},{3,7},{7,3},{8,12},{12,8},{9,1... | collective-permute-start | bytes 9437192 | tf_op jit(solution)/shard_map/ppermute | solution.py:650
  187.2 31.5 %collective-permute-start.10 = (bf16[512,1024]{1,0:T(8,128)(2,1)S(1)}, bf16[512,1024]{1,0:T(8,128)(2,1)}, u32[]{:S(2)}, u32[]{:S(2)}) collective-permute-start(bf16[512,1024]{1,0:T(8,128)(2,1)S(1)} %multiply_convert_fusion), channel_id=1, source_target_pairs={{0,1},{1,0},{2,3},{3,2},{4,5},{5,4},{6,7},{7,6},{8,9},{9,8},{10,11... | collective-permute-start | bytes 3145736 | tf_op jit(solution)/shard_map/ppermute | solution.py:421
  210.6 8.1 collective-permute-start.12
  217.7 107.9 %collective-permute-start.15 = (bf16[4,8,3,128,128]{4,3,2,1,0:T(8,128)(2,1)}, bf16[4,8,3,128,128]{4,3,2,1,0:T(8,128)(2,1)}, u32[]{:S(2)}, u32[]{:S(2)}) collective-permute-start(bf16[4,8,3,128,128]{4,3,2,1,0:T(8,128)(2,1)} %bitcast.300), channel_id=1, source_target_pairs={{0,4},{4,0},{1,5},{5,1},{2,6},{6,2},{3,7},{7,3},{8,12},{12,8},{9,1... | collective-permute-start | bytes 9437192 | tf_op jit(solution)/shard_map/ppermute | solution.py:650
  218.4 616.3 %reduce-scatter.14.cloned.1.call-start = ((), (), s32[]{:S(2)}) async-start(), calls=%async_computation.14 | async-start | bytes 3932160 | tf_op jit(solution)/shard_map/reduce_scatter | solution.py:693
  315.3 77.7 %collective-permute-start.14 = (bf16[4,8,3,128,128]{4,3,2,1,0:T(8,128)(2,1)}, bf16[4,8,3,128,128]{4,3,2,1,0:T(8,128)(2,1)}, u32[]{:S(2)}, u32[]{:S(2)}) collective-permute-start(bf16[4,8,3,128,128]{4,3,2,1,0:T(8,128)(2,1)} %shard_map.156.refs_0_), channel_id=1, source_target_pairs={{0,4},{4,0},{1,5},{5,1},{2,6},{6,2},{3,7},{7,3},{8,12},{12,8},{9,1... | collective-permute-start | bytes 9437192 | tf_op jit(solution)/shard_map/ppermute | solution.py:650
  387.6 70.5 %collective-permute-start.16 = (bf16[4,8,3,128,128]{4,3,2,1,0:T(8,128)(2,1)}, bf16[4,8,3,128,128]{4,3,2,1,0:T(8,128)(2,1)}, u32[]{:S(2)}, u32[]{:S(2)}) collective-permute-start(bf16[4,8,3,128,128]{4,3,2,1,0:T(8,128)(2,1)} %shard_map.159), channel_id=1, source_target_pairs={{0,4},{4,0},{1,5},{5,1},{2,6},{6,2},{3,7},{7,3},{8,12},{12,8},{9,1... | collective-permute-start | bytes 9437192 | tf_op jit(solution)/shard_map/ppermute | solution.py:654
  520.1 316.9 %reduce-scatter.6.cloned.1.call-start = ((), (), s32[]{:S(2)}) async-start(), calls=%async_computation.10 | async-start | bytes 3932160 | tf_op jit(solution)/shard_map/reduce_scatter | solution.py:725
  526.6 326.9 %reduce-scatter.12.cloned.1.call-start = ((), (), s32[]{:S(2)}) async-start(), calls=%async_computation.13 | async-start | bytes 3932160 | tf_op jit(solution)/shard_map/reduce_scatter | solution.py:693
  527.4 337.5 %reduce-scatter.8.cloned.1.call-start = ((), (), s32[]{:S(2)}) async-start(), calls=%async_computation.11 | async-start | bytes 3932160 | tf_op jit(solution)/shard_map/reduce_scatter | solution.py:725
  553.5 5.7 collective-permute-start.21
  553.5 70.8 %collective-permute-start.23 = (bf16[4,8,3,128,128]{4,3,2,1,0:T(8,128)(2,1)}, bf16[4,8,3,128,128]{4,3,2,1,0:T(8,128)(2,1)}, u32[]{:S(2)}, u32[]{:S(2)}) collective-permute-start(bf16[4,8,3,128,128]{4,3,2,1,0:T(8,128)(2,1)} %shard_map.161), channel_id=1, source_target_pairs={{0,4},{4,0},{1,5},{5,1},{2,6},{6,2},{3,7},{7,3},{8,12},{12,8},{9,1... | collective-permute-start | bytes 9437192 | tf_op jit(solution)/shard_map/ppermute | solution.py:654
  558.7 4.9 collective-permute-start.18
  559.0 7.2 collective-permute-start.20
  561.9 26.1 %collective-permute-start.22 = (bf16[512,1024]{1,0:T(8,128)(2,1)S(1)}, bf16[512,1024]{1,0:T(8,128)(2,1)S(1)}, u32[]{:S(2)}, u32[]{:S(2)}) collective-permute-start(bf16[512,1024]{1,0:T(8,128)(2,1)S(1)} %fusion.15), channel_id=1, source_target_pairs={{0,2},{1,3},{2,0},{3,1},{4,6},{5,7},{6,4},{7,5},{8,10},{9,11},{10,... | collective-permute-start | bytes 3145736 | tf_op jit(solution)/shard_map/ppermute | solution.py:435
  563.6 25.3 %collective-permute-start.17 = (bf16[512,1024]{1,0:T(8,128)(2,1)S(1)}, bf16[512,1024]{1,0:T(8,128)(2,1)S(1)}, u32[]{:S(2)}, u32[]{:S(2)}) collective-permute-start(bf16[512,1024]{1,0:T(8,128)(2,1)S(1)} %get-tuple-element.90), channel_id=1, source_target_pairs={{0,1},{1,0},{2,3},{3,2},{4,5},{5,4},{6,7},{7,6},{8,9},{9,8},{10,11... | collective-permute-start | bytes 3145736 | tf_op jit(solution)/shard_map/ppermute | solution.py:430
  565.7 44.0 %collective-permute-start.19 = (bf16[512,1024]{1,0:T(8,128)(2,1)S(1)}, bf16[512,1024]{1,0:T(8,128)(2,1)S(1)}, u32[]{:S(2)}, u32[]{:S(2)}) collective-permute-start(bf16[512,1024]{1,0:T(8,128)(2,1)S(1)} %add_convert_fusion.4), channel_id=1, source_target_pairs={{0,2},{1,3},{2,0},{3,1},{4,6},{5,7},{6,4},{7,5},{8,10},{9,11},{10,... | collective-permute-start | bytes 3145736 | tf_op jit(solution)/shard_map/ppermute | solution.py:435
  630.8 115.2 %collective-permute-start.24 = (bf16[4,8,3,128,128]{4,3,2,1,0:T(8,128)(2,1)}, bf16[4,8,3,128,128]{4,3,2,1,0:T(8,128)(2,1)}, u32[]{:S(2)}, u32[]{:S(2)}) collective-permute-start(bf16[4,8,3,128,128]{4,3,2,1,0:T(8,128)(2,1)} %shard_map.164), channel_id=1, source_target_pairs={{0,4},{4,0},{1,5},{5,1},{2,6},{6,2},{3,7},{7,3},{8,12},{12,8},{9,1... | collective-permute-start | bytes 9437192 | tf_op jit(solution)/shard_map/ppermute | solution.py:654
  636.3 75.8 %all-to-all-start.2 = ((bf16[1,512,8,128]{3,1,0,2:T(8,128)(2,1)}), bf16[1,512,8,128]{3,1,0,2:T(8,128)(2,1)S(1)}, u32[]{:S(2)}, u32[]{:S(2)}) async-start(bf16[1,512,8,128]{3,1,0,2:T(8,128)(2,1)} %copy.91), calls=%async_computation.2 | async-start | bytes 2097152 | tf_op jit(solution)/shard_map/all_to_all | solution.py:717
  644.9 117.8 %collective-permute-start.37 = (bf16[4,2,2,32,1024]{4,3,2,1,0:T(8,128)(2,1)}, bf16[4,2,2,32,1024]{4,3,2,1,0:T(8,128)(2,1)}, u32[]{:S(2)}, u32[]{:S(2)}) collective-permute-start(bf16[4,2,2,32,1024]{4,3,2,1,0:T(8,128)(2,1)} %dynamic-slice_bitcast_fusion.1), channel_id=1, source_target_pairs={{0,1},{1,0},{2,3},{3,2},{4,5},{5,4},{6,7},{7,6},{8,9},{9,8},{10,11... | collective-permute-start | bytes 3145736 | tf_op jit(solution)/shard_map/ppermute | solution.py:482
  746.0 28.3 %all-to-all-start.3 = ((bf16[1,1024,4,256]{3,2,0,1:T(4,128)(2,1)}), bf16[1,1024,4,256]{3,2,0,1:T(4,128)(2,1)S(1)}, u32[]{:S(2)}, u32[]{:S(2)}) async-start(bf16[1,1024,4,256]{3,2,0,1:T(4,128)(2,1)} %bitcast.243), calls=%async_computation.3 | async-start | bytes 4194304 | tf_op jit(solution)/shard_map/all_to_all | solution.py:729
  749.9 117.4 %reduce-scatter.10.cloned.1.call-start = ((), (), s32[]{:S(2)}) async-start(), calls=%async_computation.12 | async-start | bytes 3932160 | tf_op jit(solution)/shard_map/reduce_scatter | solution.py:725
  766.2 26.4 %collective-permute-start.38 = (bf16[4,2,32,1024]{3,2,1,0:T(8,128)(2,1)}, bf16[4,2,32,1024]{3,2,1,0:T(8,128)(2,1)}, u32[]{:S(2)}, u32[]{:S(2)}) collective-permute-start(bf16[4,2,32,1024]{3,2,1,0:T(8,128)(2,1)} %fusion.30), channel_id=1, source_target_pairs={{0,2},{1,3},{2,0},{3,1},{4,6},{5,7},{6,4},{7,5},{8,10},{9,11},{10,... | collective-permute-start | bytes 1572872 | tf_op jit(solution)/shard_map/ppermute | solution.py:482
  787.0 13.3 %collective-permute-start.31 = (bf16[4,2,2,64,1024]{4,3,2,1,0:T(8,128)(2,1)}, bf16[4,2,2,64,1024]{4,3,2,1,0:T(8,128)(2,1)}, u32[]{:S(2)}, u32[]{:S(2)}) collective-permute-start(bf16[4,2,2,64,1024]{4,3,2,1,0:T(8,128)(2,1)} %dynamic-slice_bitcast_fusion), channel_id=1, source_target_pairs={{0,1},{1,0},{2,3},{3,2},{4,5},{5,4},{6,7},{7,6},{8,9},{9,8},{10,11... | collective-permute-start | bytes 6291464 | tf_op jit(solution)/shard_map/ppermute | solution.py:482
  792.5 1.9 collective-permute-start.25
  794.1 17.7 %collective-permute-start.39 = (bf16[4,32,1024]{2,1,0:T(8,128)(2,1)S(1)}, bf16[4,32,1024]{2,1,0:T(8,128)(2,1)S(1)}, u32[]{:S(2)}, u32[]{:S(2)}) collective-permute-start(bf16[4,32,1024]{2,1,0:T(8,128)(2,1)S(1)} %fusion.36), channel_id=1, source_target_pairs={{0,4},{4,0},{1,5},{5,1},{2,6},{6,2},{3,7},{7,3},{8,12},{12,8},{9,1... | collective-permute-start | bytes 786440 | tf_op jit(solution)/shard_map/ppermute | solution.py:474
  794.5 4.0 collective-permute-start.26
  798.5 8.2 collective-permute-start.27
  803.1 24.1 %collective-permute-start.32 = (bf16[4,2,64,1024]{3,2,1,0:T(8,128)(2,1)S(1)}, bf16[4,2,64,1024]{3,2,1,0:T(8,128)(2,1)S(1)}, u32[]{:S(2)}, u32[]{:S(2)}) collective-permute-start(bf16[4,2,64,1024]{3,2,1,0:T(8,128)(2,1)S(1)} %fusion.19), channel_id=1, source_target_pairs={{0,2},{1,3},{2,0},{3,1},{4,6},{5,7},{6,4},{7,5},{8,10},{9,11},{10,... | collective-permute-start | bytes 3145736 | tf_op jit(solution)/shard_map/ppermute | solution.py:482
  806.7 24.2 %collective-permute-start.28 = (bf16[16,128]{1,0:T(8,128)(2,1)S(1)}, bf16[16,128]{1,0:T(8,128)(2,1)S(1)}, u32[]{:S(2)}, u32[]{:S(2)}) collective-permute-start(bf16[16,128]{1,0:T(8,128)(2,1)S(1)} %get-tuple-element.103), channel_id=1, source_target_pairs={{0,8},{8,16},{16,24},{24,0},{1,9},{9,17},{17,25},{25,1},{2,10},{10... | collective-permute-start | bytes 12296 | tf_op jit(solution)/shard_map/ppermute | solution.py:474
  808.3 24.7 %collective-permute-start.29 = (bf16[16,128]{1,0:T(8,128)(2,1)S(1)}, bf16[16,128]{1,0:T(8,128)(2,1)S(1)}, u32[]{:S(2)}, u32[]{:S(2)}) collective-permute-start(bf16[16,128]{1,0:T(8,128)(2,1)S(1)} %get-tuple-element.105), channel_id=1, source_target_pairs={{0,16},{8,24},{16,0},{24,8},{1,17},{9,25},{17,1},{25,9},{2,18},{10... | collective-permute-start | bytes 12296 | tf_op jit(solution)/shard_map/ppermute | solution.py:474
  808.9 24.5 %collective-permute-start.30 = (bf16[16,128]{1,0:T(8,128)(2,1)S(1)}, bf16[16,128]{1,0:T(8,128)(2,1)S(1)}, u32[]{:S(2)}, u32[]{:S(2)}) collective-permute-start(bf16[16,128]{1,0:T(8,128)(2,1)S(1)} %get-tuple-element.104), channel_id=1, source_target_pairs={{0,24},{8,0},{16,8},{24,16},{1,25},{9,1},{17,9},{25,17},{2,26},{10... | collective-permute-start | bytes 12296 | tf_op jit(solution)/shard_map/ppermute | solution.py:474
  811.8 24.5 %collective-permute-start.40 = (bf16[32,1024]{1,0:T(8,128)(2,1)S(1)}, bf16[32,1024]{1,0:T(8,128)(2,1)S(1)}, u32[]{:S(2)}, u32[]{:S(2)}) collective-permute-start(bf16[32,1024]{1,0:T(8,128)(2,1)S(1)} %get-tuple-element.100), channel_id=1, source_target_pairs={{0,8},{8,16},{16,24},{24,0},{1,9},{9,17},{17,25},{25,1},{2,10},{10... | collective-permute-start | bytes 196616 | tf_op jit(solution)/shard_map/ppermute | solution.py:474
  827.2 9.1 %collective-permute-start.41 = (bf16[32,1024]{1,0:T(8,128)(2,1)S(1)}, bf16[32,1024]{1,0:T(8,128)(2,1)S(1)}, u32[]{:S(2)}, u32[]{:S(2)}) collective-permute-start(bf16[32,1024]{1,0:T(8,128)(2,1)S(1)} %get-tuple-element.102), channel_id=1, source_target_pairs={{0,16},{8,24},{16,0},{24,8},{1,17},{9,25},{17,1},{25,9},{2,18},{10... | collective-permute-start | bytes 196616 | tf_op jit(solution)/shard_map/ppermute | solution.py:474
  830.9 5.4 collective-permute-start.42
  833.0 14.9 %collective-permute-start.33 = (bf16[4,64,1024]{2,1,0:T(8,128)(2,1)S(1)}, bf16[4,64,1024]{2,1,0:T(8,128)(2,1)S(1)}, u32[]{:S(2)}, u32[]{:S(2)}) collective-permute-start(bf16[4,64,1024]{2,1,0:T(8,128)(2,1)S(1)} %fusion.31), channel_id=1, source_target_pairs={{0,4},{4,0},{1,5},{5,1},{2,6},{6,2},{3,7},{7,3},{8,12},{12,8},{9,1... | collective-permute-start | bytes 1572872 | tf_op jit(solution)/shard_map/ppermute | solution.py:474
  834.7 26.7 %collective-permute-start.43 = (bf16[8,3,128,128]{3,2,1,0:T(8,128)(2,1)}, bf16[8,3,128,128]{3,2,1,0:T(8,128)(2,1)}, u32[]{:S(2)}, u32[]{:S(2)}) collective-permute-start(bf16[8,3,128,128]{3,2,1,0:T(8,128)(2,1)} %bitcast.306), channel_id=1, source_target_pairs={{0,4},{4,0},{1,5},{5,1},{2,6},{6,2},{3,7},{7,3},{8,12},{12,8},{9,1... | collective-permute-start | bytes 2359304 | tf_op jit(solution)/shard_map/ppermute | solution.py:726
  849.8 13.3 %collective-permute-start.34 = (bf16[64,1024]{1,0:T(8,128)(2,1)}, bf16[64,1024]{1,0:T(8,128)(2,1)S(1)}, u32[]{:S(2)}, u32[]{:S(2)}) collective-permute-start(bf16[64,1024]{1,0:T(8,128)(2,1)} %get-tuple-element.97), channel_id=1, source_target_pairs={{0,8},{8,16},{16,24},{24,0},{1,9},{9,17},{17,25},{25,1},{2,10},{10... | collective-permute-start | bytes 393224 | tf_op jit(solution)/shard_map/ppermute | solution.py:474
  849.8 13.3 %collective-permute-start.35 = (bf16[64,1024]{1,0:T(8,128)(2,1)}, bf16[64,1024]{1,0:T(8,128)(2,1)S(1)}, u32[]{:S(2)}, u32[]{:S(2)}) collective-permute-start(bf16[64,1024]{1,0:T(8,128)(2,1)} %get-tuple-element.99), channel_id=1, source_target_pairs={{0,16},{8,24},{16,0},{24,8},{1,17},{9,25},{17,1},{25,9},{2,18},{10... | collective-permute-start | bytes 393224 | tf_op jit(solution)/shard_map/ppermute | solution.py:474
  850.7 12.3 %collective-permute-start.36 = (bf16[64,1024]{1,0:T(8,128)(2,1)}, bf16[64,1024]{1,0:T(8,128)(2,1)}, u32[]{:S(2)}, u32[]{:S(2)}) collective-permute-start(bf16[64,1024]{1,0:T(8,128)(2,1)} %get-tuple-element.98), channel_id=1, source_target_pairs={{0,24},{8,0},{16,8},{24,16},{1,25},{9,1},{17,9},{25,17},{2,26},{10... | collective-permute-start | bytes 393224 | tf_op jit(solution)/shard_map/ppermute | solution.py:474
  (50 other events, 432.5 us)
Sparse Core Ops, SparseCore 0:
  11.5 77.7 all-gather.11
  90.9 62.1 all-gather.19
  154.6 62.1 all-gather.21
  218.2 62.1 all-gather.17
  281.8 62.1 all-gather.13
  345.4 62.1 all-gather.15
  520.3 59.0 reduce-scatter.13
  581.6 60.2 reduce-scatter.5
  644.3 60.2 reduce-scatter.11
  706.7 60.2 reduce-scatter.7
  769.4 61.8 reduce-scatter.9

commit v4 on v3

--- a/solution.py
+++ b/solution.py
@@ -650,7 +650,7 @@
         expert_pieces[chunk].append(lax.ppermute(near, "ctx", swap_pairs(2, 1)))
 
     def cross(chunk):
-        held = after(far_sums[chunk], marks[chunk + 1])
+        held = after(far_sums[chunk], marks[chunk + 1]) if chunk > 1 else far_sums[chunk]
         arrivals.append(lax.ppermute(held, "ctx", swap_pairs(2, 1)))
 
     if paired:
@@ -679,7 +679,7 @@
             own_sums.append(grad_pieces[0])
             far_sums.append(grad_pieces[1])
             if chunk == 1:
-                cross(0)
+                cross(1)
             elif chunk == CHUNKS - 1:
                 arrivals[0] = grad_pieces[2]
         else:
@@ -687,20 +687,22 @@
                 lax.psum_scatter(grad_pieces[0], ("fsdp", "ctx"), scatter_dimension=0)
             )
     if paired:
-        for chunk in range(1, CHUNKS - 1):
-            cross(chunk)
-        last_sums = [
-            lax.psum_scatter(part, "fsdp", scatter_dimension=0)
-            for part in (far_sums[-1], own_sums[-1])
-        ]
+        cross(2)
+        first_sums, last_sums = (
+            [
+                by_rows(lax.psum_scatter(part, "fsdp", scatter_dimension=0))
+                for part in (far_sums[chunk], own_sums[chunk])
+            ]
+            for chunk in (0, CHUNKS - 1)
+        )
     grad_chances = choice_total[:, :EXPERTS] * chosen_any
     grad_logits = chances * (grad_chances - jnp.sum(grad_chances * chances, axis=-1, keepdims=True))
     router_rows = router_full.astype(jnp.float32)
     grad_router = jnp.dot(grad_logits.T, group_rows.astype(jnp.float32), precision=HIGH)
     back_group = by_rows(totals[1] + jnp.dot(grad_logits, router_rows, precision=HIGH))
+    if paired:
+        back_group, *first_sums = together(back_group, *first_sums)
     grad_second = by_rows(scatter_group(back_group))
-    moe_rows = by_rows(scatter_group(totals[0]))
-    output = (hidden + moe_rows).astype(jnp.bfloat16).reshape(tokens.shape)
     grad_gain_second = jnp.sum(grad_second * normed_second, axis=0)
     grad_hidden = cotangent.astype(jnp.float32).reshape(row_count, model_width) + rms_back(
         grad_second, normed_second, inverse_second, gain_rows[1]
@@ -708,6 +710,8 @@
     grad_attn = by_rows(grad_hidden.astype(jnp.bfloat16))
     if paired:
         grad_attn, arrivals[1] = together(grad_attn, arrivals[1])
+    moe_rows = by_rows(scatter_group(after(totals[0], grad_attn)))
+    output = (hidden + moe_rows).astype(jnp.bfloat16).reshape(tokens.shape)
     grad_output_weight = transposed_times(grad_attn, merged)
     grad_merged = (
         jnp.dot(grad_attn, output_full, preferred_element_type=jnp.float32)
@@ -719,12 +723,13 @@
         head_rows, grad_heads.reshape(local_seqs, length, -1), log_totals
     ).reshape(local_seqs, length, local_groups, 4 * head_size)
     if paired:
-        grad_head_rows, arrivals[2] = together(grad_head_rows, arrivals[2])
-        for own, arrived in zip(own_sums, arrivals):
+        for own, arrived in zip(own_sums[1:-1], arrivals):
             joined = (own.astype(jnp.float32) + arrived.astype(jnp.float32)).astype(jnp.bfloat16)
             chunk_sums.append(lax.psum_scatter(joined, "fsdp", scatter_dimension=0))
-        far = lax.ppermute(last_sums[0], "ctx", swap_pairs(2, 1))
-        chunk_sums.append(last_sums[1].astype(jnp.float32) + far.astype(jnp.float32))
+        for far, own in (first_sums, last_sums):
+            far = lax.ppermute(far, "ctx", swap_pairs(2, 1))
+            chunk_sums.append(own.astype(jnp.float32) + far.astype(jnp.float32))
+        chunk_sums = [chunk_sums[2], chunk_sums[0], chunk_sums[1], chunk_sums[3]]
     grad_turned = (
         lax.all_to_all(grad_head_rows, "ctx", split_axis=1, concat_axis=2, tiled=True)
         .astype(jnp.float32)
@@ -764,7 +769,6 @@
     small_rows = -(-small_count // (16 * LANES)) * 16
     small = jnp.pad(small, ((0, 0), (0, small_rows * LANES - small_count)))
     small_sum = scatter_dense(small.reshape(device_count, small_rows, LANES)).reshape(-1)
-    expert_sums = jnp.concatenate([part.astype(jnp.float32) for part in chunk_sums], axis=0)
     return (
         output,
         grad_inputs.reshape(tokens.shape),
@@ -772,8 +776,8 @@
         inward_sum,
         output_sum,
         small_sum[:router_count].reshape(router_weight.shape),
-        expert_sums[:, :2],
-        expert_sums[:, 2],
+        jnp.concatenate([part[:, :2].astype(jnp.float32) for part in chunk_sums], axis=0),
+        jnp.concatenate([part[:, 2].astype(jnp.float32) for part in chunk_sums], axis=0),
     )
 
 

time: 888 us -> 860 us (0.968)
  waiting for transfers between devices: 303 us -> 247 us
  local copies, waits for them, and re-layouts: 86.4 us -> 96.4 us
  other arithmetic: 95 us -> 104 us
  starting transfers between devices: 58.2 us -> 67.2 us
    all_to_all x1, waiting for transfers between devices: 67.1 us -> 0.01 us  [per_device(): lax.all_to_all(by_rows(grad_merged), 'ctx', split_axis=2, concat_axis=1,...]
    ppermute x1 -> x2, waiting for transfers between devices: 7.85 us -> 69 us  [per_device(): far = lax.ppermute(far, 'ctx', swap_pairs(2, 1))]
    ppermute x2, waiting for transfers between devices: 42.6 us -> 0.01 us  [scatter_group(): lax.ppermute((parts[2] + first).astype(jnp.bfloat16), 'tp', swap_pairs(co...]
    add x1 -> x3, other arithmetic: 1.59 us -> 15.1 us  [the longest x1 12.2 us: per_device(): totals[1] + jnp.dot(grad_logits, router_rows, precision=HIGH)]
    ppermute x3 -> x2, waiting for transfers between devices: 13.5 us -> 2.83 us  [cross(): arrivals.append(lax.ppermute(held, 'ctx', swap_pairs(2, 1)))]
    another operation x4, other arithmetic: 19.1 us -> 9.25 us
    convert_element_type x3 -> x2, other arithmetic: 19.2 us -> 11.4 us  [per_device(): (own.astype(jnp.float32) + arrived.astype(jnp.float32)).astype(jnp.bfloat16)]
    unnamed x124 -> x137, local copies, waits for them, and re-layouts: 17 us -> 21.6 us
  transfers between devices with their start and end apart: 59 -> 60, of which waited for: 21 -> 21; matrix products, arithmetic and copies ran while one was open for 22% -> 25% of each run, Pallas kernels for 25% -> 34%
where the time goes in v4:
time: 860 us; the launch traced here: 852 us
  Pallas kernels  286 us (33%)
  waiting for transfers between devices  247 us (29%)
  other arithmetic  104 us (12%)
  local copies, waits for them, and re-layouts  96.4 us (11%)
  starting transfers between devices  67.2 us (8%)
  matrix products  35.7 us (4%)
  between operations  16 us (2%)
    pallas_call x4, Pallas kernels, expert_pass(): pl.pallas_call(functools.partial(expert_kernel, first, steps, base_expert...  243 us
    ppermute x2, waiting for transfers between devices, per_device(): far = lax.ppermute(far, 'ctx', swap_pairs(2, 1))  69 us
    ppermute x2, waiting for transfers between devices, gather_group(): across = lax.ppermute(rows, 'tp', swap_pairs(count, 2))  46.4 us
    ppermute x3, waiting for transfers between devices, fetch(): expert_pieces[chunk].append(lax.ppermute(near, 'ctx', swap_pairs(2, 1)))  34.1 us
    pallas_call x1, Pallas kernels, attend(): pl.pallas_call(functools.partial(attend_back_kernel, block), grid=(sequen...  24.9 us
    ppermute x12, starting transfers between devices, scatter_axis(): lax.ppermute(sent, name, shifted(count, step)).astype(jnp.float32)  23.2 us
    unnamed x137, local copies, waits for them, and re-layouts  21.6 us
    all_to_all x1, waiting for transfers between devices, per_device(): lax.all_to_all(sent_heads, 'ctx', split_axis=2, concat_axis=1, tiled=True)  21.5 us
  transfers between devices with their start and end apart: 60, of which 21 were waited for; matrix products, arithmetic and copies ran while one was open for 25% of the time, Pallas kernels for 34%

profile of v4, /device:TPU:0, one launch (start us, length us, event | category | flops | bytes accessed | tf_op | source)
XLA Modules:
  0.0 851.9 jit_solution(243099496421195336)
XLA Ops:
  9.8 3.7 pad_maximum_fusion.6
  14.4 3.1 collective-permute-start.6
  17.5 2.6 collective-permute-start.5
  23.4 3.4 collective-permute-done.4
  28.4 23.0 %collective-permute-done.1 = bf16[512,1024]{1,0:T(8,128)(2,1)} collective-permute-done((bf16[512,1024]{1,0:T(8,128)(2,1)S(1)}, bf16[512,1024]{1,0:T(8,128)(2,1)}, u32[]{:S(2)}, u32[]{:S(2)}) %collective-permute-start.1) | collective-permute-done | bytes 1048608 | tf_op jit(solution)/shard_map/ppermute | solution.py:420
  55.3 9.8 %collective-permute-done.7 = bf16[4,48,1024]{2,1,0:T(8,128)(2,1)S(1)} collective-permute-done((bf16[4,48,1024]{2,1,0:T(8,128)(2,1)S(1)}, bf16[4,48,1024]{2,1,0:T(8,128)(2,1)S(1)}, u32[]{:S(2)}, u32[]{:S(2)}) %collective-permute-start.7) | collective-permute-done | bytes 393248 | tf_op jit(solution)/shard_map/ppermute | solution.py:447
  67.7 3.5 pad_maximum_fusion.refs_4_
  71.2 6.5 copy.111
  77.8 10.1 %all-gather.12.cloned.1.call-done.refs_0_ = bf16[32,80,1024]{2,1,0:T(8,128)(2,1)} async-done(((bf16[1,80,1024]{2,1,0:T(8,128)(2,1)}), bf16[32,80,1024]{2,1,0:T(8,128)(2,1)}) %all-gather.12.cloned.1.call-update) | async-done | bytes 5242896 | tf_op jit(solution)/shard_map/all_gather | solution.py:543
  89.2 4.9 slice.144
  94.9 4.7 convolution_bitcast_fusion
  102.8 3.8 all-to-all-start
  107.5 2.8 maximum_select_fusion.1
  110.6 21.5 %all-to-all-done = bf16[1,512,8,256]{3,1,0,2:T(8,128)(2,1)S(1)} async-done(((bf16[1,512,8,256]{3,1,0,2:T(8,128)(2,1)}), bf16[1,512,8,256]{3,1,0,2:T(8,128)(2,1)S(1)}, u32[]{:S(2)}, u32[]{:S(2)}) %all-to-all-start) | async-done | bytes 2097184 | tf_op jit(solution)/shard_map/all_to_all | solution.py:609
  132.1 2.9 copy.113
  135.1 3.2 reshape.474.heads_ref
  138.3 17.9 %shard_map.154 = (bf16[1,1024,512]{2,1,0:T(8,128)(2,1)S(1)}, f32[1,4,1024,2]{3,2,1,0:T(8,128)S(1)}) custom-call(bf16[1,1024,1024]{2,1,0:T(8,128)(2,1)S(1)} %reshape.474.heads_ref), custom_call_target="tpu_custom_call" | custom-call | flops 8589934592 | bytes 8388608 | tf_op jit(solution)/shard_map/pallas_call | solution.py:383
  158.7 4.6 all-to-all-start.1
  169.7 7.3 all-to-all-done.1
  179.7 3.6 multiply_reduce_fusion.2
  185.3 23.4 %collective-permute-done.11 = bf16[512,1024]{1,0:T(8,128)(2,1)} collective-permute-done((bf16[512,1024]{1,0:T(8,128)(2,1)S(1)}, bf16[512,1024]{1,0:T(8,128)(2,1)}, u32[]{:S(2)}, u32[]{:S(2)}) %collective-permute-start.11) | collective-permute-done | bytes 1048608 | tf_op jit(solution)/shard_map/ppermute | solution.py:420
  219.8 3.6 pad_maximum_fusion.1.refs_2_
  223.4 6.6 copy.118
  230.0 3.5 fusion.73
  237.4 19.0 %collective-permute-done.13.refs_1_ = bf16[4,8,3,128,128]{4,3,2,1,0:T(8,128)(2,1)} collective-permute-done((bf16[4,8,3,128,128]{4,3,2,1,0:T(8,128)(2,1)}, bf16[4,8,3,128,128]{4,3,2,1,0:T(8,128)(2,1)}, u32[]{:S(2)}, u32[]{:S(2)}) %collective-permute-start.13) | collective-permute-done | bytes 3145760 | tf_op jit(solution)/shard_map/ppermute | solution.py:650
  256.4 57.1 %shard_map.155 = (f32[2048,1024]{1,0:T(8,128)}, f32[2048,1024]{1,0:T(8,128)}, f32[2048,128]{1,0:T(8,128)}, bf16[4,8,3,128,128]{4,3,2,1,0:T(8,128)(2,1)}, bf16[4,8,3,128,128]{4,3,2,1,0:T(8,128)(2,1)}) custom-call(s32[2]{0:T(128)} %add_multiply_fusion.places_ref, bf16[4,8,3,128,128]{4,3,2,1,0:T(8,128)(2,1)} %bitcast.312, ...), custom_call_target="tpu_custom_call" | custom-call | flops 38654705664 | bytes 41943040 | tf_op jit(solution)/shard_map/pallas_call | solution.py:272
  313.9 9.9 %collective-permute-done.15.refs_1_ = bf16[4,8,3,128,128]{4,3,2,1,0:T(8,128)(2,1)} collective-permute-done((bf16[4,8,3,128,128]{4,3,2,1,0:T(8,128)(2,1)}, bf16[4,8,3,128,128]{4,3,2,1,0:T(8,128)(2,1)}, u32[]{:S(2)}, u32[]{:S(2)}) %collective-permute-start.15) | collective-permute-done | bytes 3145760 | tf_op jit(solution)/shard_map/ppermute | solution.py:650
  323.8 61.8 %shard_map.157 = (f32[2048,1024]{1,0:T(8,128)}, f32[2048,1024]{1,0:T(8,128)}, f32[2048,128]{1,0:T(8,128)}, bf16[4,8,3,128,128]{4,3,2,1,0:T(8,128)(2,1)}, bf16[4,8,3,128,128]{4,3,2,1,0:T(8,128)(2,1)}) custom-call(s32[2]{0:T(128)} %add_multiply_fusion.places_ref, bf16[4,8,3,128,128]{4,3,2,1,0:T(8,128)(2,1)} %bitcast.310, ...), custom_call_target="tpu_custom_call", output_to_operand_aliasing={{0}: (8, {}), {1}: (9, {})} | custom-call | flops 38654705664 | bytes 41943040 | tf_op jit(solution)/shard_map/pallas_call | solution.py:272
  386.0 5.2 collective-permute-done.14.refs_1_
  391.2 62.1 %shard_map.158 = (f32[2048,1024]{1,0:T(8,128)}, f32[2048,1024]{1,0:T(8,128)}, f32[2048,128]{1,0:T(8,128)}, bf16[4,8,3,128,128]{4,3,2,1,0:T(8,128)(2,1)}, bf16[4,8,3,128,128]{4,3,2,1,0:T(8,128)(2,1)}) custom-call(s32[2]{0:T(128)} %add_multiply_fusion.places_ref, ...), custom_call_target="tpu_custom_call", output_to_operand_aliasing={{0}: (8, {}), {1}: (9, {})} | custom-call | flops 38654705664 | bytes 41943040 | tf_op jit(solution)/shard_map/pallas_call | solution.py:272
  453.4 2.8 collective-permute-done.16.refs_9_
  456.2 62.0 %shard_map.159 = (f32[2048,1024]{1,0:T(8,128)}, f32[2048,1024]{1,0:T(8,128)}, f32[2048,128]{1,0:T(8,128)}, bf16[4,8,3,128,128]{4,3,2,1,0:T(8,128)(2,1)}, bf16[4,...) custom-call(s32[2]{0:T(128)} %add_multiply_fusion.places_ref, ...), custom_call_target="tpu_custom_call", output_to_operand_aliasing={{0}: (8, {}), {1}: (9, {}), {5}: (10, {})} | custom-call | flops 38654705664 | bytes 41943040 | tf_op jit(solution)/shard_map/pallas_call | solution.py:272
  518.2 6.5 add_convert_fusion.1
  526.5 3.3 multiply_reduce_fusion.3
  529.8 5.9 fusion.48
  535.8 12.2 %add.315.refs_0_ = f32[2048,1024]{1,0:T(8,128)} add(f32[2048,1024]{1,0:T(8,128)} %get-tuple-element.50, f32[2048,1024]{1,0:T(8,128)} %fusion.48) | non-fusion elementwise | flops 2097152 | bytes 25165824 | tf_op jit(solution)/shard_map/add | solution.py:702
  548.0 4.1 convert.41
  557.8 3.3 add_convert_fusion.2
  562.7 6.2 fusion.47
  572.4 68.9 %collective-permute-done.42 = bf16[8,3,128,128]{3,2,0,1:T(8,128)(2,1)} collective-permute-done((bf16[8,3,128,128]{3,2,0,1:T(8,128)(2,1)}, bf16[8,3,128,128]{3,2,0,1:T(8,128)(2,1)}, u32[]{:S(2)}, u32[]{:S(2)}) %collective-permute-start.42) | collective-permute-done | bytes 786464 | tf_op jit(solution)/shard_map/ppermute | solution.py:730
  644.9 3.2 multiply_reduce_fusion
  648.1 4.8 fusion.69
  654.2 2.8 fusion.19
  658.5 4.4 all-to-all-start.2
  667.7 4.0 convert.42
  674.4 4.9 add_convert_fusion
  679.4 3.0 copy.156
  683.9 24.9 %shard_map.164 = bf16[1,1024,1024]{2,1,0:T(8,128)(2,1)S(1)} custom-call(bf16[1,1024,1024]{2,1,0:T(8,128)(2,1)S(1)} %reshape.474.heads_ref, bf16[1,1024,512]{2,1,0:T(8,128)(2,1)S(1)} %reshape.488.grad_ref, f32[1,4,1024,2]{3,2,1,0:T(8,128)} %copy-done.3), custom_call_target="tpu_custom_call" | custom-call | flops 19327352832 | bytes 8388608 | tf_op jit(solution)/shard_map/pallas_call | solution.py:397
  710.1 4.5 reshape.489
  714.6 3.9 all-to-all-start.3
  728.2 3.7 fusion.15
  731.9 12.6 %all-to-all-done.3 = bf16[1,1024,4,256]{3,2,0,1:T(4,128)(2,1)S(1)} async-done(((bf16[1,1024,4,256]{3,2,0,1:T(4,128)(2,1)}), bf16[1,1024,4,256]{3,2,0,1:T(4,128)(2,1)S(1)}, u32[]{:S(2)}, u32[]{:S(2)}) %all-to-all-start.3) | async-done | bytes 2097184 | tf_op jit(solution)/shard_map/all_to_all | solution.py:734
  745.8 3.0 copy.126
  758.5 3.9 fusion.11
  768.4 6.6 collective-permute-done.26
  775.1 2.6 convert_add_fusion
  779.3 5.2 collective-permute-start.27
  795.3 10.0 %collective-permute-done.31 = bf16[4,2,64,1024]{3,2,1,0:T(8,128)(2,1)} collective-permute-done((bf16[4,2,64,1024]{3,2,1,0:T(8,128)(2,1)}, bf16[4,2,64,1024]{3,2,1,0:T(8,128)(2,1)}, u32[]{:S(2)}, u32[]{:S(2)}) %collective-permute-start.31) | collective-permute-done | bytes 1048608 | tf_op jit(solution)/shard_map/ppermute | solution.py:482
  813.0 4.3 collective-permute-start.40
  818.3 2.7 collective-permute-done.40
  823.3 3.9 collective-permute-start.33
  827.1 2.7 collective-permute-start.34
  829.8 3.9 fusion.21
  833.8 2.9 collective-permute-done.34
  (364 shorter events, 137.0 us)
Async XLA Ops:
  7.2 201.7 %copy-start = (s32[4,512,8]{1,2,0:T(8,128)S(1)}, s32[4,512,8]{1,2,0:T(8,128)}, u32[]{:S(2)}) copy-start(s32[4,512,8]{1,2,0:T(8,128)} %param.10) | copy-start | bytes 196612
  7.2 80.6 %all-gather.12.cloned.1.call-start = ((), (), s32[]{:S(2)}) async-start(), calls=%async_computation.10 | async-start | bytes 5406720 | tf_op jit(solution)/shard_map/all_gather | solution.py:543
  9.7 175.3 %all-gather.20.cloned.1.call-start = ((), (), s32[]{:S(2)}) async-start(), calls=%async_computation.20 | async-start | bytes 3932160 | tf_op jit(solution)/shard_map/all_gather | solution.py:584
  13.4 204.6 %all-gather.22.cloned.1.call-start = ((), (), s32[]{:S(2)}) async-start(), calls=%async_computation.21 | async-start | bytes 3932160 | tf_op jit(solution)/shard_map/all_gather | solution.py:584
  14.2 299.4 %all-gather.18.cloned.1.call-start = ((), (), s32[]{:S(2)}) async-start(), calls=%async_computation.19 | async-start | bytes 3932160 | tf_op jit(solution)/shard_map/all_gather | solution.py:584
  14.4 14.0 %collective-permute-start.6 = (bf16[48,1024]{1,0:T(8,128)(2,1)S(1)}, bf16[48,1024]{1,0:T(8,128)(2,1)S(1)}, u32[]{:S(2)}, u32[]{:S(2)}) collective-permute-start(bf16[48,1024]{1,0:T(8,128)(2,1)S(1)} %reshape.479), channel_id=1, source_target_pairs={{0,8},{8,16},{16,24},{24,0},{1,9},{9,17},{17,25},{25,1},{2,10},{10... | collective-permute-start | bytes 294920 | tf_op jit(solution)/shard_map/ppermute | solution.py:447
  17.5 10.9 %collective-permute-start.5 = (bf16[48,1024]{1,0:T(8,128)(2,1)S(1)}, bf16[48,1024]{1,0:T(8,128)(2,1)S(1)}, u32[]{:S(2)}, u32[]{:S(2)}) collective-permute-start(bf16[48,1024]{1,0:T(8,128)(2,1)S(1)} %reshape.479), channel_id=1, source_target_pairs={{0,16},{8,24},{16,0},{24,8},{1,17},{9,25},{17,1},{25,9},{2,18},{10... | collective-permute-start | bytes 294920 | tf_op jit(solution)/shard_map/ppermute | solution.py:447
  20.1 6.7 collective-permute-start.4
  21.4 30.0 %collective-permute-start.1 = (bf16[512,1024]{1,0:T(8,128)(2,1)S(1)}, bf16[512,1024]{1,0:T(8,128)(2,1)}, u32[]{:S(2)}, u32[]{:S(2)}) collective-permute-start(bf16[512,1024]{1,0:T(8,128)(2,1)S(1)} %bitcast.275), channel_id=1, source_target_pairs={{0,2},{1,3},{2,0},{3,1},{4,6},{5,7},{6,4},{7,5},{8,10},{9,11},{10,... | collective-permute-start | bytes 3145736 | tf_op jit(solution)/shard_map/ppermute | solution.py:420
  22.9 44.7 %collective-permute-start = (bf16[512,1024]{1,0:T(8,128)(2,1)S(1)}, bf16[512,1024]{1,0:T(8,128)(2,1)}, u32[]{:S(2)}, u32[]{:S(2)}) collective-permute-start(bf16[512,1024]{1,0:T(8,128)(2,1)S(1)} %bitcast.276), channel_id=1, source_target_pairs={{0,1},{1,0},{2,3},{3,2},{4,5},{5,4},{6,7},{7,6},{8,9},{9,8},{10,11... | collective-permute-start | bytes 3145736 | tf_op jit(solution)/shard_map/ppermute | solution.py:421
  23.4 76.3 %copy-start.43 = (f32[512,32]{0,1:T(8,128)}, f32[512,32]{0,1:T(8,128)S(1)}, u32[]{:S(2)}) copy-start(f32[512,32]{0,1:T(8,128)S(1)} %get-tuple-element.145) | copy-start | bytes 196612
  23.4 76.3 %copy-start.45 = (f32[512,32]{0,1:T(8,128)}, f32[512,32]{0,1:T(8,128)S(1)}, u32[]{:S(2)}) copy-start(f32[512,32]{0,1:T(8,128)S(1)} %get-tuple-element.146) | copy-start | bytes 196612
  26.8 61.0 %collective-permute-start.3 = (bf16[8,3,128,128]{3,2,1,0:T(8,128)(2,1)}, bf16[8,3,128,128]{3,2,1,0:T(8,128)(2,1)}, u32[]{:S(2)}, u32[]{:S(2)}) collective-permute-start(bf16[8,3,128,128]{3,2,1,0:T(8,128)(2,1)} %get-tuple-element.133), channel_id=1, source_target_pairs={{0,4},{4,0},{1,5},{5,1},{2,6},{6,2},{3,7},{7,3},{8,12},{12,8},{9,1... | collective-permute-start | bytes 2359304 | tf_op jit(solution)/shard_map/ppermute | solution.py:549
  51.5 16.2 %collective-permute-start.2 = (bf16[512,1024]{1,0:T(8,128)(2,1)}, bf16[512,1024]{1,0:T(8,128)(2,1)}, u32[]{:S(2)}, u32[]{:S(2)}) collective-permute-start(bf16[512,1024]{1,0:T(8,128)(2,1)} %collective-permute-done.1), channel_id=1, source_target_pairs={{0,1},{1,0},{2,3},{3,2},{4,5},{5,4},{6,7},{7,6},{8,9},{9,8},{10,11... | collective-permute-start | bytes 3145736 | tf_op jit(solution)/shard_map/ppermute | solution.py:422
  52.4 12.8 %collective-permute-start.7 = (bf16[4,48,1024]{2,1,0:T(8,128)(2,1)S(1)}, bf16[4,48,1024]{2,1,0:T(8,128)(2,1)S(1)}, u32[]{:S(2)}, u32[]{:S(2)}) collective-permute-start(bf16[4,48,1024]{2,1,0:T(8,128)(2,1)S(1)} %constant_dynamic-slice_fusion.4), channel_id=1, source_target_pairs={{0,4},{4,0},{1,5},{5,1},{2,6},{6,2},{3,7},{7,3},{8,12},{12,8},{9,1... | collective-permute-start | bytes 1179656 | tf_op jit(solution)/shard_map/ppermute | solution.py:447
  66.4 41.1 %collective-permute-start.8 = (bf16[2,4,48,1024]{3,2,0,1:T(8,128)(2,1)}, bf16[2,4,48,1024]{3,2,0,1:T(8,128)(2,1)}, u32[]{:S(2)}, u32[]{:S(2)}) collective-permute-start(bf16[2,4,48,1024]{3,2,0,1:T(8,128)(2,1)} %fusion.28), channel_id=1, source_target_pairs={{0,2},{1,3},{2,0},{3,1},{4,6},{5,7},{6,4},{7,5},{8,10},{9,11},{10,... | collective-permute-start | bytes 2359304 | tf_op jit(solution)/shard_map/ppermute | solution.py:455
  102.8 29.3 %all-to-all-start = ((bf16[1,512,8,256]{3,1,0,2:T(8,128)(2,1)}), bf16[1,512,8,256]{3,1,0,2:T(8,128)(2,1)S(1)}, u32[]{:S(2)}, u32[]{:S(2)}) async-start(bf16[1,512,8,256]{3,1,0,2:T(8,128)(2,1)} %copy.112), calls=%async_computation | async-start | bytes 4194304 | tf_op jit(solution)/shard_map/all_to_all | solution.py:609
  106.6 346.8 %all-gather.14.cloned.1.call-start = ((), (), s32[]{:S(2)}) async-start(), calls=%async_computation.17 | async-start | bytes 3932160 | tf_op jit(solution)/shard_map/all_gather | solution.py:584
  110.3 55.0 %collective-permute-start.9 = (bf16[2,2,4,48,1024]{4,3,1,2,0:T(8,128)(2,1)}, bf16[2,2,4,48,1024]{4,3,1,2,0:T(8,128)(2,1)}, u32[]{:S(2)}, u32[]{:S(2)}) collective-permute-start(bf16[2,2,4,48,1024]{4,3,1,2,0:T(8,128)(2,1)} %maximum_select_fusion.1), channel_id=1, source_target_pairs={{0,1},{1,0},{2,3},{3,2},{4,5},{5,4},{6,7},{7,6},{8,9},{9,8},{10,11... | collective-permute-start | bytes 4718600 | tf_op jit(solution)/shard_map/ppermute | solution.py:455
  158.7 18.3 %all-to-all-start.1 = ((bf16[1,1024,4,128]{3,2,0,1:T(4,128)(2,1)}), bf16[1,1024,4,128]{3,2,0,1:T(4,128)(2,1)}, u32[]{:S(2)}, u32[]{:S(2)}) async-start(bf16[1,1024,4,128]{3,2,0,1:T(4,128)(2,1)} %bitcast.267), calls=%async_computation.1 | async-start | bytes 2097152 | tf_op jit(solution)/shard_map/all_to_all | solution.py:613
  163.3 290.1 %all-gather.16.cloned.1.call-start = ((), (), s32[]{:S(2)}) async-start(), calls=%async_computation.18 | async-start | bytes 3932160 | tf_op jit(solution)/shard_map/all_gather | solution.py:586
  184.9 23.9 %collective-permute-start.11 = (bf16[512,1024]{1,0:T(8,128)(2,1)S(1)}, bf16[512,1024]{1,0:T(8,128)(2,1)}, u32[]{:S(2)}, u32[]{:S(2)}) collective-permute-start(bf16[512,1024]{1,0:T(8,128)(2,1)S(1)} %multiply_convert_fusion), channel_id=1, source_target_pairs={{0,2},{1,3},{2,0},{3,1},{4,6},{5,7},{6,4},{7,5},{8,10},{9,11},{10,... | collective-permute-start | bytes 3145736 | tf_op jit(solution)/shard_map/ppermute | solution.py:420
  185.0 71.4 %collective-permute-start.13 = (bf16[4,8,3,128,128]{4,3,2,1,0:T(8,128)(2,1)}, bf16[4,8,3,128,128]{4,3,2,1,0:T(8,128)(2,1)}, u32[]{:S(2)}, u32[]{:S(2)}) collective-permute-start(bf16[4,8,3,128,128]{4,3,2,1,0:T(8,128)(2,1)} %bitcast.311), channel_id=1, source_target_pairs={{0,4},{4,0},{1,5},{5,1},{2,6},{6,2},{3,7},{7,3},{8,12},{12,8},{9,1... | collective-permute-start | bytes 9437192 | tf_op jit(solution)/shard_map/ppermute | solution.py:650
  185.3 34.5 %collective-permute-start.10 = (bf16[512,1024]{1,0:T(8,128)(2,1)S(1)}, bf16[512,1024]{1,0:T(8,128)(2,1)}, u32[]{:S(2)}, u32[]{:S(2)}) collective-permute-start(bf16[512,1024]{1,0:T(8,128)(2,1)S(1)} %multiply_convert_fusion), channel_id=1, source_target_pairs={{0,1},{1,0},{2,3},{3,2},{4,5},{5,4},{6,7},{7,6},{8,9},{9,8},{10,11... | collective-permute-start | bytes 3145736 | tf_op jit(solution)/shard_map/ppermute | solution.py:421
  208.7 11.1 %collective-permute-start.12 = (bf16[512,1024]{1,0:T(8,128)(2,1)}, bf16[512,1024]{1,0:T(8,128)(2,1)}, u32[]{:S(2)}, u32[]{:S(2)}) collective-permute-start(bf16[512,1024]{1,0:T(8,128)(2,1)} %collective-permute-done.11), channel_id=1, source_target_pairs={{0,1},{1,0},{2,3},{3,2},{4,5},{5,4},{6,7},{7,6},{8,9},{9,8},{10,11... | collective-permute-start | bytes 3145736 | tf_op jit(solution)/shard_map/ppermute | solution.py:422
  218.1 105.7 %collective-permute-start.15 = (bf16[4,8,3,128,128]{4,3,2,1,0:T(8,128)(2,1)}, bf16[4,8,3,128,128]{4,3,2,1,0:T(8,128)(2,1)}, u32[]{:S(2)}, u32[]{:S(2)}) collective-permute-start(bf16[4,8,3,128,128]{4,3,2,1,0:T(8,128)(2,1)} %bitcast.309), channel_id=1, source_target_pairs={{0,4},{4,0},{1,5},{5,1},{2,6},{6,2},{3,7},{7,3},{8,12},{12,8},{9,1... | collective-permute-start | bytes 9437192 | tf_op jit(solution)/shard_map/ppermute | solution.py:650
  219.6 328.4 %reduce-scatter.7.cloned.1.call-start = ((), (), s32[]{:S(2)}) async-start(), calls=%async_computation.11 | async-start | bytes 3932160 | tf_op jit(solution)/shard_map/reduce_scatter | solution.py:693
  313.5 234.5 %reduce-scatter.9.cloned.1.call-start = ((), (), s32[]{:S(2)}) async-start(), calls=%async_computation.12 | async-start | bytes 3932160 | tf_op jit(solution)/shard_map/reduce_scatter | solution.py:693
  313.6 77.6 %collective-permute-start.14 = (bf16[4,8,3,128,128]{4,3,2,1,0:T(8,128)(2,1)}, bf16[4,8,3,128,128]{4,3,2,1,0:T(8,128)(2,1)}, u32[]{:S(2)}, u32[]{:S(2)}) collective-permute-start(bf16[4,8,3,128,128]{4,3,2,1,0:T(8,128)(2,1)} %shard_map.156.refs_0_), channel_id=1, source_target_pairs={{0,4},{4,0},{1,5},{5,1},{2,6},{6,2},{3,7},{7,3},{8,12},{12,8},{9,1... | collective-permute-start | bytes 9437192 | tf_op jit(solution)/shard_map/ppermute | solution.py:650
  385.6 70.6 %collective-permute-start.16 = (bf16[4,8,3,128,128]{4,3,2,1,0:T(8,128)(2,1)}, bf16[4,8,3,128,128]{4,3,2,1,0:T(8,128)(2,1)}, u32[]{:S(2)}, u32[]{:S(2)}) collective-permute-start(bf16[4,8,3,128,128]{4,3,2,1,0:T(8,128)(2,1)} %get-tuple-element.48), channel_id=1, source_target_pairs={{0,4},{4,0},{1,5},{5,1},{2,6},{6,2},{3,7},{7,3},{8,12},{12,8},{9,1... | collective-permute-start | bytes 9437192 | tf_op jit(solution)/shard_map/ppermute | solution.py:654
  386.0 332.6 %reduce-scatter.11.cloned.1.call-start = ((), (), s32[]{:S(2)}) async-start(), calls=%async_computation.13 | async-start | bytes 3932160 | tf_op jit(solution)/shard_map/reduce_scatter | solution.py:728
  524.7 264.2 %reduce-scatter.17.cloned.1.call-start = ((), (), s32[]{:S(2)}) async-start(), calls=%async_computation.16 | async-start | bytes 3932160 | tf_op jit(solution)/shard_map/reduce_scatter | solution.py:693
  525.3 283.7 %reduce-scatter.15.cloned.1.call-start = ((), (), s32[]{:S(2)}) async-start(), calls=%async_computation.15 | async-start | bytes 3932160 | tf_op jit(solution)/shard_map/reduce_scatter | solution.py:693
  553.6 4.1 collective-permute-start.18
  553.6 99.3 %collective-permute-start.20 = (bf16[4,8,3,128,128]{4,3,2,1,0:T(8,128)(2,1)}, bf16[4,8,3,128,128]{4,3,2,1,0:T(8,128)(2,1)}, u32[]{:S(2)}, u32[]{:S(2)}) collective-permute-start(bf16[4,8,3,128,128]{4,3,2,1,0:T(8,128)(2,1)} %shard_map.161), channel_id=1, source_target_pairs={{0,4},{4,0},{1,5},{5,1},{2,6},{6,2},{3,7},{7,3},{8,12},{12,8},{9,1... | collective-permute-start | bytes 9437192 | tf_op jit(solution)/shard_map/ppermute | solution.py:654
  556.3 85.0 %collective-permute-start.42 = (bf16[8,3,128,128]{3,2,0,1:T(8,128)(2,1)}, bf16[8,3,128,128]{3,2,0,1:T(8,128)(2,1)}, u32[]{:S(2)}, u32[]{:S(2)}) collective-permute-start(bf16[8,3,128,128]{3,2,0,1:T(8,128)(2,1)} %copy.129), channel_id=1, source_target_pairs={{0,4},{4,0},{1,5},{5,1},{2,6},{6,2},{3,7},{7,3},{8,12},{12,8},{9,1... | collective-permute-start | bytes 2359304 | tf_op jit(solution)/shard_map/ppermute | solution.py:730
  557.7 86.9 %collective-permute-start.17 = (bf16[512,1024]{1,0:T(8,128)(2,1)}, bf16[512,1024]{1,0:T(8,128)(2,1)}, u32[]{:S(2)}, u32[]{:S(2)}) collective-permute-start(bf16[512,1024]{1,0:T(8,128)(2,1)} %get-tuple-element.130), channel_id=1, source_target_pairs={{0,1},{1,0},{2,3},{3,2},{4,5},{5,4},{6,7},{7,6},{8,9},{9,8},{10,11... | collective-permute-start | bytes 3145736 | tf_op jit(solution)/shard_map/ppermute | solution.py:430
  561.0 83.6 %collective-permute-start.19 = (bf16[512,1024]{1,0:T(8,128)(2,1)}, bf16[512,1024]{1,0:T(8,128)(2,1)}, u32[]{:S(2)}, u32[]{:S(2)}) collective-permute-start(bf16[512,1024]{1,0:T(8,128)(2,1)} %add_convert_fusion.2), channel_id=1, source_target_pairs={{0,2},{1,3},{2,0},{3,1},{4,6},{5,7},{6,4},{7,5},{8,10},{9,11},{10,... | collective-permute-start | bytes 3145736 | tf_op jit(solution)/shard_map/ppermute | solution.py:435
  568.9 72.5 %copy-start.33 = (bf16[8,3,128,128]{3,2,1,0:T(8,128)(2,1)S(1)}, bf16[8,3,128,128]{3,2,1,0:T(8,128)(2,1)}, u32[]{:S(2)}) copy-start(bf16[8,3,128,128]{3,2,1,0:T(8,128)(2,1)} %get-tuple-element.60) | copy-start | bytes 2359300
  658.5 20.9 %all-to-all-start.2 = ((bf16[1,512,8,128]{3,1,0,2:T(8,128)(2,1)}), bf16[1,512,8,128]{3,1,0,2:T(8,128)(2,1)}, u32[]{:S(2)}, u32[]{:S(2)}) async-start(bf16[1,512,8,128]{3,1,0,2:T(8,128)(2,1)} %copy.123), calls=%async_computation.4 | async-start | bytes 2097152 | tf_op jit(solution)/shard_map/all_to_all | solution.py:721
  662.9 174.5 %reduce-scatter.13.cloned.1.call-start = ((), (), s32[]{:S(2)}) async-start(), calls=%async_computation.14 | async-start | bytes 3932160 | tf_op jit(solution)/shard_map/reduce_scatter | solution.py:728
  667.7 55.0 %collective-permute-start.36 = (bf16[4,2,2,32,1024]{4,3,2,1,0:T(8,128)(2,1)}, bf16[4,2,2,32,1024]{4,3,2,1,0:T(8,128)(2,1)}, u32[]{:S(2)}, u32[]{:S(2)}) collective-permute-start(bf16[4,2,2,32,1024]{4,3,2,1,0:T(8,128)(2,1)} %dynamic-slice_bitcast_fusion.1), channel_id=1, source_target_pairs={{0,1},{1,0},{2,3},{3,2},{4,5},{5,4},{6,7},{7,6},{8,9},{9,8},{10,11... | collective-permute-start | bytes 3145736 | tf_op jit(solution)/shard_map/ppermute | solution.py:482
  673.3 54.9 %collective-permute-start.22 = (bf16[512,1024]{1,0:T(8,128)(2,1)}, bf16[512,1024]{1,0:T(8,128)(2,1)}, u32[]{:S(2)}, u32[]{:S(2)}) collective-permute-start(bf16[512,1024]{1,0:T(8,128)(2,1)} %get-tuple-element.129), channel_id=1, source_target_pairs={{0,1},{1,0},{2,3},{3,2},{4,5},{5,4},{6,7},{7,6},{8,9},{9,8},{10,11... | collective-permute-start | bytes 3145736 | tf_op jit(solution)/shard_map/ppermute | solution.py:430
  714.6 29.9 %all-to-all-start.3 = ((bf16[1,1024,4,256]{3,2,0,1:T(4,128)(2,1)}), bf16[1,1024,4,256]{3,2,0,1:T(4,128)(2,1)S(1)}, u32[]{:S(2)}, u32[]{:S(2)}) async-start(bf16[1,1024,4,256]{3,2,0,1:T(4,128)(2,1)} %bitcast.258), calls=%async_computation.5 | async-start | bytes 4194304 | tf_op jit(solution)/shard_map/all_to_all | solution.py:734
  726.5 36.2 %collective-permute-start.37 = (bf16[4,2,32,1024]{3,2,1,0:T(8,128)(2,1)}, bf16[4,2,32,1024]{3,2,1,0:T(8,128)(2,1)}, u32[]{:S(2)}, u32[]{:S(2)}) collective-permute-start(bf16[4,2,32,1024]{3,2,1,0:T(8,128)(2,1)} %fusion.32), channel_id=1, source_target_pairs={{0,2},{1,3},{2,0},{3,1},{4,6},{5,7},{6,4},{7,5},{8,10},{9,11},{10,... | collective-permute-start | bytes 1572872 | tf_op jit(solution)/shard_map/ppermute | solution.py:482
  757.2 17.9 %collective-permute-start.30 = (bf16[4,2,2,64,1024]{4,3,2,1,0:T(8,128)(2,1)}, bf16[4,2,2,64,1024]{4,3,2,1,0:T(8,128)(2,1)}, u32[]{:S(2)}, u32[]{:S(2)}) collective-permute-start(bf16[4,2,2,64,1024]{4,3,2,1,0:T(8,128)(2,1)} %dynamic-slice_bitcast_fusion), channel_id=1, source_target_pairs={{0,1},{1,0},{2,3},{3,2},{4,5},{5,4},{6,7},{7,6},{8,9},{9,8},{10,11... | collective-permute-start | bytes 6291464 | tf_op jit(solution)/shard_map/ppermute | solution.py:482
  762.7 1.4 collective-permute-start.24
  764.2 4.1 collective-permute-start.25
  766.0 26.2 %collective-permute-start.38 = (bf16[4,32,1024]{2,1,0:T(8,128)(2,1)S(1)}, bf16[4,32,1024]{2,1,0:T(8,128)(2,1)}, u32[]{:S(2)}, u32[]{:S(2)}) collective-permute-start(bf16[4,32,1024]{2,1,0:T(8,128)(2,1)S(1)} %fusion.38), channel_id=1, source_target_pairs={{0,4},{4,0},{1,5},{5,1},{2,6},{6,2},{3,7},{7,3},{8,12},{12,8},{9,1... | collective-permute-start | bytes 786440 | tf_op jit(solution)/shard_map/ppermute | solution.py:474
  768.3 6.7 collective-permute-start.26
  778.9 26.4 %collective-permute-start.31 = (bf16[4,2,64,1024]{3,2,1,0:T(8,128)(2,1)}, bf16[4,2,64,1024]{3,2,1,0:T(8,128)(2,1)}, u32[]{:S(2)}, u32[]{:S(2)}) collective-permute-start(bf16[4,2,64,1024]{3,2,1,0:T(8,128)(2,1)} %fusion.20), channel_id=1, source_target_pairs={{0,2},{1,3},{2,0},{3,1},{4,6},{5,7},{6,4},{7,5},{8,10},{9,11},{10,... | collective-permute-start | bytes 3145736 | tf_op jit(solution)/shard_map/ppermute | solution.py:482
  779.3 9.5 %collective-permute-start.27 = (bf16[16,128]{1,0:T(8,128)(2,1)S(1)}, bf16[16,128]{1,0:T(8,128)(2,1)S(1)}, u32[]{:S(2)}, u32[]{:S(2)}) collective-permute-start(bf16[16,128]{1,0:T(8,128)(2,1)S(1)} %get-tuple-element.142), channel_id=1, source_target_pairs={{0,8},{8,16},{16,24},{24,0},{1,9},{9,17},{17,25},{25,1},{2,10},{10... | collective-permute-start | bytes 12296 | tf_op jit(solution)/shard_map/ppermute | solution.py:474
  784.5 4.3 collective-permute-start.29
  784.5 4.7 collective-permute-start.28
  788.8 41.0 %collective-permute-start.21 = (bf16[512,1024]{1,0:T(8,128)(2,1)}, bf16[512,1024]{1,0:T(8,128)(2,1)}, u32[]{:S(2)}, u32[]{:S(2)}) collective-permute-start(bf16[512,1024]{1,0:T(8,128)(2,1)} %get-tuple-element.128), channel_id=1, source_target_pairs={{0,1},{1,0},{2,3},{3,2},{4,5},{5,4},{6,7},{7,6},{8,9},{9,8},{10,11... | collective-permute-start | bytes 3145736 | tf_op jit(solution)/shard_map/ppermute | solution.py:430
  788.8 20.3 %collective-permute-start.43 = (bf16[8,3,128,128]{3,2,1,0:T(8,128)(2,1)}, bf16[8,3,128,128]{3,2,1,0:T(8,128)(2,1)}, u32[]{:S(2)}, u32[]{:S(2)}) collective-permute-start(bf16[8,3,128,128]{3,2,1,0:T(8,128)(2,1)} %bitcast.315), channel_id=1, source_target_pairs={{0,4},{4,0},{1,5},{5,1},{2,6},{6,2},{3,7},{7,3},{8,12},{12,8},{9,1... | collective-permute-start | bytes 2359304 | tf_op jit(solution)/shard_map/ppermute | solution.py:730
  789.2 40.6 %collective-permute-start.23 = (bf16[512,1024]{1,0:T(8,128)(2,1)}, bf16[512,1024]{1,0:T(8,128)(2,1)}, u32[]{:S(2)}, u32[]{:S(2)}) collective-permute-start(bf16[512,1024]{1,0:T(8,128)(2,1)} %fusion.15), channel_id=1, source_target_pairs={{0,2},{1,3},{2,0},{3,1},{4,6},{5,7},{6,4},{7,5},{8,10},{9,11},{10,... | collective-permute-start | bytes 3145736 | tf_op jit(solution)/shard_map/ppermute | solution.py:435
  793.4 19.7 %collective-permute-start.39 = (bf16[32,1024]{1,0:T(8,128)(2,1)S(1)}, bf16[32,1024]{1,0:T(8,128)(2,1)S(1)}, u32[]{:S(2)}, u32[]{:S(2)}) collective-permute-start(bf16[32,1024]{1,0:T(8,128)(2,1)S(1)} %get-tuple-element.139), channel_id=1, source_target_pairs={{0,8},{8,16},{16,24},{24,0},{1,9},{9,17},{17,25},{25,1},{2,10},{10... | collective-permute-start | bytes 196616 | tf_op jit(solution)/shard_map/ppermute | solution.py:474
  808.7 13.0 %collective-permute-start.32 = (bf16[4,64,1024]{2,1,0:T(8,128)(2,1)}, bf16[4,64,1024]{2,1,0:T(8,128)(2,1)}, u32[]{:S(2)}, u32[]{:S(2)}) collective-permute-start(bf16[4,64,1024]{2,1,0:T(8,128)(2,1)} %fusion.33), channel_id=1, source_target_pairs={{0,4},{4,0},{1,5},{5,1},{2,6},{6,2},{3,7},{7,3},{8,12},{12,8},{9,1... | collective-permute-start | bytes 1572872 | tf_op jit(solution)/shard_map/ppermute | solution.py:474
  810.7 7.5 collective-permute-start.41
  813.0 7.9 collective-permute-start.40
  823.3 10.5 %collective-permute-start.33 = (bf16[64,1024]{1,0:T(8,128)(2,1)S(1)}, bf16[64,1024]{1,0:T(8,128)(2,1)S(1)}, u32[]{:S(2)}, u32[]{:S(2)}) collective-permute-start(bf16[64,1024]{1,0:T(8,128)(2,1)S(1)} %get-tuple-element.136), channel_id=1, source_target_pairs={{0,8},{8,16},{16,24},{24,0},{1,9},{9,17},{17,25},{25,1},{2,10},{10... | collective-permute-start | bytes 393224 | tf_op jit(solution)/shard_map/ppermute | solution.py:474
  827.1 6.6 collective-permute-start.35
  827.1 9.5 %collective-permute-start.34 = (bf16[64,1024]{1,0:T(8,128)(2,1)S(1)}, bf16[64,1024]{1,0:T(8,128)(2,1)S(1)}, u32[]{:S(2)}, u32[]{:S(2)}) collective-permute-start(bf16[64,1024]{1,0:T(8,128)(2,1)S(1)} %get-tuple-element.138), channel_id=1, source_target_pairs={{0,16},{8,24},{16,0},{24,8},{1,17},{9,25},{17,1},{25,9},{2,18},{10... | collective-permute-start | bytes 393224 | tf_op jit(solution)/shard_map/ppermute | solution.py:474
  (58 other events, 408.0 us)
Sparse Core Ops, SparseCore 0:
  11.5 76.3 all-gather.11
  89.4 64.8 all-gather.19
  155.9 62.1 all-gather.21
  219.5 62.1 all-gather.17
  283.1 62.1 all-gather.13
  346.7 62.1 all-gather.15
  411.2 58.8 reduce-scatter.6
  472.4 60.2 reduce-scatter.8
  535.6 60.2 reduce-scatter.10
  598.1 60.2 reduce-scatter.16
  660.7 60.2 reduce-scatter.14
  723.2 60.2 reduce-scatter.12

commit v5 on v4

--- a/solution.py
+++ b/solution.py
@@ -650,8 +650,7 @@
         expert_pieces[chunk].append(lax.ppermute(near, "ctx", swap_pairs(2, 1)))
 
     def cross(chunk):
-        held = after(far_sums[chunk], marks[chunk + 1]) if chunk > 1 else far_sums[chunk]
-        arrivals.append(lax.ppermute(held, "ctx", swap_pairs(2, 1)))
+        arrivals.append(lax.ppermute(far_sums[chunk], "ctx", swap_pairs(2, 1)))
 
     if paired:
         fetch(0)
@@ -688,28 +687,29 @@
             )
     if paired:
         cross(2)
-        first_sums, last_sums = (
-            [
-                by_rows(lax.psum_scatter(part, "fsdp", scatter_dimension=0))
-                for part in (far_sums[chunk], own_sums[chunk])
-            ]
-            for chunk in (0, CHUNKS - 1)
-        )
+        first_sums = [
+            by_rows(lax.psum_scatter(part, "fsdp", scatter_dimension=0))
+            for part in (far_sums[0], own_sums[0])
+        ]
     grad_chances = choice_total[:, :EXPERTS] * chosen_any
     grad_logits = chances * (grad_chances - jnp.sum(grad_chances * chances, axis=-1, keepdims=True))
     router_rows = router_full.astype(jnp.float32)
     grad_router = jnp.dot(grad_logits.T, group_rows.astype(jnp.float32), precision=HIGH)
     back_group = by_rows(totals[1] + jnp.dot(grad_logits, router_rows, precision=HIGH))
     if paired:
-        back_group, *first_sums = together(back_group, *first_sums)
+        back_group, *held = together(
+            back_group, *first_sums, *arrivals, far_sums[-1], own_sums[-1]
+        )
+        first_sums, arrivals = held[:2], held[2:4]
+        last_sums = [
+            by_rows(lax.psum_scatter(part, "fsdp", scatter_dimension=0)) for part in held[4:]
+        ]
     grad_second = by_rows(scatter_group(back_group))
     grad_gain_second = jnp.sum(grad_second * normed_second, axis=0)
     grad_hidden = cotangent.astype(jnp.float32).reshape(row_count, model_width) + rms_back(
         grad_second, normed_second, inverse_second, gain_rows[1]
     )
     grad_attn = by_rows(grad_hidden.astype(jnp.bfloat16))
-    if paired:
-        grad_attn, arrivals[1] = together(grad_attn, arrivals[1])
     moe_rows = by_rows(scatter_group(after(totals[0], grad_attn)))
     output = (hidden + moe_rows).astype(jnp.bfloat16).reshape(tokens.shape)
     grad_output_weight = transposed_times(grad_attn, merged)
@@ -722,14 +722,6 @@
     grad_head_rows = attend(
         head_rows, grad_heads.reshape(local_seqs, length, -1), log_totals
     ).reshape(local_seqs, length, local_groups, 4 * head_size)
-    if paired:
-        for own, arrived in zip(own_sums[1:-1], arrivals):
-            joined = (own.astype(jnp.float32) + arrived.astype(jnp.float32)).astype(jnp.bfloat16)
-            chunk_sums.append(lax.psum_scatter(joined, "fsdp", scatter_dimension=0))
-        for far, own in (first_sums, last_sums):
-            far = lax.ppermute(far, "ctx", swap_pairs(2, 1))
-            chunk_sums.append(own.astype(jnp.float32) + far.astype(jnp.float32))
-        chunk_sums = [chunk_sums[2], chunk_sums[0], chunk_sums[1], chunk_sums[3]]
     grad_turned = (
         lax.all_to_all(grad_head_rows, "ctx", split_axis=1, concat_axis=2, tiled=True)
         .astype(jnp.float32)
@@ -746,6 +738,15 @@
         .astype(jnp.bfloat16)
         .reshape(row_count, -1)
     )
+    if paired:
+        for own, arrived in zip(own_sums[1:-1], arrivals):
+            joined = (own.astype(jnp.float32) + arrived.astype(jnp.float32)).astype(jnp.bfloat16)
+            chunk_sums.append(lax.psum_scatter(joined, "fsdp", scatter_dimension=0))
+        first_sums[0] = after(first_sums[0], grad_projected)
+        for far, own in (first_sums, last_sums):
+            far = lax.ppermute(far, "ctx", swap_pairs(2, 1))
+            chunk_sums.append(own.astype(jnp.float32) + far.astype(jnp.float32))
+        chunk_sums = [chunk_sums[2], chunk_sums[0], chunk_sums[1], chunk_sums[3]]
     grad_inward = transposed_times(grad_projected, first_low)
     grad_first = jnp.dot(grad_projected, inward_full, preferred_element_type=jnp.float32)
     grad_gain_first = jnp.sum(grad_first * normed_first, axis=0)

time: 860 us -> 834 us (0.970)
  waiting for transfers between devices: 247 us -> 226 us
    ppermute x2, waiting for transfers between devices: 69 us -> 4.37 us  [per_device(): far = lax.ppermute(far, 'ctx', swap_pairs(2, 1))]
    ppermute x2, waiting for transfers between devices: 0.01 us -> 24 us  [scatter_group(): lax.ppermute((parts[2] + first).astype(jnp.bfloat16), 'tp', swap_pairs(co...]
    reduce_scatter x4, waiting for transfers between devices: 0.03 us -> 15.2 us  [per_device(): lax.psum_scatter(part, 'fsdp', scatter_dimension=0)]
    unnamed x137 -> x133, local copies, waits for them, and re-layouts: 21.6 us -> 17.4 us
  transfers between devices with their start and end apart: 60 -> 60, of which waited for: 21 -> 26; matrix products, arithmetic and copies ran while one was open for 25% -> 26% of each run, Pallas kernels for 34% -> 35%
where the time goes in v5:
time: 834 us; the launch traced here: 826 us
  Pallas kernels  286 us (34%)
  waiting for transfers between devices  226 us (27%)
  other arithmetic  108 us (13%)
  local copies, waits for them, and re-layouts  92.6 us (11%)
  starting transfers between devices  62.2 us (7%)
  matrix products  35.2 us (4%)
  between operations  16 us (2%)
    pallas_call x4, Pallas kernels, expert_pass(): pl.pallas_call(functools.partial(expert_kernel, first, steps, base_expert...  243 us
    ppermute x2, waiting for transfers between devices, gather_group(): across = lax.ppermute(rows, 'tp', swap_pairs(count, 2))  46.4 us
    ppermute x3, waiting for transfers between devices, fetch(): expert_pieces[chunk].append(lax.ppermute(near, 'ctx', swap_pairs(2, 1)))  33.9 us
    pallas_call x1, Pallas kernels, attend(): pl.pallas_call(functools.partial(attend_back_kernel, block), grid=(sequen...  24.9 us
    ppermute x2, waiting for transfers between devices, scatter_group(): lax.ppermute((parts[2] + first).astype(jnp.bfloat16), 'tp', swap_pairs(co...  24 us
    all_to_all x1, waiting for transfers between devices, per_device(): lax.all_to_all(sent_heads, 'ctx', split_axis=2, concat_axis=1, tiled=True)  21.8 us
    pallas_call x1, Pallas kernels, attend(): pl.pallas_call(functools.partial(attend_kernel, block), grid=(sequences,...  17.9 us
    ppermute x12, starting transfers between devices, scatter_axis(): lax.ppermute(sent, name, shifted(count, step)).astype(jnp.float32)  17.7 us
  transfers between devices with their start and end apart: 60, of which 26 were waited for; matrix products, arithmetic and copies ran while one was open for 26% of the time, Pallas kernels for 35%

profile of v5, /device:TPU:0, one launch (start us, length us, event | category | flops | bytes accessed | tf_op | source)
XLA Modules:
  0.0 825.7 jit_solution(1780165263014787671)
XLA Ops:
  9.8 3.7 pad_maximum_fusion.5
  14.5 3.1 collective-permute-start.6
  23.5 3.4 collective-permute-done.4
  28.6 22.9 %collective-permute-done.1 = bf16[512,1024]{1,0:T(8,128)(2,1)} collective-permute-done((bf16[512,1024]{1,0:T(8,128)(2,1)S(1)}, bf16[512,1024]{1,0:T(8,128)(2,1)}, u32[]{:S(2)}, u32[]{:S(2)}) %collective-permute-start.1) | collective-permute-done | bytes 1048608 | tf_op jit(solution)/shard_map/ppermute | solution.py:420
  55.4 9.8 %collective-permute-done.7 = bf16[4,48,1024]{2,1,0:T(8,128)(2,1)S(1)} collective-permute-done((bf16[4,48,1024]{2,1,0:T(8,128)(2,1)S(1)}, bf16[4,48,1024]{2,1,0:T(8,128)(2,1)S(1)}, u32[]{:S(2)}, u32[]{:S(2)}) %collective-permute-start.7) | collective-permute-done | bytes 393248 | tf_op jit(solution)/shard_map/ppermute | solution.py:447
  67.7 3.5 pad_maximum_fusion.refs_4_
  71.3 6.5 copy.117
  77.8 10.0 %all-gather.12.cloned.1.call-done.refs_0_ = bf16[32,80,1024]{2,1,0:T(8,128)(2,1)} async-done(((bf16[1,80,1024]{2,1,0:T(8,128)(2,1)}), bf16[32,80,1024]{2,1,0:T(8,128)(2,1)}) %all-gather.12.cloned.1.call-update) | async-done | bytes 5242896 | tf_op jit(solution)/shard_map/all_gather | solution.py:543
  89.1 4.9 slice.143
  94.8 4.7 convolution_bitcast_fusion
  102.7 3.8 all-to-all-start
  110.3 21.8 %all-to-all-done = bf16[1,512,8,256]{3,1,0,2:T(8,128)(2,1)S(1)} async-done(((bf16[1,512,8,256]{3,1,0,2:T(8,128)(2,1)}), bf16[1,512,8,256]{3,1,0,2:T(8,128)(2,1)S(1)}, u32[]{:S(2)}, u32[]{:S(2)}) %all-to-all-start) | async-done | bytes 2097184 | tf_op jit(solution)/shard_map/all_to_all | solution.py:609
  132.0 2.9 copy.119
  135.0 3.2 reshape.475.heads_ref
  138.2 17.9 %shard_map.154 = (bf16[1,1024,512]{2,1,0:T(8,128)(2,1)S(1)}, f32[1,4,1024,2]{3,2,1,0:T(8,128)S(1)}) custom-call(bf16[1,1024,1024]{2,1,0:T(8,128)(2,1)S(1)} %reshape.475.heads_ref), custom_call_target="tpu_custom_call" | custom-call | flops 8589934592 | bytes 8388608 | tf_op jit(solution)/shard_map/pallas_call | solution.py:383
  158.6 4.6 all-to-all-start.1
  169.5 7.4 all-to-all-done.1
  179.6 3.6 multiply_reduce_fusion.2
  185.3 23.5 %collective-permute-done.11 = bf16[512,1024]{1,0:T(8,128)(2,1)} collective-permute-done((bf16[512,1024]{1,0:T(8,128)(2,1)S(1)}, bf16[512,1024]{1,0:T(8,128)(2,1)}, u32[]{:S(2)}, u32[]{:S(2)}) %collective-permute-start.11) | collective-permute-done | bytes 1048608 | tf_op jit(solution)/shard_map/ppermute | solution.py:420
  219.8 3.5 pad_maximum_fusion.1.refs_2_
  223.4 6.6 copy.124
  230.0 3.5 fusion.73
  237.4 18.9 %collective-permute-done.13.refs_1_ = bf16[4,8,3,128,128]{4,3,2,1,0:T(8,128)(2,1)} collective-permute-done((bf16[4,8,3,128,128]{4,3,2,1,0:T(8,128)(2,1)}, bf16[4,8,3,128,128]{4,3,2,1,0:T(8,128)(2,1)}, u32[]{:S(2)}, u32[]{:S(2)}) %collective-permute-start.13) | collective-permute-done | bytes 3145760 | tf_op jit(solution)/shard_map/ppermute | solution.py:650
  256.4 57.2 %shard_map.155 = (f32[2048,1024]{1,0:T(8,128)}, f32[2048,1024]{1,0:T(8,128)}, f32[2048,128]{1,0:T(8,128)}, bf16[4,8,3,128,128]{4,3,2,1,0:T(8,128)(2,1)}, bf16[4,8,3,128,128]{4,3,2,1,0:T(8,128)(2,1)}) custom-call(s32[2]{0:T(128)} %add_multiply_fusion.places_ref, bf16[4,8,3,128,128]{4,3,2,1,0:T(8,128)(2,1)} %bitcast.314, ...), custom_call_target="tpu_custom_call" | custom-call | flops 38654705664 | bytes 41943040 | tf_op jit(solution)/shard_map/pallas_call | solution.py:272
  314.0 9.8 %collective-permute-done.15.refs_1_ = bf16[4,8,3,128,128]{4,3,2,1,0:T(8,128)(2,1)} collective-permute-done((bf16[4,8,3,128,128]{4,3,2,1,0:T(8,128)(2,1)}, bf16[4,8,3,128,128]{4,3,2,1,0:T(8,128)(2,1)}, u32[]{:S(2)}, u32[]{:S(2)}) %collective-permute-start.15) | collective-permute-done | bytes 3145760 | tf_op jit(solution)/shard_map/ppermute | solution.py:650
  323.8 61.8 %shard_map.157 = (f32[2048,1024]{1,0:T(8,128)}, f32[2048,1024]{1,0:T(8,128)}, f32[2048,128]{1,0:T(8,128)}, bf16[4,8,3,128,128]{4,3,2,1,0:T(8,128)(2,1)}, bf16[4,8,3,128,128]{4,3,2,1,0:T(8,128)(2,1)}) custom-call(s32[2]{0:T(128)} %add_multiply_fusion.places_ref, bf16[4,8,3,128,128]{4,3,2,1,0:T(8,128)(2,1)} %bitcast.312, ...), custom_call_target="tpu_custom_call", output_to_operand_aliasing={{0}: (8, {}), {1}: (9, {})} | custom-call | flops 38654705664 | bytes 41943040 | tf_op jit(solution)/shard_map/pallas_call | solution.py:272
  386.0 5.2 collective-permute-done.14.refs_1_
  391.2 61.9 %shard_map.158 = (f32[2048,1024]{1,0:T(8,128)}, f32[2048,1024]{1,0:T(8,128)}, f32[2048,128]{1,0:T(8,128)}, bf16[4,8,3,128,128]{4,3,2,1,0:T(8,128)(2,1)}, bf16[4,8,3,128,128]{4,3,2,1,0:T(8,128)(2,1)}) custom-call(s32[2]{0:T(128)} %add_multiply_fusion.places_ref, ...), custom_call_target="tpu_custom_call", output_to_operand_aliasing={{0}: (8, {}), {1}: (9, {})} | custom-call | flops 38654705664 | bytes 41943040 | tf_op jit(solution)/shard_map/pallas_call | solution.py:272
  453.4 5.1 collective-permute-done.16.refs_9_
  458.6 62.1 %shard_map.159 = (f32[2048,1024]{1,0:T(8,128)}, f32[2048,1024]{1,0:T(8,128)}, f32[2048,128]{1,0:T(8,128)}, bf16[4,8,3,128,128]{4,3,2,1,0:T(8,128)(2,1)}, bf16[4,...) custom-call(s32[2]{0:T(128)} %add_multiply_fusion.places_ref, ...), custom_call_target="tpu_custom_call", output_to_operand_aliasing={{0}: (8, {}), {1}: (9, {}), {5}: (10, {})} | custom-call | flops 38654705664 | bytes 41943040 | tf_op jit(solution)/shard_map/pallas_call | solution.py:272
  520.8 3.0 multiply_reduce_fusion.3
  523.9 6.3 fusion.48
  530.2 12.2 %add.315.refs_0_ = f32[2048,1024]{1,0:T(8,128)} add(f32[2048,1024]{1,0:T(8,128)} %get-tuple-element.52, f32[2048,1024]{1,0:T(8,128)} %fusion.48) | non-fusion elementwise | flops 2097152 | bytes 25165824 | tf_op jit(solution)/shard_map/add | solution.py:698
  542.4 6.5 add_convert_fusion
  549.0 4.6 convert.32
  556.3 4.9 add_convert_fusion.1
  561.3 3.3 add_convert_fusion.2
  566.5 24.0 %collective-permute-done.20 = bf16[512,1024]{1,0:T(8,128)(2,1)} collective-permute-done((bf16[512,1024]{1,0:T(8,128)(2,1)}, bf16[512,1024]{1,0:T(8,128)(2,1)}, u32[]{:S(2)}, u32[]{:S(2)}) %collective-permute-start.20) | collective-permute-done | bytes 1048608 | tf_op jit(solution)/shard_map/ppermute | solution.py:435
  590.6 3.4 multiply_reduce_fusion
  594.0 4.6 fusion.69
  601.3 4.6 all-to-all-start.2
  605.9 3.9 convolution_convert_fusion.1
  612.1 4.6 convert.33
  619.8 3.0 copy.163
  624.3 24.9 %shard_map.162 = bf16[1,1024,1024]{2,1,0:T(8,128)(2,1)S(1)} custom-call(bf16[1,1024,1024]{2,1,0:T(8,128)(2,1)S(1)} %reshape.475.heads_ref, bf16[1,1024,512]{2,1,0:T(8,128)(2,1)S(1)} %reshape.489.grad_ref, f32[1,4,1024,2]{3,2,1,0:T(8,128)} %copy-done.3), custom_call_target="tpu_custom_call" | custom-call | flops 19327352832 | bytes 8388608 | tf_op jit(solution)/shard_map/pallas_call | solution.py:397
  650.5 4.5 reshape.490
  655.0 3.9 all-to-all-start.3
  659.2 5.5 fusion.47
  671.4 3.2 fusion.15
  675.0 8.4 %all-to-all-done.3 = bf16[1,1024,4,256]{3,2,0,1:T(4,128)(2,1)S(1)} async-done(((bf16[1,1024,4,256]{3,2,0,1:T(4,128)(2,1)}), bf16[1,1024,4,256]{3,2,0,1:T(4,128)(2,1)S(1)}, u32[]{:S(2)}, u32[]{:S(2)}) %all-to-all-start.3) | async-done | bytes 2097184 | tf_op jit(solution)/shard_map/all_to_all | solution.py:726
  683.4 3.4 copy.132
  692.9 3.9 fusion.11
  703.3 4.2 collective-permute-done.25
  711.4 4.2 collective-permute-start.27
  717.1 4.9 collective-permute-start.28
  722.0 3.0 collective-permute-done.28
  735.7 3.0 collective-permute-done.40
  740.3 4.6 fusion.21
  744.9 4.4 collective-permute-done.42
  750.7 3.0 convert_add_fusion
  766.8 11.5 %collective-permute-done.31 = bf16[4,2,64,1024]{3,2,1,0:T(8,128)(2,1)S(1)} collective-permute-done((bf16[4,2,64,1024]{3,2,1,0:T(8,128)(2,1)S(1)}, bf16[4,2,64,1024]{3,2,1,0:T(8,128)(2,1)S(1)}, u32[]{:S(2)}, u32[]{:S(2)}) %collective-permute-start.31) | collective-permute-done | bytes 1048608 | tf_op jit(solution)/shard_map/ppermute | solution.py:482
  781.1 15.2 %reduce-scatter.15.cloned.1.call-done = bf16[1,8,3,128,128]{4,3,2,1,0:T(8,128)(2,1)} async-done(((bf16[4,8,3,128,128]{4,3,2,1,0:T(8,128)(2,1)}), bf16[1,8,3,128,128]{4,3,2,1,0:T(8,128)(2,1)}) %reduce-scatter.15.cloned.1.call-update) | async-done | bytes 786448 | tf_op jit(solution)/shard_map/reduce_scatter | solution.py:705
  803.5 2.8 collective-permute-start.35
  811.6 6.2 collective-permute-done.34
  (359 shorter events, 139.1 us)
Async XLA Ops:
  7.2 201.7 %copy-start = (s32[4,512,8]{1,2,0:T(8,128)S(1)}, s32[4,512,8]{1,2,0:T(8,128)}, u32[]{:S(2)}) copy-start(s32[4,512,8]{1,2,0:T(8,128)} %param.10) | copy-start | bytes 196612
  7.2 80.6 %all-gather.12.cloned.1.call-start = ((), (), s32[]{:S(2)}) async-start(), calls=%async_computation.10 | async-start | bytes 5406720 | tf_op jit(solution)/shard_map/all_gather | solution.py:543
  9.7 175.2 %all-gather.20.cloned.1.call-start = ((), (), s32[]{:S(2)}) async-start(), calls=%async_computation.20 | async-start | bytes 3932160 | tf_op jit(solution)/shard_map/all_gather | solution.py:584
  13.5 204.5 %all-gather.22.cloned.1.call-start = ((), (), s32[]{:S(2)}) async-start(), calls=%async_computation.21 | async-start | bytes 3932160 | tf_op jit(solution)/shard_map/all_gather | solution.py:584
  14.3 299.4 %all-gather.18.cloned.1.call-start = ((), (), s32[]{:S(2)}) async-start(), calls=%async_computation.19 | async-start | bytes 3932160 | tf_op jit(solution)/shard_map/all_gather | solution.py:584
  14.5 14.1 %collective-permute-start.6 = (bf16[48,1024]{1,0:T(8,128)(2,1)S(1)}, bf16[48,1024]{1,0:T(8,128)(2,1)S(1)}, u32[]{:S(2)}, u32[]{:S(2)}) collective-permute-start(bf16[48,1024]{1,0:T(8,128)(2,1)S(1)} %reshape.480), channel_id=1, source_target_pairs={{0,8},{8,16},{16,24},{24,0},{1,9},{9,17},{17,25},{25,1},{2,10},{10... | collective-permute-start | bytes 294920 | tf_op jit(solution)/shard_map/ppermute | solution.py:447
  17.6 11.0 %collective-permute-start.5 = (bf16[48,1024]{1,0:T(8,128)(2,1)S(1)}, bf16[48,1024]{1,0:T(8,128)(2,1)S(1)}, u32[]{:S(2)}, u32[]{:S(2)}) collective-permute-start(bf16[48,1024]{1,0:T(8,128)(2,1)S(1)} %reshape.480), channel_id=1, source_target_pairs={{0,16},{8,24},{16,0},{24,8},{1,17},{9,25},{17,1},{25,9},{2,18},{10... | collective-permute-start | bytes 294920 | tf_op jit(solution)/shard_map/ppermute | solution.py:447
  20.2 6.8 collective-permute-start.4
  21.5 30.0 %collective-permute-start.1 = (bf16[512,1024]{1,0:T(8,128)(2,1)S(1)}, bf16[512,1024]{1,0:T(8,128)(2,1)}, u32[]{:S(2)}, u32[]{:S(2)}) collective-permute-start(bf16[512,1024]{1,0:T(8,128)(2,1)S(1)} %bitcast.280), channel_id=1, source_target_pairs={{0,2},{1,3},{2,0},{3,1},{4,6},{5,7},{6,4},{7,5},{8,10},{9,11},{10,... | collective-permute-start | bytes 3145736 | tf_op jit(solution)/shard_map/ppermute | solution.py:420
  23.0 44.7 %collective-permute-start = (bf16[512,1024]{1,0:T(8,128)(2,1)S(1)}, bf16[512,1024]{1,0:T(8,128)(2,1)}, u32[]{:S(2)}, u32[]{:S(2)}) collective-permute-start(bf16[512,1024]{1,0:T(8,128)(2,1)S(1)} %bitcast.281), channel_id=1, source_target_pairs={{0,1},{1,0},{2,3},{3,2},{4,5},{5,4},{6,7},{7,6},{8,9},{9,8},{10,11... | collective-permute-start | bytes 3145736 | tf_op jit(solution)/shard_map/ppermute | solution.py:421
  23.5 76.2 %copy-start.41 = (f32[512,32]{0,1:T(8,128)}, f32[512,32]{0,1:T(8,128)S(1)}, u32[]{:S(2)}) copy-start(f32[512,32]{0,1:T(8,128)S(1)} %get-tuple-element.149) | copy-start | bytes 196612
  23.5 76.2 %copy-start.43 = (f32[512,32]{0,1:T(8,128)}, f32[512,32]{0,1:T(8,128)S(1)}, u32[]{:S(2)}) copy-start(f32[512,32]{0,1:T(8,128)S(1)} %get-tuple-element.150) | copy-start | bytes 196612
  26.9 60.9 %collective-permute-start.3 = (bf16[8,3,128,128]{3,2,1,0:T(8,128)(2,1)}, bf16[8,3,128,128]{3,2,1,0:T(8,128)(2,1)}, u32[]{:S(2)}, u32[]{:S(2)}) collective-permute-start(bf16[8,3,128,128]{3,2,1,0:T(8,128)(2,1)} %get-tuple-element.137), channel_id=1, source_target_pairs={{0,4},{4,0},{1,5},{5,1},{2,6},{6,2},{3,7},{7,3},{8,12},{12,8},{9,1... | collective-permute-start | bytes 2359304 | tf_op jit(solution)/shard_map/ppermute | solution.py:549
  51.5 16.2 %collective-permute-start.2 = (bf16[512,1024]{1,0:T(8,128)(2,1)}, bf16[512,1024]{1,0:T(8,128)(2,1)}, u32[]{:S(2)}, u32[]{:S(2)}) collective-permute-start(bf16[512,1024]{1,0:T(8,128)(2,1)} %collective-permute-done.1), channel_id=1, source_target_pairs={{0,1},{1,0},{2,3},{3,2},{4,5},{5,4},{6,7},{7,6},{8,9},{9,8},{10,11... | collective-permute-start | bytes 3145736 | tf_op jit(solution)/shard_map/ppermute | solution.py:422
  52.4 12.8 %collective-permute-start.7 = (bf16[4,48,1024]{2,1,0:T(8,128)(2,1)S(1)}, bf16[4,48,1024]{2,1,0:T(8,128)(2,1)S(1)}, u32[]{:S(2)}, u32[]{:S(2)}) collective-permute-start(bf16[4,48,1024]{2,1,0:T(8,128)(2,1)S(1)} %constant_dynamic-slice_fusion.4), channel_id=1, source_target_pairs={{0,4},{4,0},{1,5},{5,1},{2,6},{6,2},{3,7},{7,3},{8,12},{12,8},{9,1... | collective-permute-start | bytes 1179656 | tf_op jit(solution)/shard_map/ppermute | solution.py:447
  66.5 40.7 %collective-permute-start.8 = (bf16[2,4,48,1024]{3,2,0,1:T(8,128)(2,1)}, bf16[2,4,48,1024]{3,2,0,1:T(8,128)(2,1)}, u32[]{:S(2)}, u32[]{:S(2)}) collective-permute-start(bf16[2,4,48,1024]{3,2,0,1:T(8,128)(2,1)} %fusion.28), channel_id=1, source_target_pairs={{0,2},{1,3},{2,0},{3,1},{4,6},{5,7},{6,4},{7,5},{8,10},{9,11},{10,... | collective-permute-start | bytes 2359304 | tf_op jit(solution)/shard_map/ppermute | solution.py:455
  102.7 29.3 %all-to-all-start = ((bf16[1,512,8,256]{3,1,0,2:T(8,128)(2,1)}), bf16[1,512,8,256]{3,1,0,2:T(8,128)(2,1)S(1)}, u32[]{:S(2)}, u32[]{:S(2)}) async-start(bf16[1,512,8,256]{3,1,0,2:T(8,128)(2,1)} %copy.118), calls=%async_computation | async-start | bytes 4194304 | tf_op jit(solution)/shard_map/all_to_all | solution.py:609
  106.5 346.9 %all-gather.14.cloned.1.call-start = ((), (), s32[]{:S(2)}) async-start(), calls=%async_computation.17 | async-start | bytes 3932160 | tf_op jit(solution)/shard_map/all_gather | solution.py:584
  110.0 55.3 %collective-permute-start.9 = (bf16[2,2,4,48,1024]{4,3,1,2,0:T(8,128)(2,1)}, bf16[2,2,4,48,1024]{4,3,1,2,0:T(8,128)(2,1)}, u32[]{:S(2)}, u32[]{:S(2)}) collective-permute-start(bf16[2,2,4,48,1024]{4,3,1,2,0:T(8,128)(2,1)} %maximum_select_fusion.1), channel_id=1, source_target_pairs={{0,1},{1,0},{2,3},{3,2},{4,5},{5,4},{6,7},{7,6},{8,9},{9,8},{10,11... | collective-permute-start | bytes 4718600 | tf_op jit(solution)/shard_map/ppermute | solution.py:455
  158.6 18.4 %all-to-all-start.1 = ((bf16[1,1024,4,128]{3,2,0,1:T(4,128)(2,1)}), bf16[1,1024,4,128]{3,2,0,1:T(4,128)(2,1)}, u32[]{:S(2)}, u32[]{:S(2)}) async-start(bf16[1,1024,4,128]{3,2,0,1:T(4,128)(2,1)} %bitcast.272), calls=%async_computation.1 | async-start | bytes 2097152 | tf_op jit(solution)/shard_map/all_to_all | solution.py:613
  163.2 290.3 %all-gather.16.cloned.1.call-start = ((), (), s32[]{:S(2)}) async-start(), calls=%async_computation.18 | async-start | bytes 3932160 | tf_op jit(solution)/shard_map/all_gather | solution.py:586
  184.8 24.0 %collective-permute-start.11 = (bf16[512,1024]{1,0:T(8,128)(2,1)S(1)}, bf16[512,1024]{1,0:T(8,128)(2,1)}, u32[]{:S(2)}, u32[]{:S(2)}) collective-permute-start(bf16[512,1024]{1,0:T(8,128)(2,1)S(1)} %multiply_convert_fusion), channel_id=1, source_target_pairs={{0,2},{1,3},{2,0},{3,1},{4,6},{5,7},{6,4},{7,5},{8,10},{9,11},{10,... | collective-permute-start | bytes 3145736 | tf_op jit(solution)/shard_map/ppermute | solution.py:420
  184.9 71.4 %collective-permute-start.13 = (bf16[4,8,3,128,128]{4,3,2,1,0:T(8,128)(2,1)}, bf16[4,8,3,128,128]{4,3,2,1,0:T(8,128)(2,1)}, u32[]{:S(2)}, u32[]{:S(2)}) collective-permute-start(bf16[4,8,3,128,128]{4,3,2,1,0:T(8,128)(2,1)} %bitcast.313), channel_id=1, source_target_pairs={{0,4},{4,0},{1,5},{5,1},{2,6},{6,2},{3,7},{7,3},{8,12},{12,8},{9,1... | collective-permute-start | bytes 9437192 | tf_op jit(solution)/shard_map/ppermute | solution.py:650
  185.3 34.5 %collective-permute-start.10 = (bf16[512,1024]{1,0:T(8,128)(2,1)S(1)}, bf16[512,1024]{1,0:T(8,128)(2,1)}, u32[]{:S(2)}, u32[]{:S(2)}) collective-permute-start(bf16[512,1024]{1,0:T(8,128)(2,1)S(1)} %multiply_convert_fusion), channel_id=1, source_target_pairs={{0,1},{1,0},{2,3},{3,2},{4,5},{5,4},{6,7},{7,6},{8,9},{9,8},{10,11... | collective-permute-start | bytes 3145736 | tf_op jit(solution)/shard_map/ppermute | solution.py:421
  208.8 11.0 %collective-permute-start.12 = (bf16[512,1024]{1,0:T(8,128)(2,1)}, bf16[512,1024]{1,0:T(8,128)(2,1)}, u32[]{:S(2)}, u32[]{:S(2)}) collective-permute-start(bf16[512,1024]{1,0:T(8,128)(2,1)} %collective-permute-done.11), channel_id=1, source_target_pairs={{0,1},{1,0},{2,3},{3,2},{4,5},{5,4},{6,7},{7,6},{8,9},{9,8},{10,11... | collective-permute-start | bytes 3145736 | tf_op jit(solution)/shard_map/ppermute | solution.py:422
  218.0 105.7 %collective-permute-start.15 = (bf16[4,8,3,128,128]{4,3,2,1,0:T(8,128)(2,1)}, bf16[4,8,3,128,128]{4,3,2,1,0:T(8,128)(2,1)}, u32[]{:S(2)}, u32[]{:S(2)}) collective-permute-start(bf16[4,8,3,128,128]{4,3,2,1,0:T(8,128)(2,1)} %bitcast.311), channel_id=1, source_target_pairs={{0,4},{4,0},{1,5},{5,1},{2,6},{6,2},{3,7},{7,3},{8,12},{12,8},{9,1... | collective-permute-start | bytes 9437192 | tf_op jit(solution)/shard_map/ppermute | solution.py:650
  219.5 322.8 %reduce-scatter.7.cloned.1.call-start = ((), (), s32[]{:S(2)}) async-start(), calls=%async_computation.11 | async-start | bytes 3932160 | tf_op jit(solution)/shard_map/reduce_scatter | solution.py:691
  313.6 228.7 %reduce-scatter.9.cloned.1.call-start = ((), (), s32[]{:S(2)}) async-start(), calls=%async_computation.12 | async-start | bytes 3932160 | tf_op jit(solution)/shard_map/reduce_scatter | solution.py:691
  313.7 77.5 %collective-permute-start.14 = (bf16[4,8,3,128,128]{4,3,2,1,0:T(8,128)(2,1)}, bf16[4,8,3,128,128]{4,3,2,1,0:T(8,128)(2,1)}, u32[]{:S(2)}, u32[]{:S(2)}) collective-permute-start(bf16[4,8,3,128,128]{4,3,2,1,0:T(8,128)(2,1)} %shard_map.156.refs_0_), channel_id=1, source_target_pairs={{0,4},{4,0},{1,5},{5,1},{2,6},{6,2},{3,7},{7,3},{8,12},{12,8},{9,1... | collective-permute-start | bytes 9437192 | tf_op jit(solution)/shard_map/ppermute | solution.py:650
  385.6 73.0 %collective-permute-start.16 = (bf16[4,8,3,128,128]{4,3,2,1,0:T(8,128)(2,1)}, bf16[4,8,3,128,128]{4,3,2,1,0:T(8,128)(2,1)}, u32[]{:S(2)}, u32[]{:S(2)}) collective-permute-start(bf16[4,8,3,128,128]{4,3,2,1,0:T(8,128)(2,1)} %get-tuple-element.50), channel_id=1, source_target_pairs={{0,4},{4,0},{1,5},{5,1},{2,6},{6,2},{3,7},{7,3},{8,12},{12,8},{9,1... | collective-permute-start | bytes 9437192 | tf_op jit(solution)/shard_map/ppermute | solution.py:653
  385.9 372.5 %reduce-scatter.17.cloned.1.call-start = ((), (), s32[]{:S(2)}) async-start(), calls=%async_computation.16 | async-start | bytes 3932160 | tf_op jit(solution)/shard_map/reduce_scatter | solution.py:705
  453.1 89.2 %collective-permute-start.17 = (bf16[4,8,3,128,128]{4,3,2,1,0:T(8,128)(2,1)}, bf16[4,8,3,128,128]{4,3,2,1,0:T(8,128)(2,1)}, u32[]{:S(2)}, u32[]{:S(2)}) collective-permute-start(bf16[4,8,3,128,128]{4,3,2,1,0:T(8,128)(2,1)} %get-tuple-element.59), channel_id=1, source_target_pairs={{0,4},{4,0},{1,5},{5,1},{2,6},{6,2},{3,7},{7,3},{8,12},{12,8},{9,1... | collective-permute-start | bytes 9437192 | tf_op jit(solution)/shard_map/ppermute | solution.py:653
  458.6 62.2 %copy-start.48 = (f32[2048]{0:T(1024)S(1)}, f32[2048]{0:T(1024)}, u32[]{:S(2)}) copy-start(f32[2048]{0:T(1024)} %copy-done.47) | copy-start | bytes 24580
  542.4 216.5 %reduce-scatter.13.cloned.1.call-start = ((), (), s32[]{:S(2)}) async-start(), calls=%async_computation.14 | async-start | bytes 3932160 | tf_op jit(solution)/shard_map/reduce_scatter | solution.py:744
  548.9 213.9 %reduce-scatter.11.cloned.1.call-start = ((), (), s32[]{:S(2)}) async-start(), calls=%async_computation.13 | async-start | bytes 3932160 | tf_op jit(solution)/shard_map/reduce_scatter | solution.py:744
  555.1 6.2 collective-permute-start.19
  561.2 5.3 collective-permute-start.18
  564.5 26.0 %collective-permute-start.20 = (bf16[512,1024]{1,0:T(8,128)(2,1)}, bf16[512,1024]{1,0:T(8,128)(2,1)}, u32[]{:S(2)}, u32[]{:S(2)}) collective-permute-start(bf16[512,1024]{1,0:T(8,128)(2,1)} %add_convert_fusion.2), channel_id=1, source_target_pairs={{0,2},{1,3},{2,0},{3,1},{4,6},{5,7},{6,4},{7,5},{8,10},{9,11},{10,... | collective-permute-start | bytes 3145736 | tf_op jit(solution)/shard_map/ppermute | solution.py:435
  601.3 18.5 %all-to-all-start.2 = ((bf16[1,512,8,128]{3,1,0,2:T(8,128)(2,1)}), bf16[1,512,8,128]{3,1,0,2:T(8,128)(2,1)}, u32[]{:S(2)}, u32[]{:S(2)}) async-start(bf16[1,512,8,128]{3,1,0,2:T(8,128)(2,1)} %copy.129), calls=%async_computation.4 | async-start | bytes 2097152 | tf_op jit(solution)/shard_map/all_to_all | solution.py:721
  612.1 53.4 %collective-permute-start.36 = (bf16[4,2,2,32,1024]{4,3,2,1,0:T(8,128)(2,1)}, bf16[4,2,2,32,1024]{4,3,2,1,0:T(8,128)(2,1)}, u32[]{:S(2)}, u32[]{:S(2)}) collective-permute-start(bf16[4,2,2,32,1024]{4,3,2,1,0:T(8,128)(2,1)} %dynamic-slice_bitcast_fusion.1), channel_id=1, source_target_pairs={{0,1},{1,0},{2,3},{3,2},{4,5},{5,4},{6,7},{7,6},{8,9},{9,8},{10,11... | collective-permute-start | bytes 3145736 | tf_op jit(solution)/shard_map/ppermute | solution.py:482
  618.3 53.2 %collective-permute-start.22 = (bf16[512,1024]{1,0:T(8,128)(2,1)}, bf16[512,1024]{1,0:T(8,128)(2,1)}, u32[]{:S(2)}, u32[]{:S(2)}) collective-permute-start(bf16[512,1024]{1,0:T(8,128)(2,1)} %get-tuple-element.133), channel_id=1, source_target_pairs={{0,1},{1,0},{2,3},{3,2},{4,5},{5,4},{6,7},{7,6},{8,9},{9,8},{10,11... | collective-permute-start | bytes 3145736 | tf_op jit(solution)/shard_map/ppermute | solution.py:430
  655.0 28.4 %all-to-all-start.3 = ((bf16[1,1024,4,256]{3,2,0,1:T(4,128)(2,1)}), bf16[1,1024,4,256]{3,2,0,1:T(4,128)(2,1)S(1)}, u32[]{:S(2)}, u32[]{:S(2)}) async-start(bf16[1,1024,4,256]{3,2,0,1:T(4,128)(2,1)} %bitcast.261), calls=%async_computation.5 | async-start | bytes 4194304 | tf_op jit(solution)/shard_map/all_to_all | solution.py:726
  658.9 137.4 %reduce-scatter.15.cloned.1.call-start = ((), (), s32[]{:S(2)}) async-start(), calls=%async_computation.15 | async-start | bytes 3932160 | tf_op jit(solution)/shard_map/reduce_scatter | solution.py:705
  665.5 74.8 %collective-permute-start.21 = (bf16[512,1024]{1,0:T(8,128)(2,1)}, bf16[512,1024]{1,0:T(8,128)(2,1)}, u32[]{:S(2)}, u32[]{:S(2)}) collective-permute-start(bf16[512,1024]{1,0:T(8,128)(2,1)} %get-tuple-element.132), channel_id=1, source_target_pairs={{0,1},{1,0},{2,3},{3,2},{4,5},{5,4},{6,7},{7,6},{8,9},{9,8},{10,11... | collective-permute-start | bytes 3145736 | tf_op jit(solution)/shard_map/ppermute | solution.py:430
  669.8 27.4 %collective-permute-start.37 = (bf16[4,2,32,1024]{3,2,1,0:T(8,128)(2,1)}, bf16[4,2,32,1024]{3,2,1,0:T(8,128)(2,1)}, u32[]{:S(2)}, u32[]{:S(2)}) collective-permute-start(bf16[4,2,32,1024]{3,2,1,0:T(8,128)(2,1)} %fusion.32), channel_id=1, source_target_pairs={{0,2},{1,3},{2,0},{3,1},{4,6},{5,7},{6,4},{7,5},{8,10},{9,11},{10,... | collective-permute-start | bytes 1572872 | tf_op jit(solution)/shard_map/ppermute | solution.py:482
  674.6 65.7 %collective-permute-start.23 = (bf16[512,1024]{1,0:T(8,128)(2,1)}, bf16[512,1024]{1,0:T(8,128)(2,1)}, u32[]{:S(2)}, u32[]{:S(2)}) collective-permute-start(bf16[512,1024]{1,0:T(8,128)(2,1)} %fusion.15), channel_id=1, source_target_pairs={{0,2},{1,3},{2,0},{3,1},{4,6},{5,7},{6,4},{7,5},{8,10},{9,11},{10,... | collective-permute-start | bytes 3145736 | tf_op jit(solution)/shard_map/ppermute | solution.py:435
  697.1 4.3 collective-permute-start.24
  701.3 14.2 %collective-permute-start.38 = (bf16[4,32,1024]{2,1,0:T(8,128)(2,1)S(1)}, bf16[4,32,1024]{2,1,0:T(8,128)(2,1)S(1)}, u32[]{:S(2)}, u32[]{:S(2)}) collective-permute-start(bf16[4,32,1024]{2,1,0:T(8,128)(2,1)S(1)} %fusion.38), channel_id=1, source_target_pairs={{0,4},{4,0},{1,5},{5,1},{2,6},{6,2},{3,7},{7,3},{8,12},{12,8},{9,1... | collective-permute-start | bytes 786440 | tf_op jit(solution)/shard_map/ppermute | solution.py:474
  701.5 6.0 collective-permute-start.25
  707.5 3.8 collective-permute-start.26
  711.1 39.6 %collective-permute-start.30 = (bf16[4,2,2,64,1024]{4,3,2,1,0:T(8,128)(2,1)}, bf16[4,2,2,64,1024]{4,3,2,1,0:T(8,128)(2,1)}, u32[]{:S(2)}, u32[]{:S(2)}) collective-permute-start(bf16[4,2,2,64,1024]{4,3,2,1,0:T(8,128)(2,1)} %dynamic-slice_bitcast_fusion), channel_id=1, source_target_pairs={{0,1},{1,0},{2,3},{3,2},{4,5},{5,4},{6,7},{7,6},{8,9},{9,8},{10,11... | collective-permute-start | bytes 6291464 | tf_op jit(solution)/shard_map/ppermute | solution.py:482
  711.4 5.7 collective-permute-start.27
  715.6 6.4 collective-permute-start.29
  717.1 7.9 collective-permute-start.28
  722.0 9.7 %collective-permute-start.39 = (bf16[32,1024]{1,0:T(8,128)(2,1)S(1)}, bf16[32,1024]{1,0:T(8,128)(2,1)S(1)}, u32[]{:S(2)}, u32[]{:S(2)}) collective-permute-start(bf16[32,1024]{1,0:T(8,128)(2,1)S(1)} %get-tuple-element.143), channel_id=1, source_target_pairs={{0,8},{8,16},{16,24},{24,0},{1,9},{9,17},{17,25},{25,1},{2,10},{10... | collective-permute-start | bytes 196616 | tf_op jit(solution)/shard_map/ppermute | solution.py:474
  725.0 8.5 %collective-permute-start.41 = (bf16[32,1024]{1,0:T(8,128)(2,1)S(1)}, bf16[32,1024]{1,0:T(8,128)(2,1)S(1)}, u32[]{:S(2)}, u32[]{:S(2)}) collective-permute-start(bf16[32,1024]{1,0:T(8,128)(2,1)S(1)} %get-tuple-element.144), channel_id=1, source_target_pairs={{0,24},{8,0},{16,8},{24,16},{1,25},{9,1},{17,9},{25,17},{2,26},{10... | collective-permute-start | bytes 196616 | tf_op jit(solution)/shard_map/ppermute | solution.py:474
  731.7 17.6 %collective-permute-start.42 = (bf16[8,3,128,128]{3,2,0,1:T(8,128)(2,1)S(1)}, bf16[8,3,128,128]{3,2,0,1:T(8,128)(2,1)}, u32[]{:S(2)}, u32[]{:S(2)}) collective-permute-start(bf16[8,3,128,128]{3,2,0,1:T(8,128)(2,1)S(1)} %copy.136), channel_id=1, source_target_pairs={{0,4},{4,0},{1,5},{5,1},{2,6},{6,2},{3,7},{7,3},{8,12},{12,8},{9,1... | collective-permute-start | bytes 2359304 | tf_op jit(solution)/shard_map/ppermute | solution.py:747
  733.5 5.2 collective-permute-start.40
  755.9 22.3 %collective-permute-start.31 = (bf16[4,2,64,1024]{3,2,1,0:T(8,128)(2,1)S(1)}, bf16[4,2,64,1024]{3,2,1,0:T(8,128)(2,1)S(1)}, u32[]{:S(2)}, u32[]{:S(2)}) collective-permute-start(bf16[4,2,64,1024]{3,2,1,0:T(8,128)(2,1)S(1)} %fusion.20), channel_id=1, source_target_pairs={{0,2},{1,3},{2,0},{3,1},{4,6},{5,7},{6,4},{7,5},{8,10},{9,11},{10,... | collective-permute-start | bytes 3145736 | tf_op jit(solution)/shard_map/ppermute | solution.py:482
  758.4 37.9 %collective-permute-start.43 = (bf16[8,3,128,128]{3,2,1,0:T(8,128)(2,1)}, bf16[8,3,128,128]{3,2,1,0:T(8,128)(2,1)}, u32[]{:S(2)}, u32[]{:S(2)}) collective-permute-start(bf16[8,3,128,128]{3,2,1,0:T(8,128)(2,1)} %bitcast.317), channel_id=1, source_target_pairs={{0,4},{4,0},{1,5},{5,1},{2,6},{6,2},{3,7},{7,3},{8,12},{12,8},{9,1... | collective-permute-start | bytes 2359304 | tf_op jit(solution)/shard_map/ppermute | solution.py:747
  781.1 20.0 %collective-permute-start.32 = (bf16[4,64,1024]{2,1,0:T(8,128)(2,1)}, bf16[4,64,1024]{2,1,0:T(8,128)(2,1)}, u32[]{:S(2)}, u32[]{:S(2)}) collective-permute-start(bf16[4,64,1024]{2,1,0:T(8,128)(2,1)} %fusion.33), channel_id=1, source_target_pairs={{0,4},{4,0},{1,5},{5,1},{2,6},{6,2},{3,7},{7,3},{8,12},{12,8},{9,1... | collective-permute-start | bytes 1572872 | tf_op jit(solution)/shard_map/ppermute | solution.py:474
  802.5 8.3 %collective-permute-start.33 = (bf16[64,1024]{1,0:T(8,128)(2,1)S(1)}, bf16[64,1024]{1,0:T(8,128)(2,1)S(1)}, u32[]{:S(2)}, u32[]{:S(2)}) collective-permute-start(bf16[64,1024]{1,0:T(8,128)(2,1)S(1)} %get-tuple-element.140), channel_id=1, source_target_pairs={{0,8},{8,16},{16,24},{24,0},{1,9},{9,17},{17,25},{25,1},{2,10},{10... | collective-permute-start | bytes 393224 | tf_op jit(solution)/shard_map/ppermute | solution.py:474
  803.5 8.1 collective-permute-start.35
  806.4 11.5 %collective-permute-start.34 = (bf16[64,1024]{1,0:T(8,128)(2,1)S(1)}, bf16[64,1024]{1,0:T(8,128)(2,1)S(1)}, u32[]{:S(2)}, u32[]{:S(2)}) collective-permute-start(bf16[64,1024]{1,0:T(8,128)(2,1)S(1)} %get-tuple-element.142), channel_id=1, source_target_pairs={{0,16},{8,24},{16,0},{24,8},{1,17},{9,25},{17,1},{25,9},{2,18},{10... | collective-permute-start | bytes 393224 | tf_op jit(solution)/shard_map/ppermute | solution.py:474
  (56 other events, 723.7 us)
Sparse Core Ops, SparseCore 0:
  11.5 76.2 all-gather.11
  89.3 64.8 all-gather.19
  155.8 62.1 all-gather.21
  219.5 62.1 all-gather.17
  283.1 62.1 all-gather.13
  346.7 62.1 all-gather.15
  411.1 58.8 reduce-scatter.6
  472.4 60.2 reduce-scatter.8
  542.5 62.4 reduce-scatter.16
  607.2 60.2 reduce-scatter.12
  669.8 62.9 reduce-scatter.10
  735.0 61.2 reduce-scatter.14
